TPU v7x, 512 devices: a whole 4x8x8 slice. The times are simulated.
512 devices in a mesh: req: 8 (over z), cand: 32 (over y, x), user: 2 (over core).
Axes of the slice: x: 4, y: 8, z: 8, core: 2. Of those that a mesh axis runs over, the one named last changes fastest.
Arguments:
- table: bfloat16 [262144, 512], P(('req', 'cand')), may hold values from -6 to 6
- hot_table: bfloat16 [256, 512], replicated, may hold values from -6 to 6
- hot_ids: int32 [256], replicated, may hold values from 0 to 262143, as said below
- hist_ids: int32 [256, 1024], P(('req', 'cand'), 'user'), may hold values from 0 to 262143, as said below
- cand_ids: int32 [256, 1024], P(('req', 'cand'), 'user'), may hold values from 0 to 262143, as said below
- w_in: bfloat16 [1, 512, 2048], replicated, may hold values from -0.25 to 0.25
- w_out: bfloat16 [1, 512, 512], replicated, may hold values from -0.25 to 0.25
- in_gain: float32 [1, 512], replicated, may hold values from 0.25 to 1.75
- attn_gain: float32 [1, 512], replicated, may hold values from 0.25 to 1.75
Outputs:
- hist_out: bfloat16 [256, 1024, 512], P(('req', 'cand'), 'user')
- cand_out: bfloat16 [256, 1024, 512], P(('req', 'cand'), 'user')
Inputs may be any that keep to these rules, and one draw needn't show every extreme that they name: `hot_ids`: distinct row ids. `hist_ids`: the owner of row id g is g // 1024, the index along req and cand together with req slowest. Of the 512 items of one device, those not in hot_ids have at most 4 items with any one owner, and one owner has exactly 4 of every device's items. `cand_ids`: of the 512 candidates of one device, those not in hot_ids have at most 3 candidates with any one owner, and one owner has exactly 3 of every device's candidates.
All inputs are finite; a program needn't handle non-finite values.
Results may differ from a plain program's by a relative error of at most 0.0055.
Values may be sent and summed in bfloat16 or wider, within the bound.
No kernel may reach another device: no remote copies, remote signals or barrier semaphores. Data moves between devices by JAX's collectives and lax.ppermute only.
A program may use at most 64 MiB of HBM per device.

v0:
```python
import jax
import jax.numpy as jnp
from jax import lax
from jax.sharding import PartitionSpec as P

HEADS = 4


def cut_along(array, dim, peers):
    dims = array.shape
    parts = array.reshape(*dims[:dim], peers, dims[dim] // peers, *dims[dim + 1 :])
    return jnp.moveaxis(parts, dim, 0)


def in_order(parts, dim):
    parts = jnp.moveaxis(parts, 0, dim)
    dims = parts.shape
    return parts.reshape(*dims[:dim], dims[dim] * dims[dim + 1], *dims[dim + 2 :])


def one_exchange(array, axis, axes, splits, concats):
    sizes = [lax.axis_size(a) for a in axes]
    parts = cut_along(array, splits[0], sizes[0])
    parts = jnp.moveaxis(cut_along(parts, splits[1] + 1, sizes[1]), 0, 1)
    inside = parts.shape[2:]
    parts = parts.reshape(-1, *inside)
    parts = lax.all_to_all(parts, axis, split_axis=0, concat_axis=0, tiled=True)
    parts = in_order(parts.reshape(*sizes, *inside), concats[0] + 1)
    return in_order(parts, concats[1])


def copy_for_each(array, axis):
    peers = lax.axis_size(axis)
    return lax.all_to_all(
        jnp.broadcast_to(array[None], (peers, *array.shape)), axis, 0, 0, tiled=True
    )


def gather_directly(array, axis, dim):
    parts = copy_for_each(array, axis)
    return in_order(parts, dim)


def sent_together(arrays, axis, dim, along):
    both = jnp.concatenate(arrays, axis=along)
    whole, at, done = (gather_directly(both, axis, dim), 0, [])
    for a in arrays:
        done.append(lax.slice_in_dim(whole, at, at + a.shape[along], axis=along))
        at += a.shape[along]
    return tuple(done)


def norm_rows(values, scale_gain):
    centre_mean = jnp.mean(values, axis=-1, keepdims=True)
    centred = values - centre_mean
    variance = jnp.mean(centred * centred, axis=-1, keepdims=True)
    return centred * lax.rsqrt(variance + 1e-05) * scale_gain


def slot_ranks(owner_of, is_cold, owner_count):
    item_count = owner_of.shape[0]
    member = ((owner_of[:, None] == jnp.arange(owner_count)[None, :]) & is_cold[:, None]).astype(
        jnp.bfloat16
    )
    earlier = (jnp.arange(item_count)[:, None] > jnp.arange(item_count)[None, :]).astype(
        jnp.bfloat16
    )
    before = jnp.dot(earlier, member, preferred_element_type=jnp.float32)
    return jnp.sum(before * member, axis=1).astype(jnp.int32)


def fill_slots(row_in_owner, owner_of, slot_rank, is_cold, owner_count, capacity):
    target = jnp.where(is_cold, owner_of * capacity + slot_rank, owner_count * capacity)
    return jnp.zeros((owner_count * capacity,), jnp.int32).at[target].set(row_in_owner, mode="drop")


def per_device(table, hot_table, hot_ids, hist_ids, cand_ids, w_in, w_out, in_gain, attn_gain):
    req_count = lax.axis_size("req")
    cand_axis_count = lax.axis_size("cand")
    owner_count = req_count * cand_axis_count
    hist_count = hist_ids.shape[1]
    cand_count = cand_ids.shape[1]
    rows_owned = table.shape[0]
    feature_count = table.shape[1]
    head_dim = feature_count // HEADS
    cap_hist = max(2, 2 * hist_count // owner_count)
    cap_cand = max(2, 3 * cand_count // (2 * owner_count))
    slot_count = cap_hist + cap_cand
    wanted = jnp.concatenate([hist_ids[0], cand_ids[0]])
    hot_hit = wanted[:, None] == hot_ids[None, :]
    is_hot = jnp.any(hot_hit, axis=1)
    is_cold = jnp.logical_not(is_hot)
    hot_rows = jnp.dot(
        hot_hit.astype(jnp.bfloat16), hot_table, preferred_element_type=jnp.float32
    ).astype(jnp.bfloat16)
    owner_of = wanted // rows_owned
    row_in_owner = wanted % rows_owned
    rank_hist = slot_ranks(owner_of[:hist_count], is_cold[:hist_count], owner_count)
    rank_cand = slot_ranks(owner_of[hist_count:], is_cold[hist_count:], owner_count)
    send_hist = fill_slots(
        row_in_owner[:hist_count],
        owner_of[:hist_count],
        rank_hist,
        is_cold[:hist_count],
        owner_count,
        cap_hist,
    )
    send_cand = fill_slots(
        row_in_owner[hist_count:],
        owner_of[hist_count:],
        rank_cand,
        is_cold[hist_count:],
        owner_count,
        cap_cand,
    )
    asked = jnp.concatenate(
        [
            send_hist.reshape(req_count, cand_axis_count, cap_hist),
            send_cand.reshape(req_count, cand_axis_count, cap_cand),
        ],
        axis=2,
    )
    row_numbers = one_exchange(asked, ("req", "cand"), ("req", "cand"), (0, 1), (0, 1))
    fetched = jnp.take(table, row_numbers.reshape(-1), axis=0).reshape(
        row_numbers.shape + (feature_count,)
    )
    replied = one_exchange(fetched, ("req", "cand"), ("req", "cand"), (0, 1), (0, 1))
    replies_flat = replied.reshape(owner_count * slot_count, feature_count)
    slot_offset = jnp.concatenate(
        [jnp.zeros((hist_count,), jnp.int32), jnp.full((cand_count,), cap_hist, jnp.int32)]
    )
    slot_rank = jnp.concatenate([rank_hist, rank_cand])
    row_pick = jnp.where(is_cold, owner_of * slot_count + slot_offset + slot_rank, 0)
    cold_rows = jnp.take(replies_flat, row_pick, axis=0)
    embedded = jnp.where(is_hot[:, None], hot_rows, cold_rows)
    hist_x = embedded[:hist_count]
    cand_x = embedded[hist_count:]
    score_scale = 1.0 / head_dim**0.5
    query_positions = lax.axis_index("user") * hist_count + jnp.arange(hist_count)
    weights_in = w_in[0]
    hist_in = norm_rows(hist_x.astype(jnp.float32), in_gain[0]).astype(jnp.bfloat16)
    cand_in = norm_rows(cand_x.astype(jnp.float32), in_gain[0]).astype(jnp.bfloat16)
    projected = jax.nn.silu(jnp.dot(hist_in, weights_in, preferred_element_type=jnp.float32))
    hist_u = projected[:, :feature_count]
    hist_v = projected[:, feature_count : 2 * feature_count].astype(jnp.bfloat16)
    hist_q = projected[:, 2 * feature_count : 3 * feature_count].astype(jnp.bfloat16)
    hist_k = projected[:, 3 * feature_count :].astype(jnp.bfloat16)
    cand_u = jax.nn.silu(
        jnp.dot(cand_in, weights_in[:, :feature_count], preferred_element_type=jnp.float32)
    )
    cand_q = jax.nn.silu(
        jnp.dot(
            cand_in,
            weights_in[:, 2 * feature_count : 3 * feature_count],
            preferred_element_type=jnp.float32,
        )
    ).astype(jnp.bfloat16)
    hist_heads = hist_q.reshape(hist_count, HEADS, head_dim)
    cand_heads = cand_q.reshape(cand_count, HEADS, head_dim)
    kv_piece = sent_together((hist_k, hist_v), "user", 0, 1)
    key_heads = kv_piece[0].reshape(-1, HEADS, head_dim)
    value_heads = kv_piece[1].reshape(-1, HEADS, head_dim)
    key_positions = jnp.arange(key_heads.shape[0])
    causal = key_positions[None, :] <= query_positions[:, None]
    hist_scores = (
        jnp.einsum("qhd,khd->hqk", hist_heads, key_heads, preferred_element_type=jnp.float32)
        * score_scale
    )
    hist_weights = jnp.where(causal[None], jax.nn.silu(hist_scores), 0.0).astype(jnp.bfloat16)
    cand_scores = (
        jnp.einsum("qhd,khd->hqk", cand_heads, key_heads, preferred_element_type=jnp.float32)
        * score_scale
    )
    cand_weights = jax.nn.silu(cand_scores).astype(jnp.bfloat16)
    hist_total = jnp.einsum(
        "hqk,khd->qhd", hist_weights, value_heads, preferred_element_type=jnp.float32
    )
    cand_total = jnp.einsum(
        "hqk,khd->qhd", cand_weights, value_heads, preferred_element_type=jnp.float32
    )
    hist_gated = (
        norm_rows(hist_total.reshape(hist_count, feature_count), attn_gain[0]) * hist_u
    ).astype(jnp.bfloat16)
    cand_gated = (
        norm_rows(cand_total.reshape(cand_count, feature_count), attn_gain[0]) * cand_u
    ).astype(jnp.bfloat16)
    hist_x = (
        hist_x.astype(jnp.float32)
        + jnp.dot(hist_gated, w_out[0], preferred_element_type=jnp.float32)
    ).astype(jnp.bfloat16)
    cand_x = (
        cand_x.astype(jnp.float32)
        + jnp.dot(cand_gated, w_out[0], preferred_element_type=jnp.float32)
    ).astype(jnp.bfloat16)
    return (hist_x[None], cand_x[None])


def solution(mesh):
    in_specs = (
        P(("req", "cand"), None),
        P(),
        P(),
        P(("req", "cand"), "user"),
        P(("req", "cand"), "user"),
        P(),
        P(),
        P(),
        P(),
    )
    out_specs = (P(("req", "cand"), "user", None), P(("req", "cand"), "user", None))
    return jax.shard_map(
        per_device, mesh=mesh, in_specs=in_specs, out_specs=out_specs, check_vma=False
    )
```

profile of v0, /device:TPU:1, one launch (start us, length us, event | category | flops | bytes accessed | tf_op | source)
XLA Modules:
  0.0 168.4 jit_solution(3399948533563698129)
XLA Ops:
  3.3 2.4 %scatter_custom_fusion.1 = s32[768]{0:T(1024)S(1)} fusion(s32[512]{0:T(512)S(1)} %get-tuple-element.20, s32[512]{0:T(512)S(1)} %get-tuple-element.36, s32[]{:T(128)} %constant.92.clone.1), kind=kCustom, calls=%fused_computation.130 | custom fusion | bytes 3076 | tf_op jit(solution)/shard_map/scatter | solution.py:74
  6.0 2.4 %scatter_custom_fusion = s32[1024]{0:T(1024)S(1)} fusion(s32[512]{0:T(512)S(1)} %get-tuple-element.19, s32[512]{0:T(512)S(1)} %get-tuple-element.37, s32[]{:T(128)} %constant.92.clone.1), kind=kCustom, calls=%fused_computation.132 | custom fusion | bytes 4100 | tf_op jit(solution)/shard_map/scatter | solution.py:74
  8.7 35.0 %all_to_all.15 = s32[256,1,1,7]{3,2,1,0:T(1,128)S(1)} all-to-all(s32[256,1,1,7]{3,2,1,0:T(1,128)S(1)} %bitcast.100), channel_id=1, replica_groups=mesh['req'=8,'cand'=32,'user'=2] {'req','cand'}, dimensions={0} | all-to-all | bytes 14336 | tf_op jit(solution)/shard_map/all_to_all | solution.py:27
  43.9 6.1 %gather_fusion = bf16[1792,512]{1,0:T(8,128)(2,1)} fusion(bf16[1024,512]{1,0:T(8,128)(2,1)S(1)} %copy-done, s32[2048]{0:T(1024)S(1)} %pad_clamp_fusion), kind=kCustom, calls=%fused_computation | custom fusion | bytes 3677184 | tf_op jit(solution)/shard_map/jit(_take)/gather | solution.py:124
  50.0 2.6 %gather.11 = bf16[256,1,1,7,512]{4,3,0,2,1:T(8,128)(2,1)S(1)} reshape(bf16[1792,512]{1,0:T(8,128)(2,1)} %gather_fusion) | data formatting | bytes 3670016 | tf_op jit(solution)/shard_map/jit(_take)/gather | solution.py:124
  52.6 1.6 select_bitcast_fusion
  54.2 9.5 %all-to-all-start.1 = ((bf16[256,1,1,7,512]{4,3,2,1,0:T(8,128)(2,1)}), bf16[256,1,1,7,512]{4,3,2,1,0:T(8,128)(2,1)S(1)}, u32[]{:S(2)}, u32[]{:S(2)}) async-start(bf16[256,1,1,7,512]{4,3,2,1,0:T(8,128)(2,1)} %select_bitcast_fusion), calls=%async_computation.1 | async-start | bytes 4194304 | tf_op jit(solution)/shard_map/all_to_all | solution.py:27
  63.9 1.2 iota_compare_fusion
  65.1 47.4 %all-to-all-done.1 = bf16[256,1,1,7,512]{4,3,2,1,0:T(8,128)(2,1)S(1)} async-done(((bf16[256,1,1,7,512]{4,3,2,1,0:T(8,128)(2,1)}), bf16[256,1,1,7,512]{4,3,2,1,0:T(8,128)(2,1)S(1)}, u32[]{:S(2)}, u32[]{:S(2)}) %all-to-all-start.1) | async-done | bytes 1835040 | tf_op jit(solution)/shard_map/all_to_all | solution.py:27
  112.4 1.3 copy-done.1
  113.8 2.6 %reshape_reshape.10 = bf16[1792,512]{1,0:T(8,128)(2,1)S(1)} reshape(bf16[8,32,1,7,512]{4,3,1,0,2:T(8,128)(2,1)} %bitcast.89) | data formatting | bytes 3670016 | tf_op jit(solution)/shard_map/reshape;reshape | solution.py:128
  116.4 5.1 %gather_fusion.1 = bf16[1024,512]{1,0:T(8,128)(2,1)} fusion(bf16[1792,512]{1,0:T(8,128)(2,1)S(1)} %reshape_reshape.10, s32[1024]{0:T(1024)S(1)} %broadcast_clamp_fusion), kind=kCustom, calls=%fused_computation.1 | custom fusion | bytes 2101248 | tf_op jit(solution)/shard_map/jit(_take)/gather | solution.py:134
  121.5 1.5 copy.58
  124.7 4.0 %fusion.111 = (bf16[512,2048]{1,0:T(8,128)(2,1)S(1)}, f32[512,2048]{1,0:T(8,128)}) fusion(bf16[1,512,2048]{2,1,0:T(8,128)(2,1)S(1)} %copy-done.8, f32[512]{0:T(512)S(1)} %bitcast.114, f32[512]{0:T(512)S(1)} %add_rsqrt_fusion.3, f32[512]{0:T(512)S(1)} %broadcast_multiply_fusion.3, bf16[1024,512]{0,1:T(8,128)(2,1)S(1)} %fusion.6), kind=kOutput, calls=%fused_computation.149 | convolution fusion | flops 1080295424 | bytes 8919040 | tf_op jit(solution)/shard_map/dot_general | solution.py:143
  130.7 1.5 copy.59
  132.4 9.9 %all_to_all.16 = bf16[2,512,1024]{1,2,0:T(8,128)(2,1)S(1)} all-to-all(bf16[2,512,1024]{1,2,0:T(8,128)(2,1)S(1)} %broadcast_in_dim.105), channel_id=1, replica_groups=mesh['req'=8,'cand'=32,'user'=2] {'user'}, dimensions={0} | all-to-all | bytes 4194304 | tf_op jit(solution)/shard_map/all_to_all | solution.py:34
  142.6 1.5 fusion.107
  144.1 5.9 %fusion.112 = (f32[512]{0:T(512)S(1)}, f32[4,128,512]{2,1,0:T(8,128)S(1)}) fusion(bf16[1024,4,128]{0,2,1:T(8,128)(2,1)} %bitcast.98, pred[512,1024]{1,0:T(8,128)(4,1)} %iota_compare_fusion, bf16[1024,4,128]{0,2,1:T(8,128)(2,1)} %bitcast.96, bf16[64,4,8,128]{3,2,1,0:T(8,128)(2,1)} %get-tuple-element.14), kind=kOutput, calls=%fused_computation.150 | convolution fusion | flops 1088683520 | bytes 4196352 | tf_op jit(solution)/shard_map/hqk,khd->qhd/dot_general | solution.py:175
  150.1 1.3 copy.78
  151.6 2.3 %fusion.15 = bf16[1,512,512]{1,2,0:T(8,128)(2,1)S(1)} fusion(f32[512,2048]{1,0:T(8,128)} %get-tuple-element.31, f32[512,512]{1,0:T(8,128)} %copy.78, bf16[1,512,512]{2,1,0:T(8,128)(2,1)} %param.15, f32[512]{0:T(512)S(1)} %bitcast.110, f32[512]{0:T(512)S(1)} %add_rsqrt_fusion.2, f32[512]{0:T(512)S(1)} %broadcast_multiply_fusion.2, ...), kind=kOutput, calls=%fused_computation.30 | convolution fusion | flops 270532608 | bytes 3676160 | tf_op jit(solution)/shard_map/dot_general | solution.py:189
  154.9 2.6 %fusion.52 = bf16[64,4,8,128]{3,2,1,0:T(8,128)(2,1)} fusion(bf16[512,2048]{1,0:T(8,128)(2,1)} %bitcast.112, f32[512]{0:T(512)S(1)} %add_rsqrt_fusion.1, f32[512]{0:T(512)S(1)} %broadcast_multiply_fusion.1, f32[512]{0:T(512)S(1)} %bitcast.115, bf16[1024,512]{0,1:T(8,128)(2,1)S(1)} %fusion.6), kind=kOutput, calls=%fused_computation.62 | convolution fusion | flops 271056896 | bytes 1579008 | tf_op jit(solution)/shard_map/dot_general | solution.py:152
  157.5 5.7 %fusion.115 = (f32[512]{0:T(512)S(1)}, f32[4,128,512]{2,1,0:T(8,128)S(1)}) fusion(bf16[1024,4,128]{0,2,1:T(8,128)(2,1)} %bitcast.99, bf16[1024,4,128]{0,2,1:T(8,128)(2,1)} %bitcast.97, bf16[64,4,8,128]{3,2,1,0:T(8,128)(2,1)} %fusion.52), kind=kOutput, calls=%fused_computation.151 | convolution fusion | flops 1086586368 | bytes 3672064 | tf_op jit(solution)/shard_map/hqk,khd->qhd/dot_general | solution.py:178
  163.2 1.3 copy.79
  164.8 2.7 %fusion.14 = bf16[1,512,512]{1,2,0:T(8,128)(2,1)S(1)} fusion(f32[512,512]{1,0:T(8,128)} %copy.79, bf16[512,2048]{1,0:T(8,128)(2,1)} %bitcast.113, bf16[1,512,512]{2,1,0:T(8,128)(2,1)} %param.15, f32[512]{0:T(512)S(1)} %add_rsqrt_fusion, f32[512]{0:T(512)S(1)} %broadcast_multiply_fusion, f32[512]{0:T(512)S(1)} %add_rsqrt_fusion.1, ...), kind=kOutput, calls=%fused_computation.29 | convolution fusion | flops 541327360 | bytes 3682304 | tf_op jit(solution)/shard_map/dot_general | solution.py:193
  (61 shorter events, 9.9 us)
Async XLA Ops:
  0.6 43.3 %copy-start = (bf16[1024,512]{1,0:T(8,128)(2,1)S(1)}, bf16[1024,512]{1,0:T(8,128)(2,1)}, u32[]{:S(2)}) copy-start(bf16[1024,512]{1,0:T(8,128)(2,1)} %param.9) | copy-start | bytes 3145732
  54.2 9.6 %copy-start.2 = (s32[1,512]{1,0:T(1,128)S(1)}, s32[1,512]{1,0:T(1,128)}, u32[]{:S(2)}) copy-start(s32[1,512]{1,0:T(1,128)} %param.13) | copy-start | bytes 6148
  54.2 9.6 %copy-start.3 = (s32[1,512]{1,0:T(1,128)S(1)}, s32[1,512]{1,0:T(1,128)}, u32[]{:S(2)}) copy-start(s32[1,512]{1,0:T(1,128)} %param.12) | copy-start | bytes 6148
  54.2 9.6 %copy-start.5 = (s32[1024]{0:T(1024)S(1)}, s32[1024]{0:T(1024)}, u32[]{:S(2)}) copy-start(s32[1024]{0:T(1024)} %constant.98.clone.1) | copy-start | bytes 12292
  54.2 9.6 %copy-start.4 = (s32[1024,1]{0,1:T(1,128)S(1)}, s32[1024,1]{0,1:T(1,128)}, u32[]{:S(2)}) copy-start(s32[1024,1]{0,1:T(1,128)} %constant.107.clone.1) | copy-start | bytes 12292
  54.2 58.2 %all-to-all-start.1 = ((bf16[256,1,1,7,512]{4,3,2,1,0:T(8,128)(2,1)}), bf16[256,1,1,7,512]{4,3,2,1,0:T(8,128)(2,1)S(1)}, u32[]{:S(2)}, u32[]{:S(2)}) async-start(bf16[256,1,1,7,512]{4,3,2,1,0:T(8,128)(2,1)} %select_bitcast_fusion), calls=%async_computation.1 | async-start | bytes 4194304 | tf_op jit(solution)/shard_map/all_to_all | solution.py:27
  112.4 1.4 copy-start.1
  121.5 1.5 copy-start.7
  121.5 1.5 copy-start.9
  123.1 1.6 copy-start.8
  123.1 1.6 copy-start.10
  150.1 1.6 copy-start.6
where the time goes:
time: 169 us; the launch traced here: 168 us
  waiting for transfers between devices  47.4 us (28%)
  blocking collectives  44.9 us (27%)
  local copies, waits for them, and re-layouts  34.3 us (20%)
  matrix products  24.5 us (14%)
  starting transfers between devices  9.51 us (6%)
  other arithmetic  6.83 us (4%)
    all_to_all x1, waiting for transfers between devices, one_exchange(): parts = lax.all_to_all(parts, axis, split_axis=0, concat_axis=0, tiled=True)  47.4 us
    all_to_all x1, blocking collectives, one_exchange(): parts = lax.all_to_all(parts, axis, split_axis=0, concat_axis=0, tiled=True)  35 us
    all_to_all x1, blocking collectives, copy_for_each(): lax.all_to_all(jnp.broadcast_to(array[None], (peers, *array.shape)), axis...  9.93 us
    all_to_all x1, starting transfers between devices, one_exchange(): parts = lax.all_to_all(parts, axis, split_axis=0, concat_axis=0, tiled=True)  9.51 us
    gather x2, local copies, waits for them, and re-layouts, per_device(): jnp.take(table, row_numbers.reshape(-1), axis=0)  8.68 us
    gather x2, local copies, waits for them, and re-layouts, per_device(): cold_rows = jnp.take(replies_flat, row_pick, axis=0)  6.6 us
    dot_general x1, matrix products, per_device(): jnp.einsum('hqk,khd->qhd', hist_weights, value_heads, preferred_element_t...  5.93 us
    dot_general x1, matrix products, per_device(): jnp.einsum('hqk,khd->qhd', cand_weights, value_heads, preferred_element_t...  5.75 us
  transfers between devices with their start and end apart: 1, of which 1 were waited for; matrix products, arithmetic and copies ran while one was open for 1% of the time, Pallas kernels for 0%

commit v1 on v0

v1 whole, which is shorter than its diff:
```python
import jax
import jax.numpy as jnp
from jax import lax
from jax.experimental import pallas as pl
from jax.experimental.pallas import tpu as pltpu
from jax.sharding import PartitionSpec as P

HEADS = 4
SLOTS = 4
LANES = 8
F32 = jnp.float32
BF16 = jnp.bfloat16
I32 = jnp.int32
VMEM_BYTES = 32 * 1024 * 1024


def iota(shape, dim):
    return lax.broadcasted_iota(I32, shape, dim)


def dot(a, b):
    return jnp.dot(a, b, preferred_element_type=F32)


def dot_nt(a, b):
    return lax.dot_general(a, b, (((1,), (1,)), ((), ())), preferred_element_type=F32)


def to_column(row):
    n = row.shape[1]
    diag = iota((n, n), 0) == iota((n, n), 1)
    return jnp.sum(jnp.where(diag, row, 0.0), axis=1, keepdims=True)


def silu(v):
    half = 0.5 * v
    return half + half * jnp.tanh(half)


def norm(z, gain):
    centred = z - jnp.mean(z, axis=1, keepdims=True)
    variance = jnp.mean(centred * centred, axis=1, keepdims=True)
    return centred * lax.rsqrt(variance + 1e-05) * gain


def ask_kernel(hist_ids, cand_ids, hot_ids, asked, picks, *, owners, shift):
    hot_count = hot_ids.shape[1]
    hot_column = to_column(hot_ids[...].astype(F32))
    total = jnp.zeros((owners, LANES), F32)
    for side, (ids_ref, first) in enumerate(((hist_ids, 0), (cand_ids, SLOTS))):
        ids = ids_ref[...]
        n = ids.shape[1]
        hit = hot_column == ids.astype(F32)
        is_hot = jnp.max(jnp.where(hit, 1.0, 0.0), axis=0, keepdims=True)
        hot_at = jnp.sum(
            jnp.where(hit, iota((hot_count, n), 0).astype(F32), 0.0), axis=0, keepdims=True
        )
        owner = lax.shift_right_logical(ids, shift)
        row = ids & ((1 << shift) - 1)
        of_cold = jnp.where(is_hot > 0.5, -1, owner)
        member = (iota((owners, n), 0) == of_cold).astype(F32)
        member_low = member.astype(BF16)
        earlier = (iota((n, n), 0) < iota((n, n), 1)).astype(F32).astype(BF16)
        before = dot(member_low, earlier)
        rank = jnp.sum(before * member, axis=0, keepdims=True)
        slot = rank + first
        here = iota((LANES, n), 0).astype(F32) == slot
        high = jnp.where(here, lax.shift_right_logical(row, 5).astype(F32), 0.0).astype(BF16)
        low = jnp.where(here, (row & 31).astype(F32), 0.0).astype(BF16)
        total = total + 32.0 * dot_nt(member_low, high) + dot_nt(member_low, low)
        cold_at = owner.astype(F32) * SLOTS + rank
        picks[side : side + 1, :] = jnp.where(is_hot > 0.5, owners * SLOTS + hot_at, cold_at)
    asked[...] = total.astype(I32)


def ask(hist_ids, cand_ids, hot_ids, owners, shift):
    n = hist_ids.shape[1]
    return pl.pallas_call(
        lambda *refs: ask_kernel(*refs, owners=owners, shift=shift),
        out_shape=(
            jax.ShapeDtypeStruct((owners, LANES), I32),
            jax.ShapeDtypeStruct((2, n), F32),
        ),
        compiler_params=pltpu.CompilerParams(vmem_limit_bytes=VMEM_BYTES),
        cost_estimate=pl.CostEstimate(flops=10**9, bytes_accessed=10**5, transcendentals=0),
        name="ask",
    )(hist_ids, cand_ids, hot_ids)


def columns_kernel(picks, columns):
    columns[:, 0:1] = to_column(picks[0:1, :])
    columns[:, 1:2] = to_column(picks[1:2, :])


def columns_of(picks):
    n = picks.shape[1]
    return pl.pallas_call(
        columns_kernel,
        out_shape=jax.ShapeDtypeStruct((n, 2), F32),
        compiler_params=pltpu.CompilerParams(vmem_limit_bytes=VMEM_BYTES),
        cost_estimate=pl.CostEstimate(flops=10**8, bytes_accessed=10**5, transcendentals=0),
        name="columns",
    )(picks)


def fetch_kernel(numbers, table, sent, *, first):
    owners = numbers.shape[0]
    rows, width = table.shape
    count = owners * SLOTS
    n = numbers[...]
    spread = (lax.shift_right_logical(iota((count, owners), 0), 2) == iota((count, owners), 1))
    spread = spread.astype(F32).astype(BF16)
    high = lax.shift_right_logical(n, 5).astype(F32).astype(BF16)
    low = (n & 31).astype(F32).astype(BF16)
    every = 32.0 * dot(spread, high) + dot(spread, low)
    lane = iota((count, LANES), 1) == (iota((count, LANES), 0) & (SLOTS - 1)) + first
    number = jnp.sum(jnp.where(lane, every, 0.0), axis=1, keepdims=True).astype(I32)
    chosen = (iota((count, rows), 1) == number).astype(F32).astype(BF16)
    half = width // 2
    left = dot(chosen, table[:, :half]).reshape(owners // 2, 8, half)
    right = dot(chosen, table[:, half:]).reshape(owners // 2, 8, half)
    upper = iota(left.shape, 1) < 4
    even = jnp.where(upper, left, pltpu.roll(right, 4, 1))
    odd = jnp.where(upper, pltpu.roll(left, 4, 1), right)
    sent[:, 0] = even.astype(BF16)
    sent[:, 1] = odd.astype(BF16)


def fetch(numbers, table, first):
    owners = numbers.shape[0]
    rows, width = table.shape
    sent = pl.pallas_call(
        lambda *refs: fetch_kernel(*refs, first=first),
        out_shape=jax.ShapeDtypeStruct((owners // 2, 2, 8, width // 2), BF16),
        compiler_params=pltpu.CompilerParams(vmem_limit_bytes=VMEM_BYTES),
        cost_estimate=pl.CostEstimate(
            flops=3 * 10**9, bytes_accessed=3 * 10**6, transcendentals=0
        ),
        name="fetch",
    )(numbers, table)
    return sent.reshape(owners, 8, width // 2)


def picked_rows(replies, hot, column):
    pairs, _, _, half = replies.shape
    even = replies[:, 0].astype(F32)
    odd = replies[:, 1].astype(F32)
    upper = iota(even.shape, 1) < 4
    left = jnp.where(upper, even, pltpu.roll(odd, 4, 1)).reshape(pairs * 8, half).astype(BF16)
    right = jnp.where(upper, pltpu.roll(even, 4, 1), odd).reshape(pairs * 8, half).astype(BF16)
    n = column.shape[0]
    count = pairs * 8
    at = column.astype(I32)
    cold = (iota((n, count), 1) == at).astype(F32).astype(BF16)
    warm = (iota((n, hot.shape[0]), 1) == at - count).astype(F32).astype(BF16)
    found = jnp.concatenate([dot(cold, left), dot(cold, right)], axis=1)
    return found + dot(warm, hot[...])


def encode_kernel(replies, hot, columns, w_in, gain, x_out, u_out, q_out, kv_out):
    width = hot.shape[1]
    x = picked_rows(replies, hot, columns[:, 0:1])
    x_out[...] = x.astype(BF16)
    inner = norm(x, gain[...]).astype(BF16)
    u_out[...] = silu(dot(inner, w_in[:, :width]))
    kv_out[:, width:] = silu(dot(inner, w_in[:, width : 2 * width])).astype(BF16)
    q_out[...] = silu(dot(inner, w_in[:, 2 * width : 3 * width])).astype(BF16)
    kv_out[:, :width] = silu(dot(inner, w_in[:, 3 * width :])).astype(BF16)


def encode(replies, hot, columns, w_in, gain):
    n = columns.shape[0]
    width = hot.shape[1]
    owners = replies.shape[0]
    return pl.pallas_call(
        encode_kernel,
        out_shape=(
            jax.ShapeDtypeStruct((n, width), BF16),
            jax.ShapeDtypeStruct((n, width), F32),
            jax.ShapeDtypeStruct((n, width), BF16),
            jax.ShapeDtypeStruct((n, 2 * width), BF16),
        ),
        compiler_params=pltpu.CompilerParams(vmem_limit_bytes=VMEM_BYTES),
        cost_estimate=pl.CostEstimate(
            flops=3 * 10**9, bytes_accessed=7 * 10**6, transcendentals=10**6
        ),
        name="encode",
    )(replies.reshape(owners // 2, 2, 8, width // 2), hot, columns, w_in, gain)


def weighed(q, k, v, head_dim, keep=None):
    s = dot_nt(q, k) * (0.5 / head_dim**0.5)
    w = s + s * jnp.tanh(s)
    if keep is not None:
        w = jnp.where(keep, w, 0.0)
    return dot(w.astype(BF16), v)


def finish(mix, gain, u, w_out, x):
    gated = (norm(mix, gain) * u).astype(BF16)
    return (x + dot(gated, w_out)).astype(BF16)


def history_kernel(user, x, u, q, own, other, gain, w_out, out, mix):
    n, width = x.shape
    head_dim = width // HEADS
    causal = iota((n, n), 1) <= iota((n, n), 0)
    for h in range(HEADS):
        at = slice(h * head_dim, (h + 1) * head_dim)
        past = slice(width + h * head_dim, width + (h + 1) * head_dim)
        mix[:, at] = weighed(q[:, at], own[:, at], own[:, past], head_dim, causal)

    @pl.when(user[0] == 1)
    def _():
        for h in range(HEADS):
            at = slice(h * head_dim, (h + 1) * head_dim)
            past = slice(width + h * head_dim, width + (h + 1) * head_dim)
            mix[:, at] += weighed(q[:, at], other[:, at], other[:, past], head_dim)

    out[...] = finish(mix[...], gain[...], u[...], w_out[...], x[...].astype(F32))


def history(user, x, u, q, own, other, gain, w_out):
    vmem = pl.BlockSpec(memory_space=pltpu.VMEM)
    return pl.pallas_call(
        history_kernel,
        out_shape=jax.ShapeDtypeStruct(x.shape, BF16),
        in_specs=[pl.BlockSpec(memory_space=pltpu.SMEM)] + [vmem] * 7,
        out_specs=vmem,
        scratch_shapes=[pltpu.VMEM(x.shape, F32)],
        compiler_params=pltpu.CompilerParams(vmem_limit_bytes=VMEM_BYTES),
        cost_estimate=pl.CostEstimate(
            flops=2 * 10**9, bytes_accessed=5 * 10**6, transcendentals=2 * 10**6
        ),
        name="history",
    )(user, x, u, q, own, other, gain, w_out)


def candidates_kernel(
    replies, hot, columns, w_in, in_gain, own, other, gain, w_out, _, out, mix
):
    width = hot.shape[1]
    head_dim = width // HEADS
    x = picked_rows(replies, hot, columns[:, 1:2])
    inner = norm(x, in_gain[...]).astype(BF16)
    u = silu(dot(inner, w_in[:, :width]))
    q = silu(dot(inner, w_in[:, 2 * width : 3 * width])).astype(BF16)
    for h in range(HEADS):
        at = slice(h * head_dim, (h + 1) * head_dim)
        past = slice(width + h * head_dim, width + (h + 1) * head_dim)
        mix[:, at] = weighed(q[:, at], own[:, at], own[:, past], head_dim) + weighed(
            q[:, at], other[:, at], other[:, past], head_dim
        )
    out[...] = finish(mix[...], gain[...], u, w_out[...], x)


def candidates(replies, hot, columns, w_in, in_gain, own, other, gain, w_out, after):
    n = columns.shape[0]
    width = hot.shape[1]
    owners = replies.shape[0]
    return pl.pallas_call(
        candidates_kernel,
        out_shape=jax.ShapeDtypeStruct((n, width), BF16),
        in_specs=[pl.BlockSpec(memory_space=pltpu.VMEM)] * 9
        + [pl.BlockSpec(memory_space=pl.ANY)],
        out_specs=pl.BlockSpec(memory_space=pltpu.VMEM),
        scratch_shapes=[pltpu.VMEM((n, width), F32)],
        compiler_params=pltpu.CompilerParams(vmem_limit_bytes=VMEM_BYTES),
        cost_estimate=pl.CostEstimate(
            flops=4 * 10**9, bytes_accessed=7 * 10**6, transcendentals=3 * 10**6
        ),
        name="candidates",
    )(
        replies.reshape(owners // 2, 2, 8, width // 2),
        hot,
        columns,
        w_in,
        in_gain,
        own,
        other,
        gain,
        w_out,
        after,
    )


def exchange(array):
    return lax.all_to_all(array, ("req", "cand"), 0, 0, tiled=True)


def per_device(table, hot_table, hot_ids, hist_ids, cand_ids, w_in, w_out, in_gain, attn_gain):
    owners = lax.axis_size("req") * lax.axis_size("cand")
    shift = (table.shape[0] - 1).bit_length()
    asked, picks = ask(hist_ids, cand_ids, hot_ids[None], owners, shift)
    numbers = exchange(asked[:, None, :])[:, 0, :]
    hist_replies = exchange(fetch(numbers, table, 0))
    cand_replies = exchange(fetch(numbers, table, SLOTS))
    columns = columns_of(picks)
    x, u, q, own = encode(hist_replies, hot_table, columns, w_in[0], in_gain)
    other = lax.ppermute(own, "user", [(0, 1), (1, 0)])
    user = lax.axis_index("user")[None].astype(I32)
    hist_out = history(user, x, u, q, own, other, attn_gain, w_out[0])
    cand_out = candidates(
        cand_replies,
        hot_table,
        columns,
        w_in[0],
        in_gain,
        own,
        other,
        attn_gain,
        w_out[0],
        hist_out,
    )
    return hist_out[None], cand_out[None]


def solution(mesh):
    rows = P(("req", "cand"), None)
    split = P(("req", "cand"), "user")
    in_specs = (rows, P(), P(), split, split, P(), P(), P(), P())
    out_specs = (P(("req", "cand"), "user", None), P(("req", "cand"), "user", None))
    return jax.shard_map(
        per_device, mesh=mesh, in_specs=in_specs, out_specs=out_specs, check_vma=False
    )
```

time: 169 us -> 133 us (0.79)
  the two profiles are of different devices: /device:TPU:1 before, /device:TPU:8 now
where the time goes in v1:
time: 133 us; the launch traced here: 132 us
  waiting for transfers between devices  37.6 us (28%)
  blocking collectives  34.6 us (26%)
  local copies, waits for them, and re-layouts  20.6 us (15%)
  starting transfers between devices  19.7 us (15%)
  Pallas kernels  18.8 us (14%)
    all_to_all x2, waiting for transfers between devices, exchange(): return lax.all_to_all(array, ('req', 'cand'), 0, 0, tiled=True)  36 us
    all_to_all x1, blocking collectives, exchange(): return lax.all_to_all(array, ('req', 'cand'), 0, 0, tiled=True)  34.6 us
    unnamed x52, local copies, waits for them, and re-layouts  20.6 us
    all_to_all x2, starting transfers between devices, exchange(): return lax.all_to_all(array, ('req', 'cand'), 0, 0, tiled=True)  17.8 us
    pallas_call x1, Pallas kernels, candidates(): pl.pallas_call(candidates_kernel, out_shape=jax.ShapeDtypeStruct((n, widt...  6.35 us
    pallas_call x2, Pallas kernels, fetch(): pl.pallas_call(lambda *refs: fetch_kernel(*refs, first=first), out_shape=...  5.44 us
    pallas_call x1, Pallas kernels, history(): pl.pallas_call(history_kernel, out_shape=jax.ShapeDtypeStruct(x.shape, BF...  3.06 us
  transfers between devices with their start and end apart: 3, of which 3 were waited for; matrix products, arithmetic and copies ran while one was open for 0% of the time, Pallas kernels for 6%

profile of v1, /device:TPU:8, one launch (start us, length us, event | category | flops | bytes accessed | tf_op | source)
XLA Modules:
  0.0 132.2 jit_solution(5418709694128094884)
XLA Ops:
  2.8 1.2 ask.1
  4.0 34.6 %all_to_all.15 = s32[256,1,8]{2,1,0:T(1,128)S(1)} all-to-all(s32[256,1,8]{2,1,0:T(1,128)S(1)} %bitcast.18), channel_id=1, replica_groups=mesh['req'=8,'cand'=32,'user'=2] {'req','cand'}, dimensions={0} | all-to-all | bytes 16384 | tf_op jit(solution)/shard_map/all_to_all | solution.py:288
  38.7 2.8 %fetch.2 = bf16[128,2,8,256]{3,2,1,0:T(8,128)(2,1)} custom-call(s32[256,8]{1,0:T(8,128)S(1)} %bitcast.16, bf16[1024,512]{1,0:T(8,128)(2,1)S(1)} %copy-done.2), custom_call_target="tpu_custom_call" | custom-call | flops 3000000000 | bytes 3000000 | tf_op jit(solution)/shard_map/fetch/pallas_call | solution.py:132
  41.5 8.7 %all-to-all-start.1 = ((bf16[256,8,256]{2,1,0:T(8,128)(2,1)}), bf16[256,8,256]{2,1,0:T(8,128)(2,1)S(1)}, u32[]{:S(2)}, u32[]{:S(2)}) async-start(bf16[256,8,256]{2,1,0:T(8,128)(2,1)} %bitcast.5), calls=%async_computation.1 | async-start | bytes 2097152 | tf_op jit(solution)/shard_map/all_to_all | solution.py:288
  50.2 2.6 %fetch.3 = bf16[128,2,8,256]{3,2,1,0:T(8,128)(2,1)} custom-call(s32[256,8]{1,0:T(8,128)S(1)} %bitcast.17, bf16[1024,512]{1,0:T(8,128)(2,1)S(1)} %copy-done.2), custom_call_target="tpu_custom_call" | custom-call | flops 3000000000 | bytes 3000000 | tf_op jit(solution)/shard_map/fetch/pallas_call | solution.py:132
  52.8 28.1 %all-to-all-done.1 = bf16[256,8,256]{2,1,0:T(8,128)(2,1)S(1)} async-done(((bf16[256,8,256]{2,1,0:T(8,128)(2,1)}), bf16[256,8,256]{2,1,0:T(8,128)(2,1)S(1)}, u32[]{:S(2)}, u32[]{:S(2)}) %all-to-all-start.1) | async-done | bytes 1048608 | tf_op jit(solution)/shard_map/all_to_all | solution.py:288
  81.0 9.1 %all-to-all-start.2 = ((bf16[256,8,256]{2,1,0:T(8,128)(2,1)}), bf16[256,8,256]{2,1,0:T(8,128)(2,1)S(1)}, u32[]{:S(2)}, u32[]{:S(2)}) async-start(bf16[256,8,256]{2,1,0:T(8,128)(2,1)} %bitcast.10), calls=%async_computation.2 | async-start | bytes 2097152 | tf_op jit(solution)/shard_map/all_to_all | solution.py:288
  90.3 1.7 %copy-done = bf16[1,512,2048]{2,1,0:T(8,128)(2,1)S(1)} copy-done((bf16[1,512,2048]{2,1,0:T(8,128)(2,1)S(1)}, bf16[1,512,2048]{2,1,0:T(8,128)(2,1)}, u32[]{:S(2)}) %copy-start) | copy-done | bytes 2097176
  92.0 2.5 %encode.1 = (bf16[512,512]{1,0:T(8,128)(2,1)S(1)}, f32[512,512]{1,0:T(8,128)S(1)}, bf16[512,512]{1,0:T(8,128)(2,1)S(1)}, bf16[512,1024]{1,0:T(8,128)(2,1)S(1)}) custom-call(bf16[128,2,8,256]{3,2,1,0:T(8,128)(2,1)S(1)} %bitcast.15, bf16[256,512]{1,0:T(8,128)(2,1)S(1)} %copy-done.11, f32[512,2]{1,0:T(8,128)S(1)} %columns.1, bf16[512,2048]{1,0:T(8,128)(2,1)S(1)} %bitcast.19, ...), custom_call_target="tpu_custom_call" | custom-call | flops 3000000000 | bytes 7000000 | tf_op jit(solution)/shard_map/encode/pallas_call | solution.py:175
  97.1 1.9 %collective-permute-start = (bf16[512,1024]{1,0:T(8,128)(2,1)S(1)}, bf16[512,1024]{1,0:T(8,128)(2,1)S(1)}, u32[]{:S(2)}, u32[]{:S(2)}) collective-permute-start(bf16[512,1024]{1,0:T(8,128)(2,1)S(1)} %get-tuple-element.13.own), channel_id=1, source_target_pairs={{0,1},{1,0},{2,3},{3,2},{4,5},{5,4},{6,7},{7,6},{8,9},{9,8},{10,11... | collective-permute-start | bytes 3145736 | tf_op jit(solution)/shard_map/ppermute | solution.py:300
  100.0 1.6 %collective-permute-done.other = bf16[512,1024]{1,0:T(8,128)(2,1)S(1)} collective-permute-done((bf16[512,1024]{1,0:T(8,128)(2,1)S(1)}, bf16[512,1024]{1,0:T(8,128)(2,1)S(1)}, u32[]{:S(2)}, u32[]{:S(2)}) %collective-permute-start) | collective-permute-done | bytes 1048608 | tf_op jit(solution)/shard_map/ppermute | solution.py:300
  102.6 1.2 copy-done.4
  103.9 1.2 copy-done.7
  105.1 1.0 copy-done.9
  106.1 1.2 copy-done.21
  107.4 1.0 copy-done.23
  108.4 1.0 copy-done.25
  109.4 3.1 %history.1._ = bf16[512,512]{1,0:T(8,128)(2,1)} custom-call(s32[1]{0:T(128)} %bitcast.user, bf16[512,512]{1,0:T(8,128)(2,1)S(1)} %copy-done.23, f32[512,512]{1,0:T(8,128)S(1)} %copy-done.21, bf16[512,512]{1,0:T(8,128)(2,1)S(1)} %copy-done.25, bf16[512,1024]{1,0:T(8,128)(2,1)S(1)} %copy-done.4, bf16[512,1024]{1,0:T(8,128)(2,1)S(1)} %copy-done.7, ...), custom_call_target="tpu_custom_call" | custom-call | flops 2000000000 | bytes 5000000 | tf_op jit(solution)/shard_map/history/pallas_call | solution.py:225
  112.5 7.8 %all-to-all-done.2 = bf16[256,8,256]{2,1,0:T(8,128)(2,1)S(1)} async-done(((bf16[256,8,256]{2,1,0:T(8,128)(2,1)}), bf16[256,8,256]{2,1,0:T(8,128)(2,1)S(1)}, u32[]{:S(2)}, u32[]{:S(2)}) %all-to-all-start.2) | async-done | bytes 1048608 | tf_op jit(solution)/shard_map/all_to_all | solution.py:288
  120.3 1.2 copy-done.5
  121.6 1.2 copy-done.8
  122.8 1.0 copy-done.10
  123.8 1.0 copy-done.17
  125.8 6.4 %candidates.1 = bf16[512,512]{1,0:T(8,128)(2,1)} custom-call(bf16[128,2,8,256]{3,2,1,0:T(8,128)(2,1)S(1)} %bitcast.14, bf16[256,512]{1,0:T(8,128)(2,1)S(1)} %copy-done.11, f32[512,2]{1,0:T(8,128)S(1)} %copy-done.19, bf16[512,2048]{1,0:T(8,128)(2,1)S(1)} %bitcast.20, f32[1,512]{1,0:T(1,128)S(1)} %copy-done.14, bf16[512,1024]{1,0:T(8,128)(2,1)S(1)} %copy-done.5, ...), custom_call_target="tpu_custom_call" | custom-call | flops 4000000000 | bytes 7000000 | tf_op jit(solution)/shard_map/candidates/pallas_call | solution.py:261
  (42 shorter events, 7.8 us)
Async XLA Ops:
  0.6 38.0 %copy-start.2 = (bf16[1024,512]{1,0:T(8,128)(2,1)S(1)}, bf16[1024,512]{1,0:T(8,128)(2,1)}, u32[]{:S(2)}) copy-start(bf16[1024,512]{1,0:T(8,128)(2,1)} %refs_1_.5) | copy-start | bytes 3145732
  41.5 39.5 %all-to-all-start.1 = ((bf16[256,8,256]{2,1,0:T(8,128)(2,1)}), bf16[256,8,256]{2,1,0:T(8,128)(2,1)S(1)}, u32[]{:S(2)}, u32[]{:S(2)}) async-start(bf16[256,8,256]{2,1,0:T(8,128)(2,1)} %bitcast.5), calls=%async_computation.1 | async-start | bytes 2097152 | tf_op jit(solution)/shard_map/all_to_all | solution.py:288
  52.8 37.5 %copy-start.11 = (bf16[256,512]{1,0:T(8,128)(2,1)S(1)}, bf16[256,512]{1,0:T(8,128)(2,1)}, u32[]{:S(2)}) copy-start(bf16[256,512]{1,0:T(8,128)(2,1)} %hot.3) | copy-start | bytes 786436
  52.8 37.5 %copy-start.14 = (f32[1,512]{1,0:T(1,128)S(1)}, f32[1,512]{1,0:T(1,128)}, u32[]{:S(2)}) copy-start(f32[1,512]{1,0:T(1,128)} %in_gain.1) | copy-start | bytes 6148
  81.0 39.4 %all-to-all-start.2 = ((bf16[256,8,256]{2,1,0:T(8,128)(2,1)}), bf16[256,8,256]{2,1,0:T(8,128)(2,1)S(1)}, u32[]{:S(2)}, u32[]{:S(2)}) async-start(bf16[256,8,256]{2,1,0:T(8,128)(2,1)} %bitcast.10), calls=%async_computation.2 | async-start | bytes 2097152 | tf_op jit(solution)/shard_map/all_to_all | solution.py:288
  90.3 4.2 %copy-start.18 = (f32[512,2]{1,0:T(8,128)}, f32[512,2]{1,0:T(8,128)S(1)}, u32[]{:S(2)}) copy-start(f32[512,2]{1,0:T(8,128)S(1)} %columns.1) | copy-start | bytes 12292
  90.3 1.7 %copy-start = (bf16[1,512,2048]{2,1,0:T(8,128)(2,1)S(1)}, bf16[1,512,2048]{2,1,0:T(8,128)(2,1)}, u32[]{:S(2)}) copy-start(bf16[1,512,2048]{2,1,0:T(8,128)(2,1)} %param.14) | copy-start | bytes 6291460
  92.0 10.6 %copy-start.15 = (f32[1,512]{1,0:T(1,128)S(1)}, f32[1,512]{1,0:T(1,128)}, u32[]{:S(2)}) copy-start(f32[1,512]{1,0:T(1,128)} %gain.5) | copy-start | bytes 6148
  94.5 1.0 copy-start.20
  97.1 4.5 %collective-permute-start = (bf16[512,1024]{1,0:T(8,128)(2,1)S(1)}, bf16[512,1024]{1,0:T(8,128)(2,1)S(1)}, u32[]{:S(2)}, u32[]{:S(2)}) collective-permute-start(bf16[512,1024]{1,0:T(8,128)(2,1)S(1)} %get-tuple-element.13.own), channel_id=1, source_target_pairs={{0,1},{1,0},{2,3},{3,2},{4,5},{5,4},{6,7},{7,6},{8,9},{9,8},{10,11... | collective-permute-start | bytes 3145736 | tf_op jit(solution)/shard_map/ppermute | solution.py:300
  99.0 1.0 copy-start.3
  101.6 1.0 copy-start.6
  102.6 1.2 copy-start.4
  103.9 1.2 copy-start.7
  105.1 1.0 copy-start.9
  106.1 1.2 copy-start.21
  107.4 1.0 copy-start.23
  108.4 1.0 copy-start.25
  109.4 10.9 %copy-start.1 = (bf16[1,512,2048]{2,1,0:T(8,128)(2,1)S(1)}, bf16[1,512,2048]{2,1,0:T(8,128)(2,1)}, u32[]{:S(2)}) copy-start(bf16[1,512,2048]{2,1,0:T(8,128)(2,1)} %param.14) | copy-start | bytes 6291460
  120.3 1.2 copy-start.5
  121.6 1.2 copy-start.8
  122.8 1.0 copy-start.10
  123.8 1.0 copy-start.17
  124.9 0.9 copy-start.19
  (5 other events, 3.7 us)

commit v2 on v1

v2 whole, which is shorter than its diff:
```python
import jax
import jax.numpy as jnp
from jax import lax
from jax.experimental import pallas as pl
from jax.experimental.pallas import tpu as pltpu
from jax.sharding import PartitionSpec as P

HEADS = 4
SLOTS = 4
LANES = 8
F32 = jnp.float32
BF16 = jnp.bfloat16
I32 = jnp.int32
VMEM_BYTES = 20 * 1024 * 1024


def iota(shape, dim):
    return lax.broadcasted_iota(I32, shape, dim)


def dot(a, b):
    return jnp.dot(a, b, preferred_element_type=F32)


def dot_nt(a, b):
    return lax.dot_general(a, b, (((1,), (1,)), ((), ())), preferred_element_type=F32)


def to_column(row):
    n = row.shape[1]
    diag = iota((n, n), 0) == iota((n, n), 1)
    return jnp.sum(jnp.where(diag, row, 0.0), axis=1, keepdims=True)


def silu(v):
    half = 0.5 * v
    return half + half * jnp.tanh(half)


def norm(z, gain):
    centred = z - jnp.mean(z, axis=1, keepdims=True)
    variance = jnp.mean(centred * centred, axis=1, keepdims=True)
    return centred * lax.rsqrt(variance + 1e-05) * gain


def ask_kernel(hist_ids, cand_ids, hot_ids, asked, picks, *, owners, shift):
    hot_count = hot_ids.shape[1]
    hot_column = to_column(hot_ids[...].astype(F32))
    total = jnp.zeros((owners, LANES), F32)
    for side, (ids_ref, first) in enumerate(((hist_ids, 0), (cand_ids, SLOTS))):
        ids = ids_ref[...]
        n = ids.shape[1]
        hit = hot_column == ids.astype(F32)
        is_hot = jnp.max(jnp.where(hit, 1.0, 0.0), axis=0, keepdims=True)
        hot_at = jnp.sum(
            jnp.where(hit, iota((hot_count, n), 0).astype(F32), 0.0), axis=0, keepdims=True
        )
        owner = lax.shift_right_logical(ids, shift)
        row = ids & ((1 << shift) - 1)
        of_cold = jnp.where(is_hot > 0.5, -1, owner)
        member = (iota((owners, n), 0) == of_cold).astype(F32)
        member_low = member.astype(BF16)
        earlier = (iota((n, n), 0) < iota((n, n), 1)).astype(F32).astype(BF16)
        before = dot(member_low, earlier)
        rank = jnp.sum(before * member, axis=0, keepdims=True)
        slot = rank + first
        here = iota((LANES, n), 0).astype(F32) == slot
        high = jnp.where(here, lax.shift_right_logical(row, 5).astype(F32), 0.0).astype(BF16)
        low = jnp.where(here, (row & 31).astype(F32), 0.0).astype(BF16)
        total = total + 32.0 * dot_nt(member_low, high) + dot_nt(member_low, low)
        cold_at = owner.astype(F32) * SLOTS + rank
        picks[side : side + 1, :] = jnp.where(is_hot > 0.5, owners * SLOTS + hot_at, cold_at)
    asked[...] = total.astype(I32)


def ask(hist_ids, cand_ids, hot_ids, owners, shift):
    n = hist_ids.shape[1]
    return pl.pallas_call(
        lambda *refs: ask_kernel(*refs, owners=owners, shift=shift),
        out_shape=(
            jax.ShapeDtypeStruct((owners, LANES), I32),
            jax.ShapeDtypeStruct((2, n), F32),
        ),
        compiler_params=pltpu.CompilerParams(vmem_limit_bytes=VMEM_BYTES),
        cost_estimate=pl.CostEstimate(flops=10**9, bytes_accessed=10**5, transcendentals=0),
        name="ask",
    )(hist_ids, cand_ids, hot_ids)


def columns_kernel(picks, columns):
    columns[:, 0:1] = to_column(picks[0:1, :])
    columns[:, 1:2] = to_column(picks[1:2, :])


def columns_of(picks):
    n = picks.shape[1]
    return pl.pallas_call(
        columns_kernel,
        out_shape=jax.ShapeDtypeStruct((n, 2), F32),
        compiler_params=pltpu.CompilerParams(vmem_limit_bytes=VMEM_BYTES),
        cost_estimate=pl.CostEstimate(flops=10**8, bytes_accessed=10**5, transcendentals=0),
        name="columns",
    )(picks)


def number_column(numbers, first):
    owners = numbers.shape[0]
    count = owners * SLOTS
    spread = lax.shift_right_logical(iota((count, owners), 0), 2) == iota((count, owners), 1)
    spread = spread.astype(F32).astype(BF16)
    high = lax.shift_right_logical(numbers, 5).astype(F32).astype(BF16)
    low = (numbers & 31).astype(F32).astype(BF16)
    every = 32.0 * dot(spread, high) + dot(spread, low)
    place = iota((count, LANES), 0) & (SLOTS - 1)
    columns = []
    for start in first:
        lane = iota((count, LANES), 1) == place + start
        columns.append(jnp.sum(jnp.where(lane, every, 0.0), axis=1, keepdims=True).astype(I32))
    return columns


def one_hot(column, width):
    hit = iota((column.shape[0], width), 1) == column
    return hit.astype(F32).astype(BF16)


def fetch_kernel(numbers, table, sent):
    owners = numbers.shape[0]
    rows, width = table.shape
    count = owners * SLOTS
    cut = width - width // 4
    n = numbers[...]
    hist, cand = number_column(n, (0, SLOTS))
    last = (iota((count, 1), 0) & (SLOTS - 1)) == SLOTS - 1
    cand = jnp.where(last, -1, cand)
    ends = [
        dot(one_hot(n[:, SLOTS + s : SLOTS + s + 1], rows), table[:, cut:])
        for s in range(SLOTS - 1)
    ]
    ends = jnp.concatenate(ends, axis=1).astype(BF16)
    rank = iota((count, owners), 0) - (SLOTS - 1)
    place = (rank == SLOTS * iota((count, owners), 1)).astype(F32).astype(BF16)
    both = dot(one_hot(cand, rows), table[:, :cut]) + dot(place, ends)
    sent[:, :, width:] = both.reshape(owners, SLOTS, cut).astype(BF16)
    whole = dot(one_hot(hist, rows), table[...])
    sent[:, :, :width] = whole.reshape(owners, SLOTS, width).astype(BF16)


def fetch(numbers, table):
    owners = numbers.shape[0]
    rows, width = table.shape
    return pl.pallas_call(
        fetch_kernel,
        out_shape=jax.ShapeDtypeStruct((owners, SLOTS, 2 * width - width // 4), BF16),
        compiler_params=pltpu.CompilerParams(vmem_limit_bytes=VMEM_BYTES),
        cost_estimate=pl.CostEstimate(
            flops=3 * 10**9, bytes_accessed=3 * 10**6, transcendentals=0
        ),
        name="fetch",
    )(numbers, table)


def picked_hist(replies, hot, column):
    owners, _, _ = replies.shape
    width = hot.shape[1]
    count = owners * SLOTS
    dense = replies[:, :, :width].astype(F32).reshape(count, width).astype(BF16)
    at = column.astype(I32)
    return dot(one_hot(at, count), dense) + dot(one_hot(at - count, hot.shape[0]), hot[...])


def picked_cand(replies, hot, column):
    owners, _, _ = replies.shape
    width = hot.shape[1]
    count = owners * SLOTS
    part = width // 4
    cut = width - part
    dense = replies[:, :, width:].astype(F32).reshape(count, cut).astype(BF16)
    at = column.astype(I32)
    slot = at & (SLOTS - 1)
    warm = dot(one_hot(at - count, hot.shape[0]), hot[...])
    begin = dot(one_hot(at, count), dense) + warm[:, :cut]
    ends = dot(one_hot(at | (SLOTS - 1), count), dense)
    end = jnp.where(slot == 0, ends[:, :part], ends[:, 2 * part :])
    end = jnp.where(slot == 1, ends[:, part : 2 * part], end)
    end = jnp.where(at < count, end, warm[:, cut:])
    return jnp.concatenate([begin, end], axis=1)


def keys_kernel(replies, hot, columns, w_in, gain, x_out, in_out, kv_out):
    width = hot.shape[1]
    x = picked_hist(replies, hot, columns[:, 0:1])
    x_out[...] = x.astype(BF16)
    inner = norm(x, gain[...]).astype(BF16)
    in_out[...] = inner
    kv_out[:, width:] = silu(dot(inner, w_in[:, width : 2 * width])).astype(BF16)
    kv_out[:, :width] = silu(dot(inner, w_in[:, 3 * width :])).astype(BF16)


def keys(replies, hot, columns, w_in, gain):
    n = columns.shape[0]
    width = hot.shape[1]
    return pl.pallas_call(
        keys_kernel,
        out_shape=(
            jax.ShapeDtypeStruct((n, width), BF16),
            jax.ShapeDtypeStruct((n, width), BF16),
            jax.ShapeDtypeStruct((n, 2 * width), BF16),
        ),
        compiler_params=pltpu.CompilerParams(vmem_limit_bytes=VMEM_BYTES),
        cost_estimate=pl.CostEstimate(
            flops=2 * 10**9, bytes_accessed=5 * 10**6, transcendentals=10**6
        ),
        name="keys",
    )(replies, hot, columns, w_in, gain)


def queries_kernel(
    replies, hot, columns, inner, w_in, gain, y_out, hist_u, hist_q, cand_u, cand_q
):
    width = hot.shape[1]
    y = picked_cand(replies, hot, columns[:, 1:2])
    y_out[...] = y.astype(BF16)
    cand_in = norm(y, gain[...]).astype(BF16)
    w_u = w_in[:, :width]
    w_q = w_in[:, 2 * width : 3 * width]
    cand_u[...] = silu(dot(cand_in, w_u))
    cand_q[...] = silu(dot(cand_in, w_q)).astype(BF16)
    hist_u[...] = silu(dot(inner[...], w_u))
    hist_q[...] = silu(dot(inner[...], w_q)).astype(BF16)


def queries(replies, hot, columns, inner, w_in, gain):
    n = columns.shape[0]
    width = hot.shape[1]
    return pl.pallas_call(
        queries_kernel,
        out_shape=(
            jax.ShapeDtypeStruct((n, width), BF16),
            jax.ShapeDtypeStruct((n, width), F32),
            jax.ShapeDtypeStruct((n, width), BF16),
            jax.ShapeDtypeStruct((n, width), F32),
            jax.ShapeDtypeStruct((n, width), BF16),
        ),
        compiler_params=pltpu.CompilerParams(vmem_limit_bytes=VMEM_BYTES),
        cost_estimate=pl.CostEstimate(
            flops=3 * 10**9, bytes_accessed=7 * 10**6, transcendentals=10**6
        ),
        name="queries",
    )(replies, hot, columns, inner, w_in, gain)


def weighed(q, k, v, head_dim, keep=None):
    s = dot_nt(q, k) * (0.5 / head_dim**0.5)
    w = s + s * jnp.tanh(s)
    if keep is not None:
        w = jnp.where(keep, w, 0.0)
    return dot(w.astype(BF16), v)


def finish(mix, gain, u, w_out, x):
    gated = (norm(mix, gain) * u).astype(BF16)
    return (x + dot(gated, w_out)).astype(BF16)


def mix_kernel(
    user, x, y, hist_u, hist_q, cand_u, cand_q, own, other, gain, w_out, hist_out, cand_out, mix, cand_mix
):
    n, width = x.shape
    head_dim = width // HEADS
    causal = iota((n, n), 1) <= iota((n, n), 0)
    for h in range(HEADS):
        at = slice(h * head_dim, (h + 1) * head_dim)
        past = slice(width + h * head_dim, width + (h + 1) * head_dim)
        mix[:, at] = weighed(hist_q[:, at], own[:, at], own[:, past], head_dim, causal)
        cand_mix[:, at] = weighed(
            cand_q[:, at], own[:, at], own[:, past], head_dim
        ) + weighed(cand_q[:, at], other[:, at], other[:, past], head_dim)

    @pl.when(user[0] == 1)
    def _():
        for h in range(HEADS):
            at = slice(h * head_dim, (h + 1) * head_dim)
            past = slice(width + h * head_dim, width + (h + 1) * head_dim)
            mix[:, at] += weighed(hist_q[:, at], other[:, at], other[:, past], head_dim)

    hist_out[...] = finish(mix[...], gain[...], hist_u[...], w_out[...], x[...].astype(F32))
    cand_out[...] = finish(
        cand_mix[...], gain[...], cand_u[...], w_out[...], y[...].astype(F32)
    )


def mixed(user, x, y, hist_u, hist_q, cand_u, cand_q, own, other, gain, w_out):
    vmem = pl.BlockSpec(memory_space=pltpu.VMEM)
    return pl.pallas_call(
        mix_kernel,
        out_shape=(jax.ShapeDtypeStruct(x.shape, BF16), jax.ShapeDtypeStruct(y.shape, BF16)),
        in_specs=[pl.BlockSpec(memory_space=pltpu.SMEM)] + [vmem] * 10,
        out_specs=(vmem, vmem),
        scratch_shapes=[pltpu.VMEM(x.shape, F32), pltpu.VMEM(y.shape, F32)],
        compiler_params=pltpu.CompilerParams(vmem_limit_bytes=VMEM_BYTES),
        cost_estimate=pl.CostEstimate(
            flops=4 * 10**9, bytes_accessed=7 * 10**6, transcendentals=4 * 10**6
        ),
        name="mix",
    )(user, x, y, hist_u, hist_q, cand_u, cand_q, own, other, gain, w_out)


def exchange(array):
    return lax.all_to_all(array, ("req", "cand"), 0, 0, tiled=True)


def per_device(table, hot_table, hot_ids, hist_ids, cand_ids, w_in, w_out, in_gain, attn_gain):
    owners = lax.axis_size("req") * lax.axis_size("cand")
    shift = (table.shape[0] - 1).bit_length()
    asked, picks = ask(hist_ids, cand_ids, hot_ids[None], owners, shift)
    numbers = exchange(asked[:, None, :])[:, 0, :]
    replies = exchange(fetch(numbers, table))
    columns = columns_of(picks)
    x, inner, own = keys(replies, hot_table, columns, w_in[0], in_gain)
    other = lax.ppermute(own, "user", [(0, 1), (1, 0)])
    y, hist_u, hist_q, cand_u, cand_q = queries(
        replies, hot_table, columns, inner, w_in[0], in_gain
    )
    user = lax.axis_index("user")[None].astype(I32)
    hist_out, cand_out = mixed(
        user, x, y, hist_u, hist_q, cand_u, cand_q, own, other, attn_gain, w_out[0]
    )
    return hist_out[None], cand_out[None]


def solution(mesh):
    rows = P(("req", "cand"), None)
    split = P(("req", "cand"), "user")
    in_specs = (rows, P(), P(), split, split, P(), P(), P(), P())
    out_specs = (P(("req", "cand"), "user", None), P(("req", "cand"), "user", None))
    return jax.shard_map(
        per_device, mesh=mesh, in_specs=in_specs, out_specs=out_specs, check_vma=False
    )
```

time: 133 us -> 123 us (0.925)
  the two profiles are of different devices: /device:TPU:8 before, /device:TPU:1 now
where the time goes in v2:
time: 123 us
  waiting for transfers between devices  42.9 us (35%)
  blocking collectives  35 us (28%)
  Pallas kernels  19 us (15%)
  starting transfers between devices  16.2 us (13%)
  local copies, waits for them, and re-layouts  9.11 us (7%)
    all_to_all x1, waiting for transfers between devices, exchange(): return lax.all_to_all(array, ('req', 'cand'), 0, 0, tiled=True)  42.9 us
    all_to_all x1, blocking collectives, exchange(): return lax.all_to_all(array, ('req', 'cand'), 0, 0, tiled=True)  35 us
    all_to_all x1, starting transfers between devices, exchange(): return lax.all_to_all(array, ('req', 'cand'), 0, 0, tiled=True)  9.49 us
    unnamed x30, local copies, waits for them, and re-layouts  9.11 us
    pallas_call x1, Pallas kernels, mixed(): pl.pallas_call(mix_kernel, out_shape=(jax.ShapeDtypeStruct(x.shape, BF16)...  8.96 us
    ppermute x1, starting transfers between devices, per_device(): other = lax.ppermute(own, 'user', [(0, 1), (1, 0)])  6.71 us
    pallas_call x1, Pallas kernels, fetch(): pl.pallas_call(fetch_kernel, out_shape=jax.ShapeDtypeStruct((owners, SLOT...  3.59 us
    pallas_call x1, Pallas kernels, queries(): pl.pallas_call(queries_kernel, out_shape=(jax.ShapeDtypeStruct((n, width)...  3.1 us
  transfers between devices with their start and end apart: 2, of which 1 were waited for; matrix products, arithmetic and copies ran while one was open for 0% of the time, Pallas kernels for 3%

profile of v2, /device:TPU:1, one launch (start us, length us, event | category | flops | bytes accessed | tf_op | source)
XLA Modules:
  0.0 122.9 jit_solution(14907682797918869900)
XLA Ops:
  0.6 0.7 copy-done.6
  1.3 0.7 copy-done.7
  2.0 0.7 copy-done.10
  2.7 1.2 %ask.1 = (s32[256,8]{1,0:T(8,128)S(1)}, f32[2,512]{1,0:T(2,128)S(1)}) custom-call(s32[1,512]{1,0:T(1,128)S(1)} %copy-done.6, s32[1,512]{1,0:T(1,128)S(1)} %copy-done.7, s32[1,256]{1,0:T(1,128)S(1)} %bitcast.15), custom_call_target="tpu_custom_call" | custom-call | flops 1000000000 | bytes 100000 | tf_op jit(solution)/shard_map/ask/pallas_call | solution.py:78
  3.9 35.0 %all_to_all.10 = s32[256,1,8]{2,1,0:T(1,128)S(1)} all-to-all(s32[256,1,8]{2,1,0:T(1,128)S(1)} %bitcast.10), channel_id=1, replica_groups=mesh['req'=8,'cand'=32,'user'=2] {'req','cand'}, dimensions={0} | all-to-all | bytes 16384 | tf_op jit(solution)/shard_map/all_to_all | solution.py:310
  38.9 3.6 %fetch.1 = bf16[256,4,896]{2,1,0:T(4,128)(2,1)S(1)} custom-call(s32[256,8]{1,0:T(8,128)S(1)} %bitcast.11, bf16[1024,512]{1,0:T(8,128)(2,1)S(1)} %copy-done.3), custom_call_target="tpu_custom_call" | custom-call | flops 3000000000 | bytes 3000000 | tf_op jit(solution)/shard_map/fetch/pallas_call | solution.py:152
  42.5 1.3 %copy-done = bf16[256,4,896]{2,1,0:T(4,128)(2,1)} copy-done((bf16[256,4,896]{2,1,0:T(4,128)(2,1)}, bf16[256,4,896]{2,1,0:T(4,128)(2,1)S(1)}, u32[]{:S(2)}) %copy-start) | copy-done | bytes 1835032
  43.7 9.5 %all-to-all-start.1 = ((bf16[256,4,896]{2,1,0:T(4,128)(2,1)}), bf16[256,4,896]{2,1,0:T(4,128)(2,1)S(1)}, u32[]{:S(2)}, u32[]{:S(2)}) async-start(bf16[256,4,896]{2,1,0:T(4,128)(2,1)} %copy-done), calls=%async_computation.1 | async-start | bytes 3670016 | tf_op jit(solution)/shard_map/all_to_all | solution.py:310
  53.3 0.2 columns.1
  53.5 42.9 %all-to-all-done.1.replies = bf16[256,4,896]{2,1,0:T(4,128)(2,1)S(1)} async-done(((bf16[256,4,896]{2,1,0:T(4,128)(2,1)}), bf16[256,4,896]{2,1,0:T(4,128)(2,1)S(1)}, u32[]{:S(2)}, u32[]{:S(2)}) %all-to-all-start.1) | async-done | bytes 1835040 | tf_op jit(solution)/shard_map/all_to_all | solution.py:310
  96.4 0.0 copy-done.5
  96.4 1.6 %copy-done.1 = bf16[1,512,2048]{2,1,0:T(8,128)(2,1)S(1)} copy-done((bf16[1,512,2048]{2,1,0:T(8,128)(2,1)S(1)}, bf16[1,512,2048]{2,1,0:T(8,128)(2,1)}, u32[]{:S(2)}) %copy-start.1) | copy-done | bytes 2097176
  98.0 1.8 %keys.1 = (bf16[512,512]{1,0:T(8,128)(2,1)S(1)}, bf16[512,512]{1,0:T(8,128)(2,1)S(1)}, bf16[512,1024]{1,0:T(8,128)(2,1)S(1)}) custom-call(bf16[256,4,896]{2,1,0:T(4,128)(2,1)S(1)} %all-to-all-done.1.replies, bf16[256,512]{1,0:T(8,128)(2,1)S(1)} %copy-done.5, f32[512,2]{1,0:T(8,128)S(1)} %columns.1, bf16[512,2048]{1,0:T(8,128)(2,1)S(1)} %bitcast.12, ...), custom_call_target="tpu_custom_call" | custom-call | flops 2000000000 | bytes 5000000 | tf_op jit(solution)/shard_map/keys/pallas_call | solution.py:203
  99.8 0.0 copy-start.11
  99.8 0.8 copy-done.11
  100.6 0.8 copy-done.13
  101.4 6.7 %collective-permute-start = (bf16[512,1024]{1,0:T(8,128)(2,1)S(1)}, bf16[512,1024]{1,0:T(8,128)(2,1)}, u32[]{:S(2)}, u32[]{:S(2)}) collective-permute-start(bf16[512,1024]{1,0:T(8,128)(2,1)S(1)} %get-tuple-element.23.own), channel_id=1, source_target_pairs={{0,1},{1,0},{2,3},{3,2},{4,5},{5,4},{6,7},{7,6},{8,9},{9,8},{10,11... | collective-permute-start | bytes 3145736 | tf_op jit(solution)/shard_map/ppermute | solution.py:321
  108.1 0.0 copy-start.2
  108.1 1.6 %copy-done.2 = bf16[1,512,2048]{2,1,0:T(8,128)(2,1)S(1)} copy-done((bf16[1,512,2048]{2,1,0:T(8,128)(2,1)S(1)}, bf16[1,512,2048]{2,1,0:T(8,128)(2,1)}, u32[]{:S(2)}) %copy-start.2) | copy-done | bytes 2097176
  109.7 1.0 copy-done.14
  110.8 3.1 %queries.1 = (bf16[512,512]{1,0:T(8,128)(2,1)S(1)}, f32[512,512]{1,0:T(8,128)S(1)}, bf16[512,512]{1,0:T(8,128)(2,1)S(1)}, f32[512,512]{1,0:T(8,128)S(1)}, bf16[512,512]{1,0:T(8,128)(2,1)S(1)}) custom-call(bf16[256,4,896]{2,1,0:T(4,128)(2,1)S(1)} %all-to-all-done.1.replies, bf16[256,512]{1,0:T(8,128)(2,1)S(1)} %copy-done.5, f32[512,2]{1,0:T(8,128)S(1)} %columns.1, ...), custom_call_target="tpu_custom_call" | custom-call | flops 3000000000 | bytes 7000000 | tf_op jit(solution)/shard_map/queries/pallas_call | solution.py:236
  113.9 0.0 collective-permute-done.other
  113.9 0.0 copy-done.4
  113.9 9.0 %mix.1 = (bf16[512,512]{1,0:T(8,128)(2,1)}, bf16[512,512]{1,0:T(8,128)(2,1)}) custom-call(s32[1]{0:T(128)} %bitcast.user, bf16[512,512]{1,0:T(8,128)(2,1)S(1)} %copy-done.12, bf16[512,512]{1,0:T(8,128)(2,1)S(1)} %get-tuple-element.18.y, f32[512,512]{1,0:T(8,128)S(1)} %get-tuple-element.19.hist_u, bf16[512,512]{1,0:T(8,128)(2,1)S(1)} %get-tuple-element.20.hist_q, ...), custom_call_target="tpu_custom_call" | custom-call | flops 4000000000 | bytes 7000000 | tf_op jit(solution)/shard_map/mix/pallas_call | solution.py:295
  (17 shorter events, 0.0 us)
Async XLA Ops:
  0.6 0.7 copy-start.6
  1.3 0.7 copy-start.7
  2.0 0.7 copy-start.10
  2.7 36.2 %copy-start.3 = (bf16[1024,512]{1,0:T(8,128)(2,1)S(1)}, bf16[1024,512]{1,0:T(8,128)(2,1)}, u32[]{:S(2)}) copy-start(bf16[1024,512]{1,0:T(8,128)(2,1)} %table.1) | copy-start | bytes 3145732
  42.5 1.3 %copy-start = (bf16[256,4,896]{2,1,0:T(4,128)(2,1)}, bf16[256,4,896]{2,1,0:T(4,128)(2,1)S(1)}, u32[]{:S(2)}) copy-start(bf16[256,4,896]{2,1,0:T(4,128)(2,1)S(1)} %fetch.1) | copy-start | bytes 5505028
  43.7 52.6 %copy-start.5 = (bf16[256,512]{1,0:T(8,128)(2,1)S(1)}, bf16[256,512]{1,0:T(8,128)(2,1)}, u32[]{:S(2)}) copy-start(bf16[256,512]{1,0:T(8,128)(2,1)} %hot.3) | copy-start | bytes 786436
  43.7 52.6 %copy-start.8 = (f32[1,512]{1,0:T(1,128)S(1)}, f32[1,512]{1,0:T(1,128)}, u32[]{:S(2)}) copy-start(f32[1,512]{1,0:T(1,128)} %gain.4) | copy-start | bytes 6148
  43.7 52.6 %all-to-all-start.1 = ((bf16[256,4,896]{2,1,0:T(4,128)(2,1)}), bf16[256,4,896]{2,1,0:T(4,128)(2,1)S(1)}, u32[]{:S(2)}, u32[]{:S(2)}) async-start(bf16[256,4,896]{2,1,0:T(4,128)(2,1)} %copy-done), calls=%async_computation.1 | async-start | bytes 3670016 | tf_op jit(solution)/shard_map/all_to_all | solution.py:310
  96.4 1.6 %copy-start.1 = (bf16[1,512,2048]{2,1,0:T(8,128)(2,1)S(1)}, bf16[1,512,2048]{2,1,0:T(8,128)(2,1)}, u32[]{:S(2)}) copy-start(bf16[1,512,2048]{2,1,0:T(8,128)(2,1)} %param.14) | copy-start | bytes 6291460
  99.8 0.8 copy-start.11
  100.6 0.8 copy-start.13
  101.4 12.5 %collective-permute-start = (bf16[512,1024]{1,0:T(8,128)(2,1)S(1)}, bf16[512,1024]{1,0:T(8,128)(2,1)}, u32[]{:S(2)}, u32[]{:S(2)}) collective-permute-start(bf16[512,1024]{1,0:T(8,128)(2,1)S(1)} %get-tuple-element.23.own), channel_id=1, source_target_pairs={{0,1},{1,0},{2,3},{3,2},{4,5},{5,4},{6,7},{7,6},{8,9},{9,8},{10,11... | collective-permute-start | bytes 3145736 | tf_op jit(solution)/shard_map/ppermute | solution.py:321
  108.1 1.6 %copy-start.2 = (bf16[1,512,2048]{2,1,0:T(8,128)(2,1)S(1)}, bf16[1,512,2048]{2,1,0:T(8,128)(2,1)}, u32[]{:S(2)}) copy-start(bf16[1,512,2048]{2,1,0:T(8,128)(2,1)} %param.14) | copy-start | bytes 6291460
  109.7 1.0 copy-start.14
  110.8 3.1 %copy-start.4 = (bf16[1,512,512]{2,1,0:T(8,128)(2,1)S(1)}, bf16[1,512,512]{2,1,0:T(8,128)(2,1)}, u32[]{:S(2)}) copy-start(bf16[1,512,512]{2,1,0:T(8,128)(2,1)} %param.15) | copy-start | bytes 1572868
  110.8 3.1 %copy-start.9 = (f32[1,512]{1,0:T(1,128)S(1)}, f32[1,512]{1,0:T(1,128)}, u32[]{:S(2)}) copy-start(f32[1,512]{1,0:T(1,128)} %gain.5) | copy-start | bytes 6148
  110.8 3.1 %copy-start.12 = (bf16[512,512]{1,0:T(8,128)(2,1)S(1)}, bf16[512,512]{1,0:T(8,128)(2,1)}, u32[]{:S(2)}) copy-start(bf16[512,512]{1,0:T(8,128)(2,1)} %copy-done.11) | copy-start | bytes 1572868

commit v3 on v2

v3 whole, which is shorter than its diff:
```python
import jax
import jax.numpy as jnp
from jax import lax
from jax.experimental import pallas as pl
from jax.experimental.pallas import tpu as pltpu
from jax.sharding import PartitionSpec as P

HEADS = 4
SLOTS = 4
LANES = 8
FETCH_PARTS = 2
F32 = jnp.float32
BF16 = jnp.bfloat16
I32 = jnp.int32
ASK_BYTES = 63 * 1024 * 1024
VMEM_BYTES = 62 * 1024 * 1024
COLUMN_BYTES = 60 * 1024 * 1024
HBM = pl.BlockSpec(memory_space=pltpu.HBM)
VMEM = pl.BlockSpec(memory_space=pltpu.VMEM)
SMEM = pl.BlockSpec(memory_space=pltpu.SMEM)
KEYS_BYTES = 63 * 1024 * 1024
LAYER_BYTES = 62 * 1024 * 1024 + 512 * 1024
DMA = pltpu.SemaphoreType.DMA


def iota(shape, dim):
    return lax.broadcasted_iota(I32, shape, dim)


def dot(a, b):
    return jnp.dot(a, b, preferred_element_type=F32)


def dot_nt(a, b):
    return lax.dot_general(a, b, (((1,), (1,)), ((), ())), preferred_element_type=F32)


def to_column(row):
    n = row.shape[1]
    diag = iota((n, n), 0) == iota((n, n), 1)
    return jnp.sum(jnp.where(diag, row, 0.0), axis=1, keepdims=True)


def silu(v):
    half = 0.5 * v
    return half + half * jnp.tanh(half)


def norm(z, gain):
    centred = z - jnp.mean(z, axis=1, keepdims=True)
    variance = jnp.mean(centred * centred, axis=1, keepdims=True)
    return centred * lax.rsqrt(variance + 1e-05) * gain


def started(pairs, sems):
    copies = [pltpu.make_async_copy(a, b, sems.at[i]) for i, (a, b) in enumerate(pairs)]
    for copy in copies:
        copy.start()
    return copies


def ask_kernel(hist_in, cand_in, hot_in, asked, picks, hist_ids, cand_ids, hot_ids, sems, *, owners, shift):
    pairs = ((hot_in, hot_ids), (hist_in, hist_ids), (cand_in, cand_ids))
    for copy in started(pairs, sems):
        copy.wait()
    hot_count = hot_ids.shape[1]
    hot_column = to_column(hot_ids[...].astype(F32))
    total = jnp.zeros((owners, LANES), F32)
    for side, (ids_ref, first) in enumerate(((hist_ids, 0), (cand_ids, SLOTS))):
        ids = ids_ref[...]
        n = ids.shape[1]
        hit = hot_column == ids.astype(F32)
        is_hot = jnp.max(jnp.where(hit, 1.0, 0.0), axis=0, keepdims=True)
        hot_at = jnp.sum(
            jnp.where(hit, iota((hot_count, n), 0).astype(F32), 0.0), axis=0, keepdims=True
        )
        owner = lax.shift_right_logical(ids, shift)
        row = ids & ((1 << shift) - 1)
        of_cold = jnp.where(is_hot > 0.5, -1, owner)
        member = (iota((owners, n), 0) == of_cold).astype(F32)
        member_low = member.astype(BF16)
        earlier = (iota((n, n), 0) < iota((n, n), 1)).astype(F32).astype(BF16)
        before = dot(member_low, earlier)
        rank = jnp.sum(before * member, axis=0, keepdims=True)
        slot = rank + first
        here = iota((LANES, n), 0).astype(F32) == slot
        high = jnp.where(here, lax.shift_right_logical(row, 5).astype(F32), 0.0).astype(BF16)
        low = jnp.where(here, (row & 31).astype(F32), 0.0).astype(BF16)
        total = total + 32.0 * dot_nt(member_low, high) + dot_nt(member_low, low)
        cold_at = owner.astype(F32) * SLOTS + rank
        picks[side : side + 1, :] = jnp.where(is_hot > 0.5, owners * SLOTS + hot_at, cold_at)
    asked[...] = total.astype(I32)


def ask(hist_ids, cand_ids, hot_ids, owners, shift):
    n = hist_ids.shape[1]
    return pl.pallas_call(
        lambda *refs: ask_kernel(*refs, owners=owners, shift=shift),
        out_shape=(
            jax.ShapeDtypeStruct((owners, LANES), I32),
            jax.ShapeDtypeStruct((2, n), F32),
        ),
        in_specs=[HBM] * 3,
        out_specs=(VMEM, VMEM),
        scratch_shapes=[
            pltpu.VMEM((1, n), I32),
            pltpu.VMEM((1, n), I32),
            pltpu.VMEM(hot_ids.shape, I32),
            DMA((3,)),
        ],
        compiler_params=pltpu.CompilerParams(vmem_limit_bytes=ASK_BYTES),
        cost_estimate=pl.CostEstimate(flops=10**9, bytes_accessed=10**5, transcendentals=0),
        name="ask",
    )(hist_ids, cand_ids, hot_ids)


def columns_kernel(picks, columns):
    columns[:, 0:1] = to_column(picks[0:1, :])
    columns[:, 1:2] = to_column(picks[1:2, :])


def columns_of(picks):
    n = picks.shape[1]
    return pl.pallas_call(
        columns_kernel,
        out_shape=jax.ShapeDtypeStruct((n, 2), F32),
        compiler_params=pltpu.CompilerParams(vmem_limit_bytes=COLUMN_BYTES),
        cost_estimate=pl.CostEstimate(flops=10**8, bytes_accessed=10**5, transcendentals=0),
        name="columns",
    )(picks)


def number_column(numbers, first):
    owners = numbers.shape[0]
    count = owners * SLOTS
    spread = lax.shift_right_logical(iota((count, owners), 0), 2) == iota((count, owners), 1)
    spread = spread.astype(F32).astype(BF16)
    high = lax.shift_right_logical(numbers, 5).astype(F32).astype(BF16)
    low = (numbers & 31).astype(F32).astype(BF16)
    every = 32.0 * dot(spread, high) + dot(spread, low)
    place = iota((count, LANES), 0) & (SLOTS - 1)
    columns = []
    for start in first:
        lane = iota((count, LANES), 1) == place + start
        columns.append(jnp.sum(jnp.where(lane, every, 0.0), axis=1, keepdims=True).astype(I32))
    return columns


def one_hot(column, width):
    hit = iota((column.shape[0], width), 1) == column
    return hit.astype(F32).astype(BF16)


def fetch_kernel(numbers, table_in, out, table, sent, sems):
    owners = numbers.shape[0]
    rows, width = table.shape
    (arrival,) = started(((table_in, table),), sems.at[pl.ds(FETCH_PARTS, 1)])
    cut = width - width // 4
    n = numbers[...]
    hist, cand = number_column(n, (0, SLOTS))
    arrival.wait()
    copies = []
    for part in range(FETCH_PARTS):
        step = owners // FETCH_PARTS
        count = step * SLOTS
        mine = slice(part * step, (part + 1) * step)
        wide = slice(part * count, (part + 1) * count)
        last = (iota((count, 1), 0) & (SLOTS - 1)) == SLOTS - 1
        ends = [
            dot(one_hot(n[mine, SLOTS + s : SLOTS + s + 1], rows), table[:, cut:])
            for s in range(SLOTS - 1)
        ]
        ends = jnp.concatenate(ends, axis=1).astype(BF16)
        rank = iota((count, step), 0) - (SLOTS - 1)
        place = (rank == SLOTS * iota((count, step), 1)).astype(F32).astype(BF16)
        begin = dot(one_hot(jnp.where(last, -1, cand[wide]), rows), table[:, :cut])
        both = begin + dot(place, ends)
        sent[mine, :, width:] = both.reshape(step, SLOTS, cut).astype(BF16)
        whole = dot(one_hot(hist[wide], rows), table[...])
        sent[mine, :, :width] = whole.reshape(step, SLOTS, width).astype(BF16)
        copies.append(pltpu.make_async_copy(sent.at[mine], out.at[mine], sems.at[part]))
        copies[-1].start()
    for copy in copies:
        copy.wait()


def fetch(numbers, table):
    owners = numbers.shape[0]
    rows, width = table.shape
    shape = (owners, SLOTS, 2 * width - width // 4)
    return pl.pallas_call(
        fetch_kernel,
        out_shape=jax.ShapeDtypeStruct(shape, BF16),
        in_specs=[VMEM, HBM],
        out_specs=HBM,
        scratch_shapes=[
            pltpu.VMEM(table.shape, BF16),
            pltpu.VMEM(shape, BF16),
            DMA((FETCH_PARTS + 1,)),
        ],
        compiler_params=pltpu.CompilerParams(vmem_limit_bytes=VMEM_BYTES),
        cost_estimate=pl.CostEstimate(
            flops=3 * 10**9, bytes_accessed=3 * 10**6, transcendentals=0
        ),
        name="fetch",
    )(numbers, table)


def picked_hist(replies, hot, column, arrival):
    owners, _, width = replies.shape
    count = owners * SLOTS
    at = column.astype(I32)
    warm = dot(one_hot(at - count, hot.shape[0]), hot[...])
    cold = one_hot(at, count)
    arrival.wait()
    dense = replies[...].astype(F32).reshape(count, width).astype(BF16)
    return dot(cold, dense) + warm


def picked_cand(replies, hot, column, arrival):
    owners, _, cut = replies.shape
    count = owners * SLOTS
    part = hot.shape[1] - cut
    at = column.astype(I32)
    slot = at & (SLOTS - 1)
    warm = dot(one_hot(at - count, hot.shape[0]), hot[...])
    arrival.wait()
    dense = replies[...].astype(F32).reshape(count, cut).astype(BF16)
    begin = dot(one_hot(at, count), dense) + warm[:, :cut]
    ends = dot(one_hot(at | (SLOTS - 1), count), dense)
    end = jnp.where(slot == 0, ends[:, :part], ends[:, 2 * part :])
    end = jnp.where(slot == 1, ends[:, part : 2 * part], end)
    end = jnp.where(at < count, end, warm[:, cut:])
    return jnp.concatenate([begin, end], axis=1)


def keys_kernel(
    hot, columns, gain, replies_in, w_in, x_out, in_out, kv_out,
    replies, x_own, in_own, kv_own, w_v, w_k, sems,
):
    width = hot.shape[1]
    side = pl.ds(0, width)
    (arrival,) = started(((replies_in.at[:, :, side], replies),), sems.at[pl.ds(6, 1)])
    at_v = pl.ds(width, width)
    at_k = pl.ds(3 * width, width)
    v_in, k_in = started(((w_in.at[:, at_v], w_v), (w_in.at[:, at_k], w_k)), sems)
    x = picked_hist(replies, hot, columns[:, 0:1], arrival)
    x_own[...] = x.astype(BF16)
    inner = norm(x, gain[...]).astype(BF16)
    in_own[...] = inner
    done = started(((x_own, x_out), (in_own, in_out)), sems.at[pl.ds(2, 2)])
    v_in.wait()
    kv_own[:, width:] = silu(dot(inner, w_v[...])).astype(BF16)
    lower = pl.ds(0, width)
    done += started(
        ((kv_own.at[:, at_v], kv_out.at[:, at_v]),), sems.at[pl.ds(4, 1)]
    )
    k_in.wait()
    kv_own[:, :width] = silu(dot(inner, w_k[...])).astype(BF16)
    done += started(
        ((kv_own.at[:, lower], kv_out.at[:, lower]),), sems.at[pl.ds(5, 1)]
    )
    for copy in done:
        copy.wait()


def keys(replies, hot, columns, w_in, gain):
    n = columns.shape[0]
    width = hot.shape[1]
    return pl.pallas_call(
        keys_kernel,
        out_shape=(
            jax.ShapeDtypeStruct((n, width), BF16),
            jax.ShapeDtypeStruct((n, width), BF16),
            jax.ShapeDtypeStruct((n, 2 * width), BF16),
        ),
        in_specs=[VMEM] * 3 + [HBM] * 2,
        out_specs=(HBM, HBM, HBM),
        scratch_shapes=[
            pltpu.VMEM((replies.shape[0], SLOTS, width), BF16),
            pltpu.VMEM((n, width), BF16),
            pltpu.VMEM((n, width), BF16),
            pltpu.VMEM((n, 2 * width), BF16),
            pltpu.VMEM((width, width), BF16),
            pltpu.VMEM((width, width), BF16),
            DMA((7,)),
        ],
        compiler_params=pltpu.CompilerParams(vmem_limit_bytes=KEYS_BYTES),
        cost_estimate=pl.CostEstimate(
            flops=2 * 10**9, bytes_accessed=5 * 10**6, transcendentals=10**6
        ),
        name="keys",
    )(hot, columns, gain, replies, w_in)


def weights(q, k, head_dim):
    half = dot_nt(q, k) * (0.5 / head_dim**0.5)
    return half + half * jnp.tanh(half)


def layer_kernel(
    user, hot, columns, in_gain, gain, replies_in, x_in, hist_in, own_in, other_in, w_in, w_last,
    hist_out, cand_out,
    replies, xs, ins, own, other, w_q, w_u, w_out, qs, us, mix, outs, sems,
):
    n, width = x_in.shape
    head_dim = width // HEADS
    hist, cand = pl.ds(0, n), pl.ds(n, n)
    arrival, in_q, in_in, in_u, in_own, in_other, in_out, in_x = started(
        (
            (replies_in.at[:, :, pl.ds(width, replies.shape[2])], replies),
            (w_in.at[:, pl.ds(2 * width, width)], w_q),
            (hist_in, ins.at[hist]),
            (w_in.at[:, pl.ds(0, width)], w_u),
            (own_in, own),
            (other_in, other),
            (w_last, w_out),
            (x_in, xs.at[hist]),
        ),
        sems,
    )
    y = picked_cand(replies, hot, columns[:, 1:2], arrival)
    xs[cand, :] = y.astype(BF16)
    ins[cand, :] = norm(y, in_gain[...]).astype(BF16)
    in_q.wait()
    in_in.wait()
    qs[...] = silu(dot(ins[...], w_q[...])).astype(BF16)
    in_u.wait()
    us[...] = silu(dot(ins[...], w_u[...]))
    in_own.wait()
    in_other.wait()
    causal = iota((n, n), 1) <= iota((n, n), 0)

    def heads(everyone):
        for h in range(HEADS):
            at = slice(h * head_dim, (h + 1) * head_dim)
            past = slice(width + h * head_dim, width + (h + 1) * head_dim)
            near = weights(qs[:, at], own[:, at], head_dim)
            near = jnp.concatenate([jnp.where(causal, near[:n], 0.0), near[n:]], axis=0)
            total = dot(near.astype(BF16), own[:, past])
            if everyone:
                far = weights(qs[:, at], other[:, at], head_dim)
                mix[:, at] = total + dot(far.astype(BF16), other[:, past])
            else:
                far = weights(qs[n:, at], other[:, at], head_dim)
                mix[:n, at] = total[:n]
                mix[n:, at] = total[n:] + dot(far.astype(BF16), other[:, past])

    @pl.when(user[0] == 1)
    def _():
        heads(True)

    @pl.when(user[0] == 0)
    def _():
        heads(False)

    in_out.wait()
    in_x.wait()
    done = []
    for i, (rows, out) in enumerate(((hist, hist_out), (cand, cand_out))):
        gated = (norm(mix[rows, :], gain[...]) * us[rows, :]).astype(BF16)
        outs[rows, :] = (xs[rows, :].astype(F32) + dot(gated, w_out[...])).astype(BF16)
        done += started(((outs.at[rows], out),), sems.at[pl.ds(8 + i, 1)])
    for copy in done:
        copy.wait()


def layer(user, replies, hot, columns, in_gain, gain, x, hist_in, own, other, w_in, w_out):
    n, width = x.shape
    shape = jax.ShapeDtypeStruct(x.shape, BF16)
    return pl.pallas_call(
        layer_kernel,
        out_shape=(shape, shape),
        in_specs=[SMEM] + [VMEM] * 4 + [HBM] * 7,
        out_specs=(HBM, HBM),
        scratch_shapes=[
            pltpu.VMEM((replies.shape[0], SLOTS, replies.shape[2] - width), BF16),
            pltpu.VMEM((2 * n, width), BF16),
            pltpu.VMEM((2 * n, width), BF16),
            pltpu.VMEM((n, 2 * width), BF16),
            pltpu.VMEM((n, 2 * width), BF16),
            pltpu.VMEM((width, width), BF16),
            pltpu.VMEM((width, width), BF16),
            pltpu.VMEM((width, width), BF16),
            pltpu.VMEM((2 * n, width), BF16),
            pltpu.VMEM((2 * n, width), F32),
            pltpu.VMEM((2 * n, width), F32),
            pltpu.VMEM((2 * n, width), BF16),
            DMA((10,)),
        ],
        compiler_params=pltpu.CompilerParams(vmem_limit_bytes=LAYER_BYTES),
        cost_estimate=pl.CostEstimate(
            flops=6 * 10**9, bytes_accessed=9 * 10**6, transcendentals=6 * 10**6
        ),
        name="layer",
    )(user, hot, columns, in_gain, gain, replies, x, hist_in, own, other, w_in, w_out)


def exchange(array):
    return lax.all_to_all(array, ("req", "cand"), 0, 0, tiled=True)


def per_device(table, hot_table, hot_ids, hist_ids, cand_ids, w_in, w_out, in_gain, attn_gain):
    owners = lax.axis_size("req") * lax.axis_size("cand")
    shift = (table.shape[0] - 1).bit_length()
    asked, picks = ask(hist_ids, cand_ids, hot_ids[None], owners, shift)
    numbers = exchange(asked[:, None, :])[:, 0, :]
    replies = exchange(fetch(numbers, table))
    columns = columns_of(picks)
    x, inner, own = keys(replies, hot_table, columns, w_in[0], in_gain)
    other = lax.ppermute(own, "user", [(0, 1), (1, 0)])
    user = lax.axis_index("user")[None].astype(I32)
    hist_out, cand_out = layer(
        user,
        replies,
        hot_table,
        columns,
        in_gain,
        attn_gain,
        x,
        inner,
        own,
        other,
        w_in[0],
        w_out[0],
    )
    return hist_out[None], cand_out[None]


def solution(mesh):
    rows = P(("req", "cand"), None)
    split = P(("req", "cand"), "user")
    in_specs = (rows, P(), P(), split, split, P(), P(), P(), P())
    out_specs = (P(("req", "cand"), "user", None), P(("req", "cand"), "user", None))
    return jax.shard_map(
        per_device, mesh=mesh, in_specs=in_specs, out_specs=out_specs, check_vma=False
    )
```

time: 123 us -> 128 us (1.041)
  Pallas kernels: 19 us -> 28.6 us
  local copies, waits for them, and re-layouts: 9.11 us -> 0.96 us
  starting transfers between devices: 16.2 us -> 17.5 us
    unnamed x30 -> x2, local copies, waits for them, and re-layouts: 9.11 us -> 0.96 us
    pallas_call x3 -> x2, Pallas kernels: 15.7 us -> 19.2 us  [the longest x1 12.7 us: layer(): pl.pallas_call(layer_kernel, out_shape=(shape, shape), in_specs=[SMEM] +...]
    pallas_call x1, Pallas kernels: 1.85 us -> 5.13 us  [keys(): pl.pallas_call(keys_kernel, out_shape=(jax.ShapeDtypeStruct((n, width), B...]
    ppermute x1, waiting for transfers between devices: 0.01 us -> 2.47 us  [per_device(): other = lax.ppermute(own, 'user', [(0, 1), (1, 0)])]
    all_to_all x1, waiting for transfers between devices: 42.9 us -> 40.8 us  [exchange(): return lax.all_to_all(array, ('req', 'cand'), 0, 0, tiled=True)]
    all_to_all x1, starting transfers between devices: 9.49 us -> 10.9 us  [exchange(): return lax.all_to_all(array, ('req', 'cand'), 0, 0, tiled=True)]
    pallas_call x1, Pallas kernels: 0.21 us -> 1.62 us  [columns_of(): pl.pallas_call(columns_kernel, out_shape=jax.ShapeDtypeStruct((n, 2), F32...]
    pallas_call x1, Pallas kernels: 1.24 us -> 2.63 us  [ask(): pl.pallas_call(lambda *refs: ask_kernel(*refs, owners=owners, shift=shift...]
  transfers between devices with their start and end apart: 2 -> 2, of which waited for: 1 -> 2; matrix products, arithmetic and copies ran while one was open for 0% -> 0% of each run, Pallas kernels for 3% -> 1%
where the time goes in v3:
time: 128 us; the launch traced here: 127 us
  waiting for transfers between devices  43.3 us (34%)
  blocking collectives  35.9 us (28%)
  Pallas kernels  28.6 us (22%)
  starting transfers between devices  17.5 us (14%)
    all_to_all x1, waiting for transfers between devices, exchange(): return lax.all_to_all(array, ('req', 'cand'), 0, 0, tiled=True)  40.8 us
    all_to_all x1, blocking collectives, exchange(): return lax.all_to_all(array, ('req', 'cand'), 0, 0, tiled=True)  35.9 us
    pallas_call x1, Pallas kernels, layer(): pl.pallas_call(layer_kernel, out_shape=(shape, shape), in_specs=[SMEM] +...  12.7 us
    all_to_all x1, starting transfers between devices, exchange(): return lax.all_to_all(array, ('req', 'cand'), 0, 0, tiled=True)  10.9 us
    ppermute x1, starting transfers between devices, per_device(): other = lax.ppermute(own, 'user', [(0, 1), (1, 0)])  6.54 us
    pallas_call x1, Pallas kernels, fetch(): pl.pallas_call(fetch_kernel, out_shape=jax.ShapeDtypeStruct(shape, BF16),...  6.52 us
    pallas_call x1, Pallas kernels, keys(): pl.pallas_call(keys_kernel, out_shape=(jax.ShapeDtypeStruct((n, width), B...  5.13 us
    pallas_call x1, Pallas kernels, ask(): pl.pallas_call(lambda *refs: ask_kernel(*refs, owners=owners, shift=shift...  2.63 us
  transfers between devices with their start and end apart: 2, of which 2 were waited for; matrix products, arithmetic and copies ran while one was open for 0% of the time, Pallas kernels for 1%

profile of v3, /device:TPU:1, one launch (start us, length us, event | category | flops | bytes accessed | tf_op | source)
XLA Modules:
  0.0 127.1 jit_solution(5629575454846388728)
XLA Ops:
  0.6 2.6 %ask.1 = (s32[256,8]{1,0:T(8,128)}, f32[2,512]{1,0:T(2,128)}) custom-call(s32[1,512]{1,0:T(1,128)} %refs_0_.1, s32[1,512]{1,0:T(1,128)} %refs_1_.1, s32[1,256]{1,0:T(1,128)} %bitcast.15), custom_call_target="tpu_custom_call" | custom-call | flops 1000000000 | bytes 100000 | tf_op jit(solution)/shard_map/ask/pallas_call | solution.py:97
  3.3 35.9 %all_to_all.10 = s32[256,1,8]{2,1,0:T(1,128)} all-to-all(s32[256,1,8]{2,1,0:T(1,128)} %bitcast.10), channel_id=1, replica_groups=mesh['req'=8,'cand'=32,'user'=2] {'req','cand'}, dimensions={0} | all-to-all | bytes 16384 | tf_op jit(solution)/shard_map/all_to_all | solution.py:400
  39.2 6.5 %fetch.1 = bf16[256,4,896]{2,1,0:T(4,128)(2,1)} custom-call(s32[256,8]{1,0:T(8,128)} %bitcast.11, bf16[1024,512]{1,0:T(8,128)(2,1)} %table_in.1), custom_call_target="tpu_custom_call" | custom-call | flops 3000000000 | bytes 3000000 | tf_op jit(solution)/shard_map/fetch/pallas_call | solution.py:191
  45.7 10.9 %all-to-all-start.1 = ((bf16[256,4,896]{2,1,0:T(4,128)(2,1)}), bf16[256,4,896]{2,1,0:T(4,128)(2,1)}, u32[]{:S(2)}, u32[]{:S(2)}) async-start(bf16[256,4,896]{2,1,0:T(4,128)(2,1)} %fetch.1), calls=%async_computation.1 | async-start | bytes 3670016 | tf_op jit(solution)/shard_map/all_to_all | solution.py:400
  56.6 1.6 %columns.1 = f32[512,2]{1,0:T(8,128)} custom-call(f32[2,512]{1,0:T(2,128)} %get-tuple-element.9.picks), custom_call_target="tpu_custom_call" | custom-call | flops 100000000 | bytes 100000 | tf_op jit(solution)/shard_map/columns/pallas_call | solution.py:124
  58.2 40.8 %all-to-all-done.1.replies_in = bf16[256,4,896]{2,1,0:T(4,128)(2,1)} async-done(((bf16[256,4,896]{2,1,0:T(4,128)(2,1)}), bf16[256,4,896]{2,1,0:T(4,128)(2,1)}, u32[]{:S(2)}, u32[]{:S(2)}) %all-to-all-start.1) | async-done | bytes 1835040 | tf_op jit(solution)/shard_map/all_to_all | solution.py:400
  99.0 5.1 %keys.1 = (bf16[512,512]{1,0:T(8,128)(2,1)}, bf16[512,512]{1,0:T(8,128)(2,1)}, bf16[512,1024]{1,0:T(8,128)(2,1)}) custom-call(bf16[256,512]{1,0:T(8,128)(2,1)} %hot.3, f32[512,2]{1,0:T(8,128)} %columns.1, f32[1,512]{1,0:T(1,128)} %in_gain.1, bf16[256,4,896]{2,1,0:T(4,128)(2,1)} %all-to-all-done.1.replies_in, bf16[512,2048]{1,0:T(8,128)(2,1)} %bitcast.12), custom_call_target="tpu_custom_call" | custom-call | flops 2000000000 | bytes 5000000 | tf_op jit(solution)/shard_map/keys/pallas_call | solution.py:270
  104.2 6.5 %collective-permute-start = (bf16[512,1024]{1,0:T(8,128)(2,1)}, bf16[512,1024]{1,0:T(8,128)(2,1)S(1)}, u32[]{:S(2)}, u32[]{:S(2)}) collective-permute-start(bf16[512,1024]{1,0:T(8,128)(2,1)} %get-tuple-element.13.own_in), channel_id=1, source_target_pairs={{0,1},{1,0},{2,3},{3,2},{4,5},{5,4},{6,7},{7,6},{8,9},{9,8},{10,11... | collective-permute-start | bytes 3145736 | tf_op jit(solution)/shard_map/ppermute | solution.py:411
  110.7 2.5 %collective-permute-done.other_in = bf16[512,1024]{1,0:T(8,128)(2,1)S(1)} collective-permute-done((bf16[512,1024]{1,0:T(8,128)(2,1)}, bf16[512,1024]{1,0:T(8,128)(2,1)S(1)}, u32[]{:S(2)}, u32[]{:S(2)}) %collective-permute-start) | collective-permute-done | bytes 1048608 | tf_op jit(solution)/shard_map/ppermute | solution.py:411
  113.2 0.0 copy-start
  113.2 1.0 copy-done
  114.2 12.7 %layer.1 = (bf16[512,512]{1,0:T(8,128)(2,1)}, bf16[512,512]{1,0:T(8,128)(2,1)}) custom-call(s32[1]{0:T(128)} %bitcast.user, bf16[256,512]{1,0:T(8,128)(2,1)} %hot.3, f32[512,2]{1,0:T(8,128)} %columns.1, f32[1,512]{1,0:T(1,128)} %in_gain.1, f32[1,512]{1,0:T(1,128)} %gain.3, bf16[256,4,896]{2,1,0:T(4,128)(2,1)} %all-to-all-done.1.replies_in, ...), custom_call_target="tpu_custom_call" | custom-call | flops 6000000000 | bytes 9000000 | tf_op jit(solution)/shard_map/layer/pallas_call | solution.py:371
Async XLA Ops:
  45.7 53.4 %all-to-all-start.1 = ((bf16[256,4,896]{2,1,0:T(4,128)(2,1)}), bf16[256,4,896]{2,1,0:T(4,128)(2,1)}, u32[]{:S(2)}, u32[]{:S(2)}) async-start(bf16[256,4,896]{2,1,0:T(4,128)(2,1)} %fetch.1), calls=%async_computation.1 | async-start | bytes 3670016 | tf_op jit(solution)/shard_map/all_to_all | solution.py:400
  104.2 9.0 %collective-permute-start = (bf16[512,1024]{1,0:T(8,128)(2,1)}, bf16[512,1024]{1,0:T(8,128)(2,1)S(1)}, u32[]{:S(2)}, u32[]{:S(2)}) collective-permute-start(bf16[512,1024]{1,0:T(8,128)(2,1)} %get-tuple-element.13.own_in), channel_id=1, source_target_pairs={{0,1},{1,0},{2,3},{3,2},{4,5},{5,4},{6,7},{7,6},{8,9},{9,8},{10,11... | collective-permute-start | bytes 3145736 | tf_op jit(solution)/shard_map/ppermute | solution.py:411
  113.2 1.0 copy-start

commit v4 on v3

--- a/solution.py
+++ b/solution.py
@@ -9,17 +9,19 @@
 SLOTS = 4
 LANES = 8
 FETCH_PARTS = 2
+TABLE_PARTS = 4
+SPARE = 16
 F32 = jnp.float32
 BF16 = jnp.bfloat16
 I32 = jnp.int32
-ASK_BYTES = 63 * 1024 * 1024
-VMEM_BYTES = 62 * 1024 * 1024
-COLUMN_BYTES = 60 * 1024 * 1024
+ASK_BYTES = 64512 * 1024
+VMEM_BYTES = 53248 * 1024
+COLUMN_BYTES = 51200 * 1024
 HBM = pl.BlockSpec(memory_space=pltpu.HBM)
 VMEM = pl.BlockSpec(memory_space=pltpu.VMEM)
 SMEM = pl.BlockSpec(memory_space=pltpu.SMEM)
-KEYS_BYTES = 63 * 1024 * 1024
-LAYER_BYTES = 62 * 1024 * 1024 + 512 * 1024
+KEYS_BYTES = 50176 * 1024
+LAYER_BYTES = 50176 * 1024
 DMA = pltpu.SemaphoreType.DMA
 
 
@@ -114,22 +116,6 @@
     )(hist_ids, cand_ids, hot_ids)
 
 
-def columns_kernel(picks, columns):
-    columns[:, 0:1] = to_column(picks[0:1, :])
-    columns[:, 1:2] = to_column(picks[1:2, :])
-
-
-def columns_of(picks):
-    n = picks.shape[1]
-    return pl.pallas_call(
-        columns_kernel,
-        out_shape=jax.ShapeDtypeStruct((n, 2), F32),
-        compiler_params=pltpu.CompilerParams(vmem_limit_bytes=COLUMN_BYTES),
-        cost_estimate=pl.CostEstimate(flops=10**8, bytes_accessed=10**5, transcendentals=0),
-        name="columns",
-    )(picks)
-
-
 def number_column(numbers, first):
     owners = numbers.shape[0]
     count = owners * SLOTS
@@ -154,32 +140,42 @@
 def fetch_kernel(numbers, table_in, out, table, sent, sems):
     owners = numbers.shape[0]
     rows, width = table.shape
-    (arrival,) = started(((table_in, table),), sems.at[pl.ds(FETCH_PARTS, 1)])
     cut = width - width // 4
-    n = numbers[...]
-    hist, cand = number_column(n, (0, SLOTS))
-    arrival.wait()
+    piece = rows // TABLE_PARTS
+    pieces = [pl.ds(i * piece, piece) for i in range(TABLE_PARTS)]
+    arrivals = started(tuple((table_in.at[p], table.at[p]) for p in pieces), sems)
+    hist, cand = number_column(numbers[...], (0, SLOTS))
+    step = owners // FETCH_PARTS
+    count = step * SLOTS
+    place = iota((count, step), 0) - (SLOTS - 1) == SLOTS * iota((count, step), 1)
+    place = place.astype(F32).astype(BF16)
+    last = (iota((count, 1), 0) & (SLOTS - 1)) == SLOTS - 1
+    for arrival in arrivals:
+        arrival.wait()
     copies = []
     for part in range(FETCH_PARTS):
-        step = owners // FETCH_PARTS
-        count = step * SLOTS
         mine = slice(part * step, (part + 1) * step)
+        block = pl.ds(part * step, step)
         wide = slice(part * count, (part + 1) * count)
-        last = (iota((count, 1), 0) & (SLOTS - 1)) == SLOTS - 1
+        whole = dot(one_hot(hist[wide], rows), table[...])
+        sent[mine, :, :width] = whole.reshape(step, SLOTS, width).astype(BF16)
+        first = TABLE_PARTS + 2 * part
+        side = pl.ds(0, width)
+        copies += started(
+            ((sent.at[block, :, side], out.at[block, :, side]),), sems.at[pl.ds(first, 1)]
+        )
         ends = [
-            dot(one_hot(n[mine, SLOTS + s : SLOTS + s + 1], rows), table[:, cut:])
+            dot(one_hot(numbers[mine, SLOTS + s : SLOTS + s + 1], rows), table[:, cut:])
             for s in range(SLOTS - 1)
         ]
         ends = jnp.concatenate(ends, axis=1).astype(BF16)
-        rank = iota((count, step), 0) - (SLOTS - 1)
-        place = (rank == SLOTS * iota((count, step), 1)).astype(F32).astype(BF16)
         begin = dot(one_hot(jnp.where(last, -1, cand[wide]), rows), table[:, :cut])
         both = begin + dot(place, ends)
         sent[mine, :, width:] = both.reshape(step, SLOTS, cut).astype(BF16)
-        whole = dot(one_hot(hist[wide], rows), table[...])
-        sent[mine, :, :width] = whole.reshape(step, SLOTS, width).astype(BF16)
-        copies.append(pltpu.make_async_copy(sent.at[mine], out.at[mine], sems.at[part]))
-        copies[-1].start()
+        side = pl.ds(width, cut)
+        copies += started(
+            ((sent.at[block, :, side], out.at[block, :, side]),), sems.at[pl.ds(first + 1, 1)]
+        )
     for copy in copies:
         copy.wait()
 
@@ -196,7 +192,7 @@
         scratch_shapes=[
             pltpu.VMEM(table.shape, BF16),
             pltpu.VMEM(shape, BF16),
-            DMA((FETCH_PARTS + 1,)),
+            DMA((TABLE_PARTS + 2 * FETCH_PARTS,)),
         ],
         compiler_params=pltpu.CompilerParams(vmem_limit_bytes=VMEM_BYTES),
         cost_estimate=pl.CostEstimate(
@@ -206,26 +202,27 @@
     )(numbers, table)
 
 
-def picked_hist(replies, hot, column, arrival):
-    owners, _, width = replies.shape
+def picked_hist(replies, hot, column):
+    owners = replies.shape[0]
+    width = hot.shape[1]
     count = owners * SLOTS
     at = column.astype(I32)
     warm = dot(one_hot(at - count, hot.shape[0]), hot[...])
     cold = one_hot(at, count)
-    arrival.wait()
-    dense = replies[...].astype(F32).reshape(count, width).astype(BF16)
+    dense = replies[:, :, :width].astype(F32).reshape(count, width).astype(BF16)
     return dot(cold, dense) + warm
 
 
-def picked_cand(replies, hot, column, arrival):
-    owners, _, cut = replies.shape
+def picked_cand(replies, hot, column):
+    owners = replies.shape[0]
+    width = hot.shape[1]
     count = owners * SLOTS
-    part = hot.shape[1] - cut
+    part = width // 4
+    cut = width - part
     at = column.astype(I32)
     slot = at & (SLOTS - 1)
     warm = dot(one_hot(at - count, hot.shape[0]), hot[...])
-    arrival.wait()
-    dense = replies[...].astype(F32).reshape(count, cut).astype(BF16)
+    dense = replies[:, :, width:].astype(F32).reshape(count, cut).astype(BF16)
     begin = dot(one_hot(at, count), dense) + warm[:, :cut]
     ends = dot(one_hot(at | (SLOTS - 1), count), dense)
     end = jnp.where(slot == 0, ends[:, :part], ends[:, 2 * part :])
@@ -235,62 +232,50 @@
 
 
 def keys_kernel(
-    hot, columns, gain, replies_in, w_in, x_out, in_out, kv_out,
-    replies, x_own, in_own, kv_own, w_v, w_k, sems,
+    hot, picks, gain, replies, w_in, rows_out, kv, x_own, in_own, w_v, w_k, sems
 ):
-    width = hot.shape[1]
-    side = pl.ds(0, width)
-    (arrival,) = started(((replies_in.at[:, :, side], replies),), sems.at[pl.ds(6, 1)])
+    n, width = x_own.shape
+    x_out, in_out = rows_out.at[pl.ds(0, n)], rows_out.at[pl.ds(n, n)]
     at_v = pl.ds(width, width)
     at_k = pl.ds(3 * width, width)
     v_in, k_in = started(((w_in.at[:, at_v], w_v), (w_in.at[:, at_k], w_k)), sems)
-    x = picked_hist(replies, hot, columns[:, 0:1], arrival)
+    x = picked_hist(replies, hot, to_column(picks[0:1, :]))
     x_own[...] = x.astype(BF16)
     inner = norm(x, gain[...]).astype(BF16)
     in_own[...] = inner
     done = started(((x_own, x_out), (in_own, in_out)), sems.at[pl.ds(2, 2)])
     v_in.wait()
-    kv_own[:, width:] = silu(dot(inner, w_v[...])).astype(BF16)
-    lower = pl.ds(0, width)
-    done += started(
-        ((kv_own.at[:, at_v], kv_out.at[:, at_v]),), sems.at[pl.ds(4, 1)]
-    )
+    kv[:, width:] = silu(dot(inner, w_v[...])).astype(BF16)
     k_in.wait()
-    kv_own[:, :width] = silu(dot(inner, w_k[...])).astype(BF16)
-    done += started(
-        ((kv_own.at[:, lower], kv_out.at[:, lower]),), sems.at[pl.ds(5, 1)]
-    )
+    kv[:, :width] = silu(dot(inner, w_k[...])).astype(BF16)
     for copy in done:
         copy.wait()
 
 
-def keys(replies, hot, columns, w_in, gain):
-    n = columns.shape[0]
+def keys(replies, hot, picks, w_in, gain):
+    n = picks.shape[1]
     width = hot.shape[1]
     return pl.pallas_call(
         keys_kernel,
         out_shape=(
-            jax.ShapeDtypeStruct((n, width), BF16),
-            jax.ShapeDtypeStruct((n, width), BF16),
+            jax.ShapeDtypeStruct((SPARE * n, width), BF16),
             jax.ShapeDtypeStruct((n, 2 * width), BF16),
         ),
-        in_specs=[VMEM] * 3 + [HBM] * 2,
-        out_specs=(HBM, HBM, HBM),
+        in_specs=[VMEM] * 4 + [HBM],
+        out_specs=(HBM, VMEM),
         scratch_shapes=[
-            pltpu.VMEM((replies.shape[0], SLOTS, width), BF16),
             pltpu.VMEM((n, width), BF16),
             pltpu.VMEM((n, width), BF16),
-            pltpu.VMEM((n, 2 * width), BF16),
             pltpu.VMEM((width, width), BF16),
             pltpu.VMEM((width, width), BF16),
-            DMA((7,)),
+            DMA((4,)),
         ],
         compiler_params=pltpu.CompilerParams(vmem_limit_bytes=KEYS_BYTES),
         cost_estimate=pl.CostEstimate(
             flops=2 * 10**9, bytes_accessed=5 * 10**6, transcendentals=10**6
         ),
         name="keys",
-    )(hot, columns, gain, replies, w_in)
+    )(hot, picks, gain, replies, w_in)
 
 
 def weights(q, k, head_dim):
@@ -299,27 +284,26 @@
 
 
 def layer_kernel(
-    user, hot, columns, in_gain, gain, replies_in, x_in, hist_in, own_in, other_in, w_in, w_last,
+    user, hot, picks, in_gain, gain, replies, other_in, rows_in, own_in, w_in, w_last,
     hist_out, cand_out,
-    replies, xs, ins, own, other, w_q, w_u, w_out, qs, us, mix, outs, sems,
+    xs, ins, own, other, w_q, w_u, w_out, qs, us, mix, outs, sems,
 ):
-    n, width = x_in.shape
+    n, width = own.shape[0], own.shape[1] // 2
     head_dim = width // HEADS
     hist, cand = pl.ds(0, n), pl.ds(n, n)
-    arrival, in_q, in_in, in_u, in_own, in_other, in_out, in_x = started(
+    in_q, in_in, in_u, in_own, in_other, in_out, in_x = started(
         (
-            (replies_in.at[:, :, pl.ds(width, replies.shape[2])], replies),
             (w_in.at[:, pl.ds(2 * width, width)], w_q),
-            (hist_in, ins.at[hist]),
+            (rows_in.at[pl.ds(n, n)], ins.at[hist]),
             (w_in.at[:, pl.ds(0, width)], w_u),
             (own_in, own),
             (other_in, other),
             (w_last, w_out),
-            (x_in, xs.at[hist]),
+            (rows_in.at[hist], xs.at[hist]),
         ),
         sems,
     )
-    y = picked_cand(replies, hot, columns[:, 1:2], arrival)
+    y = picked_cand(replies, hot, to_column(picks[1:2, :]))
     xs[cand, :] = y.astype(BF16)
     ins[cand, :] = norm(y, in_gain[...]).astype(BF16)
     in_q.wait()
@@ -360,21 +344,20 @@
     for i, (rows, out) in enumerate(((hist, hist_out), (cand, cand_out))):
         gated = (norm(mix[rows, :], gain[...]) * us[rows, :]).astype(BF16)
         outs[rows, :] = (xs[rows, :].astype(F32) + dot(gated, w_out[...])).astype(BF16)
-        done += started(((outs.at[rows], out),), sems.at[pl.ds(8 + i, 1)])
+        done += started(((outs.at[rows], out),), sems.at[pl.ds(7 + i, 1)])
     for copy in done:
         copy.wait()
 
 
-def layer(user, replies, hot, columns, in_gain, gain, x, hist_in, own, other, w_in, w_out):
-    n, width = x.shape
-    shape = jax.ShapeDtypeStruct(x.shape, BF16)
+def layer(user, replies, hot, picks, in_gain, gain, rows, own, other, w_in, w_out):
+    n, width = own.shape[0], own.shape[1] // 2
+    shape = jax.ShapeDtypeStruct((n, width), BF16)
     return pl.pallas_call(
         layer_kernel,
         out_shape=(shape, shape),
-        in_specs=[SMEM] + [VMEM] * 4 + [HBM] * 7,
+        in_specs=[SMEM] + [VMEM] * 5 + [HBM] * 5,
         out_specs=(HBM, HBM),
         scratch_shapes=[
-            pltpu.VMEM((replies.shape[0], SLOTS, replies.shape[2] - width), BF16),
             pltpu.VMEM((2 * n, width), BF16),
             pltpu.VMEM((2 * n, width), BF16),
             pltpu.VMEM((n, 2 * width), BF16),
@@ -386,14 +369,14 @@
             pltpu.VMEM((2 * n, width), F32),
             pltpu.VMEM((2 * n, width), F32),
             pltpu.VMEM((2 * n, width), BF16),
-            DMA((10,)),
+            DMA((9,)),
         ],
         compiler_params=pltpu.CompilerParams(vmem_limit_bytes=LAYER_BYTES),
         cost_estimate=pl.CostEstimate(
             flops=6 * 10**9, bytes_accessed=9 * 10**6, transcendentals=6 * 10**6
         ),
         name="layer",
-    )(user, hot, columns, in_gain, gain, replies, x, hist_in, own, other, w_in, w_out)
+    )(user, hot, picks, in_gain, gain, replies, other, rows, own, w_in, w_out)
 
 
 def exchange(array):
@@ -406,19 +389,17 @@
     asked, picks = ask(hist_ids, cand_ids, hot_ids[None], owners, shift)
     numbers = exchange(asked[:, None, :])[:, 0, :]
     replies = exchange(fetch(numbers, table))
-    columns = columns_of(picks)
-    x, inner, own = keys(replies, hot_table, columns, w_in[0], in_gain)
+    rows, own = keys(replies, hot_table, picks, w_in[0], in_gain)
     other = lax.ppermute(own, "user", [(0, 1), (1, 0)])
     user = lax.axis_index("user")[None].astype(I32)
     hist_out, cand_out = layer(
         user,
         replies,
         hot_table,
-        columns,
+        picks,
         in_gain,
         attn_gain,
-        x,
-        inner,
+        rows,
         own,
         other,
         w_in[0],

time: 128 us -> 121 us (0.945)
  blocking collectives: 35.9 us -> 88.3 us
  waiting for transfers between devices: 43.3 us -> 2.39 us
  starting transfers between devices: 17.5 us -> 6.73 us
  Pallas kernels: 28.6 us -> 20.5 us
    all_to_all x1 -> x2, blocking collectives: 35.9 us -> 88.3 us  [exchange(): return lax.all_to_all(array, ('req', 'cand'), 0, 0, tiled=True)]
    all_to_all x1 -> x0, waiting for transfers between devices: 40.8 us -> none  [exchange(): return lax.all_to_all(array, ('req', 'cand'), 0, 0, tiled=True)]
    all_to_all x1 -> x0, starting transfers between devices: 10.9 us -> none  [exchange(): return lax.all_to_all(array, ('req', 'cand'), 0, 0, tiled=True)]
    pallas_call x2 -> x1, Pallas kernels: 6.75 us -> 2.19 us  [keys(): pl.pallas_call(keys_kernel, out_shape=(jax.ShapeDtypeStruct((SPARE * n, w...]
    pallas_call x1, Pallas kernels: 12.7 us -> 10.8 us  [layer(): pl.pallas_call(layer_kernel, out_shape=(shape, shape), in_specs=[SMEM] +...]
    pallas_call x1, Pallas kernels: 6.52 us -> 4.86 us  [fetch(): pl.pallas_call(fetch_kernel, out_shape=jax.ShapeDtypeStruct(shape, BF16),...]
  transfers between devices with their start and end apart: 2 -> 1, of which waited for: 2 -> 1; matrix products, arithmetic and copies ran while one was open for 0% -> 0% of each run, Pallas kernels for 1% -> 0%
where the time goes in v4:
time: 121 us
  blocking collectives  88.3 us (73%)
  Pallas kernels  20.5 us (17%)
  starting transfers between devices  6.73 us (6%)
  waiting for transfers between devices  2.39 us (2%)
  local copies, waits for them, and re-layouts  2.21 us (2%)
    all_to_all x2, blocking collectives, exchange(): return lax.all_to_all(array, ('req', 'cand'), 0, 0, tiled=True)  88.3 us
    pallas_call x1, Pallas kernels, layer(): pl.pallas_call(layer_kernel, out_shape=(shape, shape), in_specs=[SMEM] +...  10.8 us
    ppermute x1, starting transfers between devices, per_device(): other = lax.ppermute(own, 'user', [(0, 1), (1, 0)])  6.73 us
    pallas_call x1, Pallas kernels, fetch(): pl.pallas_call(fetch_kernel, out_shape=jax.ShapeDtypeStruct(shape, BF16),...  4.86 us
    pallas_call x1, Pallas kernels, ask(): pl.pallas_call(lambda *refs: ask_kernel(*refs, owners=owners, shift=shift...  2.63 us
  transfers between devices with their start and end apart: 1, of which 1 were waited for; matrix products, arithmetic and copies ran while one was open for 0% of the time, Pallas kernels for 0%

profile of v4, /device:TPU:1, one launch (start us, length us, event | category | flops | bytes accessed | tf_op | source)
XLA Modules:
  0.0 120.9 jit_solution(2132500924750910849)
XLA Ops:
  0.6 2.6 %ask.1 = (s32[256,8]{1,0:T(8,128)}, f32[2,512]{1,0:T(2,128)}) custom-call(s32[1,512]{1,0:T(1,128)} %refs_0_.1, s32[1,512]{1,0:T(1,128)} %refs_1_.1, s32[1,256]{1,0:T(1,128)} %bitcast.15), custom_call_target="tpu_custom_call" | custom-call | flops 1000000000 | bytes 100000 | tf_op jit(solution)/shard_map/ask/pallas_call | solution.py:99
  3.3 35.1 %all_to_all.10 = s32[256,1,8]{2,1,0:T(1,128)S(1)} all-to-all(s32[256,1,8]{2,1,0:T(1,128)} %bitcast.12), channel_id=1, replica_groups=mesh['req'=8,'cand'=32,'user'=2] {'req','cand'}, dimensions={0} | all-to-all | bytes 16384 | tf_op jit(solution)/shard_map/all_to_all | solution.py:383
  38.4 0.0 copy-start
  38.4 1.2 %copy-done = bf16[1024,512]{1,0:T(8,128)(2,1)S(1)} copy-done((bf16[1024,512]{1,0:T(8,128)(2,1)S(1)}, bf16[1024,512]{1,0:T(8,128)(2,1)}, u32[]{:S(2)}) %copy-start) | copy-done | bytes 1048600
  39.6 4.9 %fetch.1 = bf16[256,4,896]{2,1,0:T(4,128)(2,1)} custom-call(s32[256,8]{1,0:T(8,128)S(1)} %bitcast.10, bf16[1024,512]{1,0:T(8,128)(2,1)S(1)} %copy-done), custom_call_target="tpu_custom_call" | custom-call | flops 3000000000 | bytes 3000000 | tf_op jit(solution)/shard_map/fetch/pallas_call | solution.py:187
  44.5 0.0 copy-start.2
  44.5 0.0 copy-start.4
  44.5 0.0 copy-start.6
  44.5 53.2 %all_to_all.11.replies = bf16[256,4,896]{2,1,0:T(4,128)(2,1)S(1)} all-to-all(bf16[256,4,896]{2,1,0:T(4,128)(2,1)} %fetch.1), channel_id=1, replica_groups=mesh['req'=8,'cand'=32,'user'=2] {'req','cand'}, dimensions={0} | all-to-all | bytes 3670016 | tf_op jit(solution)/shard_map/all_to_all | solution.py:383
  97.7 0.0 copy-done.2
  97.7 0.0 copy-done.4
  97.7 0.0 copy-done.6
  97.7 0.0 copy-start.1
  97.7 0.0 copy-start.5
  97.7 2.2 %keys.1 = (bf16[8192,512]{1,0:T(8,128)(2,1)}, bf16[512,1024]{1,0:T(8,128)(2,1)S(1)}) custom-call(bf16[256,512]{1,0:T(8,128)(2,1)S(1)} %copy-done.2, f32[2,512]{1,0:T(2,128)S(1)} %copy-done.6, f32[1,512]{1,0:T(1,128)S(1)} %copy-done.4, bf16[256,4,896]{2,1,0:T(4,128)(2,1)S(1)} %all_to_all.11.replies, bf16[512,2048]{1,0:T(8,128)(2,1)} %bitcast.13), custom_call_target="tpu_custom_call" | custom-call | flops 2000000000 | bytes 5000000 | tf_op jit(solution)/shard_map/keys/pallas_call | solution.py:258
  99.9 6.7 %collective-permute-start = (bf16[512,1024]{1,0:T(8,128)(2,1)S(1)}, bf16[512,1024]{1,0:T(8,128)(2,1)}, u32[]{:S(2)}, u32[]{:S(2)}) collective-permute-start(bf16[512,1024]{1,0:T(8,128)(2,1)S(1)} %get-tuple-element.10.own_in), channel_id=1, source_target_pairs={{0,1},{1,0},{2,3},{3,2},{4,5},{5,4},{6,7},{7,6},{8,9},{9,8},{10,11... | collective-permute-start | bytes 3145736 | tf_op jit(solution)/shard_map/ppermute | solution.py:393
  106.6 2.4 %collective-permute-done.other_in = bf16[512,1024]{1,0:T(8,128)(2,1)} collective-permute-done((bf16[512,1024]{1,0:T(8,128)(2,1)S(1)}, bf16[512,1024]{1,0:T(8,128)(2,1)}, u32[]{:S(2)}, u32[]{:S(2)}) %collective-permute-start) | collective-permute-done | bytes 1048608 | tf_op jit(solution)/shard_map/ppermute | solution.py:393
  109.0 0.0 copy-done.1
  109.0 0.0 copy-done.5
  109.0 0.0 copy-start.3
  109.0 0.9 copy-done.3
  110.0 10.8 %layer.1 = (bf16[512,512]{1,0:T(8,128)(2,1)}, bf16[512,512]{1,0:T(8,128)(2,1)}) custom-call(s32[1]{0:T(128)} %bitcast.user, bf16[256,512]{1,0:T(8,128)(2,1)S(1)} %copy-done.3, f32[2,512]{1,0:T(2,128)S(1)} %copy-done.6, f32[1,512]{1,0:T(1,128)S(1)} %copy-done.4, f32[1,512]{1,0:T(1,128)S(1)} %copy-done.5, bf16[256,4,896]{2,1,0:T(4,128)(2,1)S(1)} %all_to_all.11.replies, ...), custom_call_target="tpu_custom_call" | custom-call | flops 6000000000 | bytes 9000000 | tf_op jit(solution)/shard_map/layer/pallas_call | solution.py:355
Async XLA Ops:
  38.4 1.2 %copy-start = (bf16[1024,512]{1,0:T(8,128)(2,1)S(1)}, bf16[1024,512]{1,0:T(8,128)(2,1)}, u32[]{:S(2)}) copy-start(bf16[1024,512]{1,0:T(8,128)(2,1)} %table_in.1) | copy-start | bytes 3145732
  44.5 53.2 %copy-start.2 = (bf16[256,512]{1,0:T(8,128)(2,1)S(1)}, bf16[256,512]{1,0:T(8,128)(2,1)}, u32[]{:S(2)}) copy-start(bf16[256,512]{1,0:T(8,128)(2,1)} %hot.3) | copy-start | bytes 786436
  44.5 53.2 %copy-start.4 = (f32[1,512]{1,0:T(1,128)S(1)}, f32[1,512]{1,0:T(1,128)}, u32[]{:S(2)}) copy-start(f32[1,512]{1,0:T(1,128)} %in_gain.1) | copy-start | bytes 6148
  44.5 53.2 %copy-start.6 = (f32[2,512]{1,0:T(2,128)S(1)}, f32[2,512]{1,0:T(2,128)}, u32[]{:S(2)}) copy-start(f32[2,512]{1,0:T(2,128)} %get-tuple-element.8.picks) | copy-start | bytes 12292
  97.7 11.4 %copy-start.1 = (bf16[1,512,512]{2,1,0:T(8,128)(2,1)S(1)}, bf16[1,512,512]{2,1,0:T(8,128)(2,1)}, u32[]{:S(2)}) copy-start(bf16[1,512,512]{2,1,0:T(8,128)(2,1)} %param.15) | copy-start | bytes 1572868
  97.7 11.3 %copy-start.5 = (f32[1,512]{1,0:T(1,128)S(1)}, f32[1,512]{1,0:T(1,128)}, u32[]{:S(2)}) copy-start(f32[1,512]{1,0:T(1,128)} %gain.3) | copy-start | bytes 6148
  99.9 9.1 %collective-permute-start = (bf16[512,1024]{1,0:T(8,128)(2,1)S(1)}, bf16[512,1024]{1,0:T(8,128)(2,1)}, u32[]{:S(2)}, u32[]{:S(2)}) collective-permute-start(bf16[512,1024]{1,0:T(8,128)(2,1)S(1)} %get-tuple-element.10.own_in), channel_id=1, source_target_pairs={{0,1},{1,0},{2,3},{3,2},{4,5},{5,4},{6,7},{7,6},{8,9},{9,8},{10,11... | collective-permute-start | bytes 3145736 | tf_op jit(solution)/shard_map/ppermute | solution.py:393
  109.0 1.0 copy-start.3

commit v5 on v4

--- a/solution.py
+++ b/solution.py
@@ -15,13 +15,14 @@
 BF16 = jnp.bfloat16
 I32 = jnp.int32
 ASK_BYTES = 64512 * 1024
-VMEM_BYTES = 53248 * 1024
-COLUMN_BYTES = 51200 * 1024
+VMEM_BYTES = 54528 * 1024
+WARM_BYTES = 61440 * 1024
+QUERY_BYTES = 52224 * 1024
 HBM = pl.BlockSpec(memory_space=pltpu.HBM)
 VMEM = pl.BlockSpec(memory_space=pltpu.VMEM)
 SMEM = pl.BlockSpec(memory_space=pltpu.SMEM)
-KEYS_BYTES = 50176 * 1024
-LAYER_BYTES = 50176 * 1024
+KEYS_BYTES = 52224 * 1024
+LAYER_BYTES = 51200 * 1024
 DMA = pltpu.SemaphoreType.DMA
 
 
@@ -202,80 +203,180 @@
     )(numbers, table)
 
 
-def picked_hist(replies, hot, column):
+def picked_hist(replies, column, warm):
     owners = replies.shape[0]
-    width = hot.shape[1]
+    width = warm.shape[1]
     count = owners * SLOTS
-    at = column.astype(I32)
-    warm = dot(one_hot(at - count, hot.shape[0]), hot[...])
-    cold = one_hot(at, count)
     dense = replies[:, :, :width].astype(F32).reshape(count, width).astype(BF16)
-    return dot(cold, dense) + warm
-
-
-def picked_cand(replies, hot, column):
+    return dot(one_hot(column.astype(I32), count), dense) + warm[...].astype(F32)
+
+
+def picked_cand(replies, column, warm):
     owners = replies.shape[0]
-    width = hot.shape[1]
+    width = warm.shape[1]
     count = owners * SLOTS
     part = width // 4
     cut = width - part
+    dense = replies[:, :, width:].astype(F32).reshape(count, cut).astype(BF16)
     at = column.astype(I32)
     slot = at & (SLOTS - 1)
-    warm = dot(one_hot(at - count, hot.shape[0]), hot[...])
-    dense = replies[:, :, width:].astype(F32).reshape(count, cut).astype(BF16)
-    begin = dot(one_hot(at, count), dense) + warm[:, :cut]
+    hot = warm[...].astype(F32)
+    begin = dot(one_hot(at, count), dense) + hot[:, :cut]
     ends = dot(one_hot(at | (SLOTS - 1), count), dense)
     end = jnp.where(slot == 0, ends[:, :part], ends[:, 2 * part :])
     end = jnp.where(slot == 1, ends[:, part : 2 * part], end)
-    end = jnp.where(at < count, end, warm[:, cut:])
+    end = jnp.where(at < count, end, hot[:, cut:])
     return jnp.concatenate([begin, end], axis=1)
 
 
+def warm_kernel(picks, hot, out, rows, sems, *, count):
+    n = picks.shape[1]
+    for side in range(2):
+        at = to_column(picks[side : side + 1, :]).astype(I32) - count
+        rows[side * n : (side + 1) * n, :] = dot(one_hot(at, hot.shape[0]), hot[...]).astype(BF16)
+    (copy,) = started(((rows, out.at[pl.ds(0, 2 * n)]),), sems)
+    copy.wait()
+
+
+def warm_rows(picks, hot, count):
+    n = picks.shape[1]
+    width = hot.shape[1]
+    return pl.pallas_call(
+        lambda *refs: warm_kernel(*refs, count=count),
+        out_shape=jax.ShapeDtypeStruct((SPARE * n, width), BF16),
+        in_specs=[VMEM, VMEM],
+        out_specs=HBM,
+        scratch_shapes=[pltpu.VMEM((2 * n, width), BF16), DMA((1,))],
+        compiler_params=pltpu.CompilerParams(vmem_limit_bytes=WARM_BYTES),
+        cost_estimate=pl.CostEstimate(
+            flops=10**9, bytes_accessed=2 * 10**6, transcendentals=0
+        ),
+        name="warm",
+    )(picks, hot)
+
+
 def keys_kernel(
-    hot, picks, gain, replies, w_in, rows_out, kv, x_own, in_own, w_v, w_k, sems
+    picks, gain, replies, warm_in, w_in, rows_out, kv, rows, ins, warm, w_v, w_k, sems
 ):
-    n, width = x_own.shape
-    x_out, in_out = rows_out.at[pl.ds(0, n)], rows_out.at[pl.ds(n, n)]
-    at_v = pl.ds(width, width)
-    at_k = pl.ds(3 * width, width)
-    v_in, k_in = started(((w_in.at[:, at_v], w_v), (w_in.at[:, at_k], w_k)), sems)
-    x = picked_hist(replies, hot, to_column(picks[0:1, :]))
-    x_own[...] = x.astype(BF16)
+    n, width = warm.shape[0] // 2, warm.shape[1]
+    hist, cand = pl.ds(0, n), pl.ds(n, n)
+    in_cand, in_hist, in_v, in_k = started(
+        (
+            (warm_in.at[cand], warm.at[cand]),
+            (warm_in.at[hist], warm.at[hist]),
+            (w_in.at[:, pl.ds(width, width)], w_v),
+            (w_in.at[:, pl.ds(3 * width, width)], w_k),
+        ),
+        sems,
+    )
+    column = to_column(picks[1:2, :])
+    in_cand.wait()
+    y = picked_cand(replies, column, warm.at[cand])
+    rows[cand, :] = y.astype(BF16)
+    ins[cand, :] = norm(y, gain[...]).astype(BF16)
+    done = started(
+        (
+            (rows.at[cand], rows_out.at[cand]),
+            (ins.at[cand], rows_out.at[pl.ds(3 * n, n)]),
+        ),
+        sems.at[pl.ds(4, 2)],
+    )
+    column = to_column(picks[0:1, :])
+    in_hist.wait()
+    x = picked_hist(replies, column, warm.at[hist])
+    rows[hist, :] = x.astype(BF16)
     inner = norm(x, gain[...]).astype(BF16)
-    in_own[...] = inner
-    done = started(((x_own, x_out), (in_own, in_out)), sems.at[pl.ds(2, 2)])
-    v_in.wait()
+    ins[hist, :] = inner
+    done += started(
+        (
+            (rows.at[hist], rows_out.at[hist]),
+            (ins.at[hist], rows_out.at[pl.ds(2 * n, n)]),
+        ),
+        sems.at[pl.ds(6, 2)],
+    )
+    in_v.wait()
     kv[:, width:] = silu(dot(inner, w_v[...])).astype(BF16)
-    k_in.wait()
+    in_k.wait()
     kv[:, :width] = silu(dot(inner, w_k[...])).astype(BF16)
     for copy in done:
         copy.wait()
 
 
-def keys(replies, hot, picks, w_in, gain):
+def keys(replies, warm, picks, w_in, gain):
     n = picks.shape[1]
-    width = hot.shape[1]
+    width = warm.shape[1]
     return pl.pallas_call(
         keys_kernel,
         out_shape=(
             jax.ShapeDtypeStruct((SPARE * n, width), BF16),
             jax.ShapeDtypeStruct((n, 2 * width), BF16),
         ),
-        in_specs=[VMEM] * 4 + [HBM],
+        in_specs=[VMEM] * 3 + [HBM] * 2,
         out_specs=(HBM, VMEM),
         scratch_shapes=[
-            pltpu.VMEM((n, width), BF16),
-            pltpu.VMEM((n, width), BF16),
+            pltpu.VMEM((2 * n, width), BF16),
+            pltpu.VMEM((2 * n, width), BF16),
+            pltpu.VMEM((2 * n, width), BF16),
             pltpu.VMEM((width, width), BF16),
             pltpu.VMEM((width, width), BF16),
-            DMA((4,)),
+            DMA((8,)),
         ],
         compiler_params=pltpu.CompilerParams(vmem_limit_bytes=KEYS_BYTES),
         cost_estimate=pl.CostEstimate(
-            flops=2 * 10**9, bytes_accessed=5 * 10**6, transcendentals=10**6
+            flops=3 * 10**9, bytes_accessed=6 * 10**6, transcendentals=10**6
         ),
         name="keys",
-    )(hot, picks, gain, replies, w_in)
+    )(picks, gain, replies, warm, w_in)
+
+
+def queries_kernel(rows_in, w_in, u_out, qs, us, ins, w_u, w_q, sems):
+    n, width = ins.shape[0] // 2, ins.shape[1]
+    hist, cand = pl.ds(0, n), pl.ds(n, n)
+    in_hist, in_u, in_cand, in_q = started(
+        (
+            (rows_in.at[pl.ds(2 * n, n)], ins.at[hist]),
+            (w_in.at[:, pl.ds(0, width)], w_u),
+            (rows_in.at[pl.ds(3 * n, n)], ins.at[cand]),
+            (w_in.at[:, pl.ds(2 * width, width)], w_q),
+        ),
+        sems,
+    )
+    in_hist.wait()
+    in_u.wait()
+    us[hist, :] = silu(dot(ins[hist, :], w_u[...]))
+    done = started(((us.at[hist], u_out.at[hist]),), sems.at[pl.ds(4, 1)])
+    in_cand.wait()
+    us[cand, :] = silu(dot(ins[cand, :], w_u[...]))
+    done += started(((us.at[cand], u_out.at[cand]),), sems.at[pl.ds(5, 1)])
+    in_q.wait()
+    qs[...] = silu(dot(ins[...], w_q[...])).astype(BF16)
+    for copy in done:
+        copy.wait()
+
+
+def queries(rows, w_in):
+    n, width = rows.shape[0] // SPARE, rows.shape[1]
+    return pl.pallas_call(
+        queries_kernel,
+        out_shape=(
+            jax.ShapeDtypeStruct((SPARE * n, width), F32),
+            jax.ShapeDtypeStruct((2 * n, width), BF16),
+        ),
+        in_specs=[HBM, HBM],
+        out_specs=(HBM, VMEM),
+        scratch_shapes=[
+            pltpu.VMEM((2 * n, width), F32),
+            pltpu.VMEM((2 * n, width), BF16),
+            pltpu.VMEM((width, width), BF16),
+            pltpu.VMEM((width, width), BF16),
+            DMA((6,)),
+        ],
+        compiler_params=pltpu.CompilerParams(vmem_limit_bytes=QUERY_BYTES),
+        cost_estimate=pl.CostEstimate(
+            flops=2 * 10**9, bytes_accessed=4 * 10**6, transcendentals=10**6
+        ),
+        name="queries",
+    )(rows, w_in)
 
 
 def weights(q, k, head_dim):
@@ -284,35 +385,16 @@
 
 
 def layer_kernel(
-    user, hot, picks, in_gain, gain, replies, other_in, rows_in, own_in, w_in, w_last,
-    hist_out, cand_out,
-    xs, ins, own, other, w_q, w_u, w_out, qs, us, mix, outs, sems,
+    user, gain, qs, own, other, rows_in, us_in, w_last, hist_out, cand_out,
+    xs, us, w_out, mix, outs, sems,
 ):
     n, width = own.shape[0], own.shape[1] // 2
     head_dim = width // HEADS
     hist, cand = pl.ds(0, n), pl.ds(n, n)
-    in_q, in_in, in_u, in_own, in_other, in_out, in_x = started(
-        (
-            (w_in.at[:, pl.ds(2 * width, width)], w_q),
-            (rows_in.at[pl.ds(n, n)], ins.at[hist]),
-            (w_in.at[:, pl.ds(0, width)], w_u),
-            (own_in, own),
-            (other_in, other),
-            (w_last, w_out),
-            (rows_in.at[hist], xs.at[hist]),
-        ),
-        sems,
-    )
-    y = picked_cand(replies, hot, to_column(picks[1:2, :]))
-    xs[cand, :] = y.astype(BF16)
-    ins[cand, :] = norm(y, in_gain[...]).astype(BF16)
-    in_q.wait()
-    in_in.wait()
-    qs[...] = silu(dot(ins[...], w_q[...])).astype(BF16)
-    in_u.wait()
-    us[...] = silu(dot(ins[...], w_u[...]))
-    in_own.wait()
-    in_other.wait()
+    both = pl.ds(0, 2 * n)
+    arrivals = started(
+        ((w_last, w_out), (us_in.at[both], us), (rows_in.at[both], xs)), sems
+    )
     causal = iota((n, n), 1) <= iota((n, n), 0)
 
     def heads(everyone):
@@ -338,45 +420,39 @@
     def _():
         heads(False)
 
-    in_out.wait()
-    in_x.wait()
+    for arrival in arrivals:
+        arrival.wait()
     done = []
     for i, (rows, out) in enumerate(((hist, hist_out), (cand, cand_out))):
         gated = (norm(mix[rows, :], gain[...]) * us[rows, :]).astype(BF16)
         outs[rows, :] = (xs[rows, :].astype(F32) + dot(gated, w_out[...])).astype(BF16)
-        done += started(((outs.at[rows], out),), sems.at[pl.ds(7 + i, 1)])
+        done += started(((outs.at[rows], out),), sems.at[pl.ds(3 + i, 1)])
     for copy in done:
         copy.wait()
 
 
-def layer(user, replies, hot, picks, in_gain, gain, rows, own, other, w_in, w_out):
+def layer(user, rows, us, qs, own, other, gain, w_out):
     n, width = own.shape[0], own.shape[1] // 2
     shape = jax.ShapeDtypeStruct((n, width), BF16)
     return pl.pallas_call(
         layer_kernel,
         out_shape=(shape, shape),
-        in_specs=[SMEM] + [VMEM] * 5 + [HBM] * 5,
+        in_specs=[SMEM] + [VMEM] * 4 + [HBM] * 3,
         out_specs=(HBM, HBM),
         scratch_shapes=[
             pltpu.VMEM((2 * n, width), BF16),
-            pltpu.VMEM((2 * n, width), BF16),
-            pltpu.VMEM((n, 2 * width), BF16),
-            pltpu.VMEM((n, 2 * width), BF16),
+            pltpu.VMEM((2 * n, width), F32),
             pltpu.VMEM((width, width), BF16),
-            pltpu.VMEM((width, width), BF16),
-            pltpu.VMEM((width, width), BF16),
-            pltpu.VMEM((2 * n, width), BF16),
             pltpu.VMEM((2 * n, width), F32),
-            pltpu.VMEM((2 * n, width), F32),
-            pltpu.VMEM((2 * n, width), BF16),
-            DMA((9,)),
+            pltpu.VMEM((2 * n, width), BF16),
+            DMA((5,)),
         ],
         compiler_params=pltpu.CompilerParams(vmem_limit_bytes=LAYER_BYTES),
         cost_estimate=pl.CostEstimate(
             flops=6 * 10**9, bytes_accessed=9 * 10**6, transcendentals=6 * 10**6
         ),
         name="layer",
-    )(user, hot, picks, in_gain, gain, replies, other, rows, own, w_in, w_out)
+    )(user, gain, qs, own, other, rows, us, w_out)
 
 
 def exchange(array):
@@ -389,22 +465,12 @@
     asked, picks = ask(hist_ids, cand_ids, hot_ids[None], owners, shift)
     numbers = exchange(asked[:, None, :])[:, 0, :]
     replies = exchange(fetch(numbers, table))
-    rows, own = keys(replies, hot_table, picks, w_in[0], in_gain)
+    warm = warm_rows(picks, hot_table, owners * SLOTS)
+    rows, own = keys(replies, warm, picks, w_in[0], in_gain)
     other = lax.ppermute(own, "user", [(0, 1), (1, 0)])
+    us, qs = queries(rows, w_in[0])
     user = lax.axis_index("user")[None].astype(I32)
-    hist_out, cand_out = layer(
-        user,
-        replies,
-        hot_table,
-        picks,
-        in_gain,
-        attn_gain,
-        rows,
-        own,
-        other,
-        w_in[0],
-        w_out[0],
-    )
+    hist_out, cand_out = layer(user, rows, us, qs, own, other, attn_gain, w_out[0])
     return hist_out[None], cand_out[None]
 
 

time: 121 us -> 119 us (0.983)
  blocking collectives: 88.3 us -> 35.1 us
  waiting for transfers between devices: 2.39 us -> 40.7 us
  starting transfers between devices: 6.73 us -> 16.1 us
  Pallas kernels: 20.5 us -> 25.8 us
  local copies, waits for them, and re-layouts: 2.21 us -> 0.02 us
    all_to_all x2 -> x1, blocking collectives: 88.3 us -> 35.1 us  [exchange(): return lax.all_to_all(array, ('req', 'cand'), 0, 0, tiled=True)]
    all_to_all x0 -> x1, waiting for transfers between devices: none -> 40.6 us  [exchange(): return lax.all_to_all(array, ('req', 'cand'), 0, 0, tiled=True)]
    all_to_all x0 -> x1, starting transfers between devices: none -> 9.38 us  [exchange(): return lax.all_to_all(array, ('req', 'cand'), 0, 0, tiled=True)]
    pallas_call x0 -> x2, Pallas kernels: none -> 5.63 us  [the longest x1 3.17 us: queries(): pl.pallas_call(queries_kernel, out_shape=(jax.ShapeDtypeStruct((SPARE * n...]
    pallas_call x1, Pallas kernels: 10.8 us -> 7.45 us  [layer(): pl.pallas_call(layer_kernel, out_shape=(shape, shape), in_specs=[SMEM] +...]
    pallas_call x1, Pallas kernels: 2.19 us -> 4.68 us  [keys(): pl.pallas_call(keys_kernel, out_shape=(jax.ShapeDtypeStruct((SPARE * n, w...]
    ppermute x1, waiting for transfers between devices: 2.39 us -> 0.01 us  [per_device(): other = lax.ppermute(own, 'user', [(0, 1), (1, 0)])]
    unnamed x14 -> x8, local copies, waits for them, and re-layouts: 2.21 us -> 0.02 us
  transfers between devices with their start and end apart: 1 -> 2, of which waited for: 1 -> 1; matrix products, arithmetic and copies ran while one was open for 0% -> 0% of each run, Pallas kernels for 0% -> 5%
where the time goes in v5:
time: 119 us
  waiting for transfers between devices  40.7 us (34%)
  blocking collectives  35.1 us (29%)
  Pallas kernels  25.8 us (22%)
  starting transfers between devices  16.1 us (14%)
    all_to_all x1, waiting for transfers between devices, exchange(): return lax.all_to_all(array, ('req', 'cand'), 0, 0, tiled=True)  40.6 us
    all_to_all x1, blocking collectives, exchange(): return lax.all_to_all(array, ('req', 'cand'), 0, 0, tiled=True)  35.1 us
    all_to_all x1, starting transfers between devices, exchange(): return lax.all_to_all(array, ('req', 'cand'), 0, 0, tiled=True)  9.38 us
    pallas_call x1, Pallas kernels, layer(): pl.pallas_call(layer_kernel, out_shape=(shape, shape), in_specs=[SMEM] +...  7.45 us
    ppermute x1, starting transfers between devices, per_device(): other = lax.ppermute(own, 'user', [(0, 1), (1, 0)])  6.73 us
    pallas_call x1, Pallas kernels, fetch(): pl.pallas_call(fetch_kernel, out_shape=jax.ShapeDtypeStruct(shape, BF16),...  5.41 us
    pallas_call x1, Pallas kernels, keys(): pl.pallas_call(keys_kernel, out_shape=(jax.ShapeDtypeStruct((SPARE * n, w...  4.68 us
    pallas_call x1, Pallas kernels, queries(): pl.pallas_call(queries_kernel, out_shape=(jax.ShapeDtypeStruct((SPARE * n...  3.17 us
  transfers between devices with their start and end apart: 2, of which 1 were waited for; matrix products, arithmetic and copies ran while one was open for 0% of the time, Pallas kernels for 5%

profile of v5, /device:TPU:1, one launch (start us, length us, event | category | flops | bytes accessed | tf_op | source)
XLA Modules:
  0.0 118.6 jit_solution(3784629291632879733)
XLA Ops:
  0.6 2.6 %ask.1 = (s32[256,8]{1,0:T(8,128)}, f32[2,512]{1,0:T(2,128)}) custom-call(s32[1,512]{1,0:T(1,128)} %refs_0_.1, s32[1,512]{1,0:T(1,128)} %refs_1_.2, s32[1,256]{1,0:T(1,128)} %bitcast.17), custom_call_target="tpu_custom_call" | custom-call | flops 1000000000 | bytes 100000 | tf_op jit(solution)/shard_map/ask/pallas_call | solution.py:100
  3.3 35.1 %all_to_all.10 = s32[256,1,8]{2,1,0:T(1,128)S(1)} all-to-all(s32[256,1,8]{2,1,0:T(1,128)} %bitcast.14), channel_id=1, replica_groups=mesh['req'=8,'cand'=32,'user'=2] {'req','cand'}, dimensions={0} | all-to-all | bytes 16384 | tf_op jit(solution)/shard_map/all_to_all | solution.py:459
  38.4 5.4 %fetch.1 = bf16[256,4,896]{2,1,0:T(4,128)(2,1)} custom-call(s32[256,8]{1,0:T(8,128)S(1)} %bitcast.11, bf16[1024,512]{1,0:T(8,128)(2,1)} %table_in.1), custom_call_target="tpu_custom_call" | custom-call | flops 3000000000 | bytes 3000000 | tf_op jit(solution)/shard_map/fetch/pallas_call | solution.py:188
  43.8 0.0 copy-start.1
  43.8 0.0 copy-start.2
  43.8 9.4 %all-to-all-start.1 = ((bf16[256,4,896]{2,1,0:T(4,128)(2,1)}), bf16[256,4,896]{2,1,0:T(4,128)(2,1)S(1)}, u32[]{:S(2)}, u32[]{:S(2)}) async-start(bf16[256,4,896]{2,1,0:T(4,128)(2,1)} %fetch.1), calls=%async_computation.1 | async-start | bytes 3670016 | tf_op jit(solution)/shard_map/all_to_all | solution.py:459
  53.2 2.5 %warm.1.warm_in = bf16[8192,512]{1,0:T(8,128)(2,1)} custom-call(f32[2,512]{1,0:T(2,128)} %get-tuple-element.10.refs_0_.picks, bf16[256,512]{1,0:T(8,128)(2,1)} %refs_1_.3), custom_call_target="tpu_custom_call" | custom-call | flops 1000000000 | bytes 2000000 | tf_op jit(solution)/shard_map/warm/pallas_call | solution.py:244
  55.7 40.6 %all-to-all-done.1.replies = bf16[256,4,896]{2,1,0:T(4,128)(2,1)S(1)} async-done(((bf16[256,4,896]{2,1,0:T(4,128)(2,1)}), bf16[256,4,896]{2,1,0:T(4,128)(2,1)S(1)}, u32[]{:S(2)}, u32[]{:S(2)}) %all-to-all-start.1) | async-done | bytes 1835040 | tf_op jit(solution)/shard_map/all_to_all | solution.py:459
  96.3 0.0 copy-done.1
  96.3 0.0 copy-done.2
  96.3 0.0 copy-start
  96.3 0.0 copy-start.3
  96.3 4.7 %keys.1 = (bf16[8192,512]{1,0:T(8,128)(2,1)}, bf16[512,1024]{1,0:T(8,128)(2,1)S(1)}) custom-call(f32[2,512]{1,0:T(2,128)S(1)} %copy-done.1, f32[1,512]{1,0:T(1,128)S(1)} %copy-done.2, bf16[256,4,896]{2,1,0:T(4,128)(2,1)S(1)} %all-to-all-done.1.replies, bf16[8192,512]{1,0:T(8,128)(2,1)} %warm.1.warm_in, bf16[512,2048]{1,0:T(8,128)(2,1)} %bitcast.12), custom_call_target="tpu_custom_call" | custom-call | flops 3000000000 | bytes 6000000 | tf_op jit(solution)/shard_map/keys/pallas_call | solution.py:308
  101.0 6.7 %collective-permute-start = (bf16[512,1024]{1,0:T(8,128)(2,1)S(1)}, bf16[512,1024]{1,0:T(8,128)(2,1)S(1)}, u32[]{:S(2)}, u32[]{:S(2)}) collective-permute-start(bf16[512,1024]{1,0:T(8,128)(2,1)S(1)} %get-tuple-element.14.own), channel_id=1, source_target_pairs={{0,1},{1,0},{2,3},{3,2},{4,5},{5,4},{6,7},{7,6},{8,9},{9,8},{10,11... | collective-permute-start | bytes 3145736 | tf_op jit(solution)/shard_map/ppermute | solution.py:470
  107.7 3.2 %queries.1 = (f32[8192,512]{1,0:T(8,128)}, bf16[1024,512]{1,0:T(8,128)(2,1)S(1)}) custom-call(bf16[8192,512]{1,0:T(8,128)(2,1)} %get-tuple-element.12.rows_in, bf16[512,2048]{1,0:T(8,128)(2,1)} %bitcast.13), custom_call_target="tpu_custom_call" | custom-call | flops 2000000000 | bytes 4000000 | tf_op jit(solution)/shard_map/queries/pallas_call | solution.py:359
  110.9 0.0 collective-permute-done.other
  110.9 0.0 copy-done
  110.9 0.0 copy-done.3
  111.0 7.4 %layer.1 = (bf16[512,512]{1,0:T(8,128)(2,1)}, bf16[512,512]{1,0:T(8,128)(2,1)}) custom-call(s32[1]{0:T(128)} %bitcast.user, f32[1,512]{1,0:T(1,128)S(1)} %copy-done.3, bf16[1024,512]{1,0:T(8,128)(2,1)S(1)} %get-tuple-element.13.qs, bf16[512,1024]{1,0:T(8,128)(2,1)S(1)} %get-tuple-element.14.own, bf16[512,1024]{1,0:T(8,128)(2,1)S(1)} %collective-permute-done.other, ...), custom_call_target="tpu_custom_call" | custom-call | flops 6000000000 | bytes 9000000 | tf_op jit(solution)/shard_map/layer/pallas_call | solution.py:437
Async XLA Ops:
  43.8 52.5 %copy-start.1 = (f32[2,512]{1,0:T(2,128)S(1)}, f32[2,512]{1,0:T(2,128)}, u32[]{:S(2)}) copy-start(f32[2,512]{1,0:T(2,128)} %get-tuple-element.10.refs_0_.picks) | copy-start | bytes 12292
  43.8 52.5 %copy-start.2 = (f32[1,512]{1,0:T(1,128)S(1)}, f32[1,512]{1,0:T(1,128)}, u32[]{:S(2)}) copy-start(f32[1,512]{1,0:T(1,128)} %gain.2) | copy-start | bytes 6148
  43.8 52.5 %all-to-all-start.1 = ((bf16[256,4,896]{2,1,0:T(4,128)(2,1)}), bf16[256,4,896]{2,1,0:T(4,128)(2,1)S(1)}, u32[]{:S(2)}, u32[]{:S(2)}) async-start(bf16[256,4,896]{2,1,0:T(4,128)(2,1)} %fetch.1), calls=%async_computation.1 | async-start | bytes 3670016 | tf_op jit(solution)/shard_map/all_to_all | solution.py:459
  96.3 14.6 %copy-start = (bf16[1,512,512]{2,1,0:T(8,128)(2,1)S(1)}, bf16[1,512,512]{2,1,0:T(8,128)(2,1)}, u32[]{:S(2)}) copy-start(bf16[1,512,512]{2,1,0:T(8,128)(2,1)} %param.15) | copy-start | bytes 1572868
  96.3 14.6 %copy-start.3 = (f32[1,512]{1,0:T(1,128)S(1)}, f32[1,512]{1,0:T(1,128)}, u32[]{:S(2)}) copy-start(f32[1,512]{1,0:T(1,128)} %gain.3) | copy-start | bytes 6148
  101.0 9.9 %collective-permute-start = (bf16[512,1024]{1,0:T(8,128)(2,1)S(1)}, bf16[512,1024]{1,0:T(8,128)(2,1)S(1)}, u32[]{:S(2)}, u32[]{:S(2)}) collective-permute-start(bf16[512,1024]{1,0:T(8,128)(2,1)S(1)} %get-tuple-element.14.own), channel_id=1, source_target_pairs={{0,1},{1,0},{2,3},{3,2},{4,5},{5,4},{6,7},{7,6},{8,9},{9,8},{10,11... | collective-permute-start | bytes 3145736 | tf_op jit(solution)/shard_map/ppermute | solution.py:470

commit v6 on v5

--- a/solution.py
+++ b/solution.py
@@ -9,14 +9,13 @@
 SLOTS = 4
 LANES = 8
 FETCH_PARTS = 2
-TABLE_PARTS = 4
 SPARE = 16
 F32 = jnp.float32
 BF16 = jnp.bfloat16
 I32 = jnp.int32
-ASK_BYTES = 64512 * 1024
-VMEM_BYTES = 54528 * 1024
-WARM_BYTES = 61440 * 1024
+ASK_BYTES = 53248 * 1024
+VMEM_BYTES = 53248 * 1024
+WARM_BYTES = 54528 * 1024
 QUERY_BYTES = 52224 * 1024
 HBM = pl.BlockSpec(memory_space=pltpu.HBM)
 VMEM = pl.BlockSpec(memory_space=pltpu.VMEM)
@@ -62,16 +61,13 @@
     return copies
 
 
-def ask_kernel(hist_in, cand_in, hot_in, asked, picks, hist_ids, cand_ids, hot_ids, sems, *, owners, shift):
-    pairs = ((hot_in, hot_ids), (hist_in, hist_ids), (cand_in, cand_ids))
-    for copy in started(pairs, sems):
-        copy.wait()
-    hot_count = hot_ids.shape[1]
-    hot_column = to_column(hot_ids[...].astype(F32))
+def ask_kernel(ids_in, asked, picks, *, owners, shift):
+    n = picks.shape[1]
+    hot_count = ids_in.shape[1] - 2 * n
+    hot_column = to_column(ids_in[:, 2 * n :].astype(F32))
     total = jnp.zeros((owners, LANES), F32)
-    for side, (ids_ref, first) in enumerate(((hist_ids, 0), (cand_ids, SLOTS))):
-        ids = ids_ref[...]
-        n = ids.shape[1]
+    for side, first in enumerate((0, SLOTS)):
+        ids = ids_in[:, side * n : (side + 1) * n]
         hit = hot_column == ids.astype(F32)
         is_hot = jnp.max(jnp.where(hit, 1.0, 0.0), axis=0, keepdims=True)
         hot_at = jnp.sum(
@@ -97,24 +93,17 @@
 
 def ask(hist_ids, cand_ids, hot_ids, owners, shift):
     n = hist_ids.shape[1]
+    ids = jnp.concatenate([hist_ids, cand_ids, hot_ids], axis=1)
     return pl.pallas_call(
         lambda *refs: ask_kernel(*refs, owners=owners, shift=shift),
         out_shape=(
             jax.ShapeDtypeStruct((owners, LANES), I32),
             jax.ShapeDtypeStruct((2, n), F32),
         ),
-        in_specs=[HBM] * 3,
-        out_specs=(VMEM, VMEM),
-        scratch_shapes=[
-            pltpu.VMEM((1, n), I32),
-            pltpu.VMEM((1, n), I32),
-            pltpu.VMEM(hot_ids.shape, I32),
-            DMA((3,)),
-        ],
         compiler_params=pltpu.CompilerParams(vmem_limit_bytes=ASK_BYTES),
         cost_estimate=pl.CostEstimate(flops=10**9, bytes_accessed=10**5, transcendentals=0),
         name="ask",
-    )(hist_ids, cand_ids, hot_ids)
+    )(ids)
 
 
 def number_column(numbers, first):
@@ -138,44 +127,38 @@
     return hit.astype(F32).astype(BF16)
 
 
-def fetch_kernel(numbers, table_in, out, table, sent, sems):
+def moved_down(x, rows):
+    return pltpu.roll(x.reshape(x.shape[0] // 8, 8, x.shape[1]), rows, 1).reshape(x.shape)
+
+
+def fetch_kernel(numbers, table, out, sent, sems):
     owners = numbers.shape[0]
     rows, width = table.shape
-    cut = width - width // 4
-    piece = rows // TABLE_PARTS
-    pieces = [pl.ds(i * piece, piece) for i in range(TABLE_PARTS)]
-    arrivals = started(tuple((table_in.at[p], table.at[p]) for p in pieces), sems)
+    part = width // 4
+    cut = width - part
     hist, cand = number_column(numbers[...], (0, SLOTS))
     step = owners // FETCH_PARTS
     count = step * SLOTS
-    place = iota((count, step), 0) - (SLOTS - 1) == SLOTS * iota((count, step), 1)
-    place = place.astype(F32).astype(BF16)
     last = (iota((count, 1), 0) & (SLOTS - 1)) == SLOTS - 1
-    for arrival in arrivals:
-        arrival.wait()
     copies = []
-    for part in range(FETCH_PARTS):
-        mine = slice(part * step, (part + 1) * step)
-        block = pl.ds(part * step, step)
-        wide = slice(part * count, (part + 1) * count)
+    for i in range(FETCH_PARTS):
+        mine = slice(i * step, (i + 1) * step)
+        block = pl.ds(i * step, step)
+        wide = slice(i * count, (i + 1) * count)
         whole = dot(one_hot(hist[wide], rows), table[...])
-        sent[mine, :, :width] = whole.reshape(step, SLOTS, width).astype(BF16)
-        first = TABLE_PARTS + 2 * part
+        sent[mine, :, :width] = whole.astype(BF16).reshape(step, SLOTS, width)
         side = pl.ds(0, width)
         copies += started(
-            ((sent.at[block, :, side], out.at[block, :, side]),), sems.at[pl.ds(first, 1)]
+            ((sent.at[block, :, side], out.at[block, :, side]),), sems.at[pl.ds(2 * i, 1)]
         )
-        ends = [
-            dot(one_hot(numbers[mine, SLOTS + s : SLOTS + s + 1], rows), table[:, cut:])
-            for s in range(SLOTS - 1)
-        ]
-        ends = jnp.concatenate(ends, axis=1).astype(BF16)
-        begin = dot(one_hot(jnp.where(last, -1, cand[wide]), rows), table[:, :cut])
-        both = begin + dot(place, ends)
-        sent[mine, :, width:] = both.reshape(step, SLOTS, cut).astype(BF16)
+        whole = dot(one_hot(cand[wide], rows), table[...])
+        ends = whole[:, cut:]
+        ends = [moved_down(ends, SLOTS - 1 - s) for s in range(SLOTS - 1)]
+        both = jnp.where(last, jnp.concatenate(ends, axis=1), whole[:, :cut])
+        sent[mine, :, width:] = both.astype(BF16).reshape(step, SLOTS, cut)
         side = pl.ds(width, cut)
         copies += started(
-            ((sent.at[block, :, side], out.at[block, :, side]),), sems.at[pl.ds(first + 1, 1)]
+            ((sent.at[block, :, side], out.at[block, :, side]),), sems.at[pl.ds(2 * i + 1, 1)]
         )
     for copy in copies:
         copy.wait()
@@ -188,13 +171,9 @@
     return pl.pallas_call(
         fetch_kernel,
         out_shape=jax.ShapeDtypeStruct(shape, BF16),
-        in_specs=[VMEM, HBM],
+        in_specs=[VMEM, VMEM],
         out_specs=HBM,
-        scratch_shapes=[
-            pltpu.VMEM(table.shape, BF16),
-            pltpu.VMEM(shape, BF16),
-            DMA((TABLE_PARTS + 2 * FETCH_PARTS,)),
-        ],
+        scratch_shapes=[pltpu.VMEM(shape, BF16), DMA((2 * FETCH_PARTS,))],
         compiler_params=pltpu.CompilerParams(vmem_limit_bytes=VMEM_BYTES),
         cost_estimate=pl.CostEstimate(
             flops=3 * 10**9, bytes_accessed=3 * 10**6, transcendentals=0
@@ -203,30 +182,25 @@
     )(numbers, table)
 
 
-def picked_hist(replies, column, warm):
+def picked_hist(replies, column, width):
     owners = replies.shape[0]
-    width = warm.shape[1]
     count = owners * SLOTS
     dense = replies[:, :, :width].astype(F32).reshape(count, width).astype(BF16)
-    return dot(one_hot(column.astype(I32), count), dense) + warm[...].astype(F32)
-
-
-def picked_cand(replies, column, warm):
+    return dot(one_hot(column.astype(I32), count), dense)
+
+
+def picked_cand(replies, column, width):
     owners = replies.shape[0]
-    width = warm.shape[1]
     count = owners * SLOTS
     part = width // 4
-    cut = width - part
-    dense = replies[:, :, width:].astype(F32).reshape(count, cut).astype(BF16)
-    at = column.astype(I32)
-    slot = at & (SLOTS - 1)
-    hot = warm[...].astype(F32)
-    begin = dot(one_hot(at, count), dense) + hot[:, :cut]
-    ends = dot(one_hot(at | (SLOTS - 1), count), dense)
-    end = jnp.where(slot == 0, ends[:, :part], ends[:, 2 * part :])
-    end = jnp.where(slot == 1, ends[:, part : 2 * part], end)
-    end = jnp.where(at < count, end, hot[:, cut:])
-    return jnp.concatenate([begin, end], axis=1)
+    dense = replies[:, :, width:].astype(F32).reshape(count, width - part)
+    place = iota((count, 1), 0) & (SLOTS - 1)
+    end = moved_down(dense[:, :part], 8 - (SLOTS - 1))
+    for s in range(1, SLOTS - 1):
+        other = moved_down(dense[:, s * part : (s + 1) * part], 8 - (SLOTS - 1 - s))
+        end = jnp.where(place == s, other, end)
+    dense = jnp.concatenate([dense, end], axis=1).astype(BF16)
+    return dot(one_hot(column.astype(I32), count), dense)
 
 
 def warm_kernel(picks, hot, out, rows, sems, *, count):
@@ -256,7 +230,7 @@
 
 
 def keys_kernel(
-    picks, gain, replies, warm_in, w_in, rows_out, kv, rows, ins, warm, w_v, w_k, sems
+    picks, gain, replies, warm_in, w_in, rows_out, kv, warm, rows, ins, w_v, w_k, sems
 ):
     n, width = warm.shape[0] // 2, warm.shape[1]
     hist, cand = pl.ds(0, n), pl.ds(n, n)
@@ -270,8 +244,9 @@
         sems,
     )
     column = to_column(picks[1:2, :])
+    y = picked_cand(replies, column, width)
     in_cand.wait()
-    y = picked_cand(replies, column, warm.at[cand])
+    y = y + warm[cand, :].astype(F32)
     rows[cand, :] = y.astype(BF16)
     ins[cand, :] = norm(y, gain[...]).astype(BF16)
     done = started(
@@ -282,8 +257,9 @@
         sems.at[pl.ds(4, 2)],
     )
     column = to_column(picks[0:1, :])
+    x = picked_hist(replies, column, width)
     in_hist.wait()
-    x = picked_hist(replies, column, warm.at[hist])
+    x = x + warm[hist, :].astype(F32)
     rows[hist, :] = x.astype(BF16)
     inner = norm(x, gain[...]).astype(BF16)
     ins[hist, :] = inner
@@ -329,47 +305,35 @@
     )(picks, gain, replies, warm, w_in)
 
 
-def queries_kernel(rows_in, w_in, u_out, qs, us, ins, w_u, w_q, sems):
+def queries_kernel(rows_in, w_in, qs, ins, w_q, sems):
     n, width = ins.shape[0] // 2, ins.shape[1]
     hist, cand = pl.ds(0, n), pl.ds(n, n)
-    in_hist, in_u, in_cand, in_q = started(
+    in_hist, in_q, in_cand = started(
         (
             (rows_in.at[pl.ds(2 * n, n)], ins.at[hist]),
-            (w_in.at[:, pl.ds(0, width)], w_u),
+            (w_in.at[:, pl.ds(2 * width, width)], w_q),
             (rows_in.at[pl.ds(3 * n, n)], ins.at[cand]),
-            (w_in.at[:, pl.ds(2 * width, width)], w_q),
         ),
         sems,
     )
     in_hist.wait()
-    in_u.wait()
-    us[hist, :] = silu(dot(ins[hist, :], w_u[...]))
-    done = started(((us.at[hist], u_out.at[hist]),), sems.at[pl.ds(4, 1)])
+    in_q.wait()
+    qs[hist, :] = silu(dot(ins[hist, :], w_q[...])).astype(BF16)
     in_cand.wait()
-    us[cand, :] = silu(dot(ins[cand, :], w_u[...]))
-    done += started(((us.at[cand], u_out.at[cand]),), sems.at[pl.ds(5, 1)])
-    in_q.wait()
-    qs[...] = silu(dot(ins[...], w_q[...])).astype(BF16)
-    for copy in done:
-        copy.wait()
+    qs[cand, :] = silu(dot(ins[cand, :], w_q[...])).astype(BF16)
 
 
 def queries(rows, w_in):
     n, width = rows.shape[0] // SPARE, rows.shape[1]
     return pl.pallas_call(
         queries_kernel,
-        out_shape=(
-            jax.ShapeDtypeStruct((SPARE * n, width), F32),
-            jax.ShapeDtypeStruct((2 * n, width), BF16),
-        ),
+        out_shape=jax.ShapeDtypeStruct((2 * n, width), BF16),
         in_specs=[HBM, HBM],
-        out_specs=(HBM, VMEM),
+        out_specs=VMEM,
         scratch_shapes=[
-            pltpu.VMEM((2 * n, width), F32),
             pltpu.VMEM((2 * n, width), BF16),
             pltpu.VMEM((width, width), BF16),
-            pltpu.VMEM((width, width), BF16),
-            DMA((6,)),
+            DMA((3,)),
         ],
         compiler_params=pltpu.CompilerParams(vmem_limit_bytes=QUERY_BYTES),
         cost_estimate=pl.CostEstimate(
@@ -385,15 +349,21 @@
 
 
 def layer_kernel(
-    user, gain, qs, own, other, rows_in, us_in, w_last, hist_out, cand_out,
-    xs, us, w_out, mix, outs, sems,
+    user, gain, qs, own, other, rows_in, w_in, w_last, hist_out, cand_out,
+    xs, ins, w_u, w_out, us, mix, outs, sems,
 ):
     n, width = own.shape[0], own.shape[1] // 2
     head_dim = width // HEADS
     hist, cand = pl.ds(0, n), pl.ds(n, n)
     both = pl.ds(0, 2 * n)
     arrivals = started(
-        ((w_last, w_out), (us_in.at[both], us), (rows_in.at[both], xs)), sems
+        (
+            (rows_in.at[pl.ds(2 * n, 2 * n)], ins),
+            (w_in.at[:, pl.ds(0, width)], w_u),
+            (w_last, w_out),
+            (rows_in.at[both], xs),
+        ),
+        sems,
     )
     causal = iota((n, n), 1) <= iota((n, n), 0)
 
@@ -422,16 +392,17 @@
 
     for arrival in arrivals:
         arrival.wait()
+    us[...] = silu(dot(ins[...], w_u[...]))
     done = []
     for i, (rows, out) in enumerate(((hist, hist_out), (cand, cand_out))):
         gated = (norm(mix[rows, :], gain[...]) * us[rows, :]).astype(BF16)
         outs[rows, :] = (xs[rows, :].astype(F32) + dot(gated, w_out[...])).astype(BF16)
-        done += started(((outs.at[rows], out),), sems.at[pl.ds(3 + i, 1)])
+        done += started(((outs.at[rows], out),), sems.at[pl.ds(4 + i, 1)])
     for copy in done:
         copy.wait()
 
 
-def layer(user, rows, us, qs, own, other, gain, w_out):
+def layer(user, rows, qs, own, other, gain, w_in, w_out):
     n, width = own.shape[0], own.shape[1] // 2
     shape = jax.ShapeDtypeStruct((n, width), BF16)
     return pl.pallas_call(
@@ -441,18 +412,20 @@
         out_specs=(HBM, HBM),
         scratch_shapes=[
             pltpu.VMEM((2 * n, width), BF16),
-            pltpu.VMEM((2 * n, width), F32),
+            pltpu.VMEM((2 * n, width), BF16),
+            pltpu.VMEM((width, width), BF16),
             pltpu.VMEM((width, width), BF16),
             pltpu.VMEM((2 * n, width), F32),
-            pltpu.VMEM((2 * n, width), BF16),
-            DMA((5,)),
+            pltpu.VMEM((2 * n, width), F32),
+            pltpu.VMEM((2 * n, width), BF16),
+            DMA((6,)),
         ],
         compiler_params=pltpu.CompilerParams(vmem_limit_bytes=LAYER_BYTES),
         cost_estimate=pl.CostEstimate(
             flops=6 * 10**9, bytes_accessed=9 * 10**6, transcendentals=6 * 10**6
         ),
         name="layer",
-    )(user, gain, qs, own, other, rows, us, w_out)
+    )(user, gain, qs, own, other, rows, w_in, w_out)
 
 
 def exchange(array):
@@ -468,9 +441,9 @@
     warm = warm_rows(picks, hot_table, owners * SLOTS)
     rows, own = keys(replies, warm, picks, w_in[0], in_gain)
     other = lax.ppermute(own, "user", [(0, 1), (1, 0)])
-    us, qs = queries(rows, w_in[0])
+    qs = queries(rows, w_in[0])
     user = lax.axis_index("user")[None].astype(I32)
-    hist_out, cand_out = layer(user, rows, us, qs, own, other, attn_gain, w_out[0])
+    hist_out, cand_out = layer(user, rows, qs, own, other, attn_gain, w_in[0], w_out[0])
     return hist_out[None], cand_out[None]
 
 

time: 119 us -> 116 us (0.975)
  Pallas kernels: 25.8 us -> 21 us
    pallas_call x1, Pallas kernels: 5.41 us -> 3.51 us  [fetch(): pl.pallas_call(fetch_kernel, out_shape=jax.ShapeDtypeStruct(shape, BF16),...]
    pallas_call x1, Pallas kernels: 2.63 us -> 1.26 us  [ask(): pl.pallas_call(lambda *refs: ask_kernel(*refs, owners=owners, shift=shift...]
  transfers between devices with their start and end apart: 2 -> 2, of which waited for: 1 -> 1; matrix products, arithmetic and copies ran while one was open for 0% -> 0% of each run, Pallas kernels for 5% -> 3%
where the time goes in v6:
time: 116 us; the launch traced here: 115 us
  waiting for transfers between devices  41.4 us (36%)
  blocking collectives  35 us (30%)
  Pallas kernels  21 us (18%)
  starting transfers between devices  16.2 us (14%)
    all_to_all x1, waiting for transfers between devices, exchange(): return lax.all_to_all(array, ('req', 'cand'), 0, 0, tiled=True)  41.4 us
    all_to_all x1, blocking collectives, exchange(): return lax.all_to_all(array, ('req', 'cand'), 0, 0, tiled=True)  35 us
    all_to_all x1, starting transfers between devices, exchange(): return lax.all_to_all(array, ('req', 'cand'), 0, 0, tiled=True)  9.51 us
    pallas_call x1, Pallas kernels, layer(): pl.pallas_call(layer_kernel, out_shape=(shape, shape), in_specs=[SMEM] +...  8.02 us
    ppermute x1, starting transfers between devices, per_device(): other = lax.ppermute(own, 'user', [(0, 1), (1, 0)])  6.73 us
    pallas_call x1, Pallas kernels, keys(): pl.pallas_call(keys_kernel, out_shape=(jax.ShapeDtypeStruct((SPARE * n, w...  4.53 us
    pallas_call x1, Pallas kernels, fetch(): pl.pallas_call(fetch_kernel, out_shape=jax.ShapeDtypeStruct(shape, BF16),...  3.51 us
  transfers between devices with their start and end apart: 2, of which 1 were waited for; matrix products, arithmetic and copies ran while one was open for 0% of the time, Pallas kernels for 3%

profile of v6, /device:TPU:1, one launch (start us, length us, event | category | flops | bytes accessed | tf_op | source)
XLA Modules:
  0.0 115.4 jit_solution(12956955520352243242)
XLA Ops:
  0.6 0.0 copy-start.2
  0.6 0.8 pad_add_fusion.refs_0_
  1.4 1.3 %ask.1 = (s32[256,8]{1,0:T(8,128)S(1)}, f32[2,512]{1,0:T(2,128)S(1)}) custom-call(s32[1,1280]{1,0:T(1,128)S(1)} %pad_add_fusion.refs_0_), custom_call_target="tpu_custom_call" | custom-call | flops 1000000000 | bytes 100000 | tf_op jit(solution)/shard_map/ask/pallas_call | solution.py:97
  2.7 35.0 %all_to_all.10 = s32[256,1,8]{2,1,0:T(1,128)S(1)} all-to-all(s32[256,1,8]{2,1,0:T(1,128)S(1)} %bitcast.10), channel_id=1, replica_groups=mesh['req'=8,'cand'=32,'user'=2] {'req','cand'}, dimensions={0} | all-to-all | bytes 16384 | tf_op jit(solution)/shard_map/all_to_all | solution.py:432
  37.7 0.0 copy-done.2
  37.7 3.5 %fetch.1 = bf16[256,4,896]{2,1,0:T(4,128)(2,1)} custom-call(s32[256,8]{1,0:T(8,128)S(1)} %bitcast.11, bf16[1024,512]{1,0:T(8,128)(2,1)S(1)} %copy-done.2), custom_call_target="tpu_custom_call" | custom-call | flops 3000000000 | bytes 3000000 | tf_op jit(solution)/shard_map/fetch/pallas_call | solution.py:171
  41.2 0.0 copy-start
  41.2 9.5 %all-to-all-start.1 = ((bf16[256,4,896]{2,1,0:T(4,128)(2,1)}), bf16[256,4,896]{2,1,0:T(4,128)(2,1)S(1)}, u32[]{:S(2)}, u32[]{:S(2)}) async-start(bf16[256,4,896]{2,1,0:T(4,128)(2,1)} %fetch.1), calls=%async_computation.1 | async-start | bytes 3670016 | tf_op jit(solution)/shard_map/all_to_all | solution.py:432
  50.7 0.0 copy-done
  50.7 0.0 copy-start.1
  50.7 1.5 %warm.1.warm_in = bf16[8192,512]{1,0:T(8,128)(2,1)} custom-call(f32[2,512]{1,0:T(2,128)S(1)} %get-tuple-element.8.refs_0_.picks, bf16[256,512]{1,0:T(8,128)(2,1)S(1)} %copy-done), custom_call_target="tpu_custom_call" | custom-call | flops 1000000000 | bytes 2000000 | tf_op jit(solution)/shard_map/warm/pallas_call | solution.py:218
  52.2 41.4 %all-to-all-done.1.replies = bf16[256,4,896]{2,1,0:T(4,128)(2,1)S(1)} async-done(((bf16[256,4,896]{2,1,0:T(4,128)(2,1)}), bf16[256,4,896]{2,1,0:T(4,128)(2,1)S(1)}, u32[]{:S(2)}, u32[]{:S(2)}) %all-to-all-start.1) | async-done | bytes 1835040 | tf_op jit(solution)/shard_map/all_to_all | solution.py:432
  93.6 0.0 copy-done.1
  93.6 4.5 %keys.1 = (bf16[8192,512]{1,0:T(8,128)(2,1)}, bf16[512,1024]{1,0:T(8,128)(2,1)S(1)}) custom-call(f32[2,512]{1,0:T(2,128)S(1)} %get-tuple-element.8.refs_0_.picks, f32[1,512]{1,0:T(1,128)S(1)} %copy-done.1, bf16[256,4,896]{2,1,0:T(4,128)(2,1)S(1)} %all-to-all-done.1.replies, bf16[8192,512]{1,0:T(8,128)(2,1)} %warm.1.warm_in, bf16[512,2048]{1,0:T(8,128)(2,1)} %bitcast.13), custom_call_target="tpu_custom_call" | custom-call | flops 3000000000 | bytes 6000000 | tf_op jit(solution)/shard_map/keys/pallas_call | solution.py:284
  98.2 6.7 %collective-permute-start = (bf16[512,1024]{1,0:T(8,128)(2,1)S(1)}, bf16[512,1024]{1,0:T(8,128)(2,1)S(1)}, u32[]{:S(2)}, u32[]{:S(2)}) collective-permute-start(bf16[512,1024]{1,0:T(8,128)(2,1)S(1)} %get-tuple-element.11.own), channel_id=1, source_target_pairs={{0,1},{1,0},{2,3},{3,2},{4,5},{5,4},{6,7},{7,6},{8,9},{9,8},{10,11... | collective-permute-start | bytes 3145736 | tf_op jit(solution)/shard_map/ppermute | solution.py:443
  104.9 0.0 copy-start.3
  104.9 0.0 copy-start.4
  104.9 2.2 %queries.1.qs = bf16[1024,512]{1,0:T(8,128)(2,1)S(1)} custom-call(bf16[8192,512]{1,0:T(8,128)(2,1)} %get-tuple-element.10.rows_in, bf16[512,2048]{1,0:T(8,128)(2,1)} %bitcast.14), custom_call_target="tpu_custom_call" | custom-call | flops 2000000000 | bytes 4000000 | tf_op jit(solution)/shard_map/queries/pallas_call | solution.py:328
  107.2 0.0 collective-permute-done.other
  107.2 0.0 copy-done.3
  107.2 0.0 copy-done.4
  107.2 8.0 %layer.1 = (bf16[512,512]{1,0:T(8,128)(2,1)}, bf16[512,512]{1,0:T(8,128)(2,1)}) custom-call(s32[1]{0:T(128)} %bitcast.user, f32[1,512]{1,0:T(1,128)S(1)} %copy-done.4, bf16[1024,512]{1,0:T(8,128)(2,1)S(1)} %queries.1.qs, bf16[512,1024]{1,0:T(8,128)(2,1)S(1)} %get-tuple-element.11.own, bf16[512,1024]{1,0:T(8,128)(2,1)S(1)} %collective-permute-done.other, ...), custom_call_target="tpu_custom_call" | custom-call | flops 6000000000 | bytes 9000000 | tf_op jit(solution)/shard_map/layer/pallas_call | solution.py:408
Async XLA Ops:
  0.6 37.0 %copy-start.2 = (bf16[1024,512]{1,0:T(8,128)(2,1)S(1)}, bf16[1024,512]{1,0:T(8,128)(2,1)}, u32[]{:S(2)}) copy-start(bf16[1024,512]{1,0:T(8,128)(2,1)} %table.1) | copy-start | bytes 3145732
  41.2 9.5 %copy-start = (bf16[256,512]{1,0:T(8,128)(2,1)S(1)}, bf16[256,512]{1,0:T(8,128)(2,1)}, u32[]{:S(2)}) copy-start(bf16[256,512]{1,0:T(8,128)(2,1)} %refs_1_.1) | copy-start | bytes 786436
  41.2 52.4 %all-to-all-start.1 = ((bf16[256,4,896]{2,1,0:T(4,128)(2,1)}), bf16[256,4,896]{2,1,0:T(4,128)(2,1)S(1)}, u32[]{:S(2)}, u32[]{:S(2)}) async-start(bf16[256,4,896]{2,1,0:T(4,128)(2,1)} %fetch.1), calls=%async_computation.1 | async-start | bytes 3670016 | tf_op jit(solution)/shard_map/all_to_all | solution.py:432
  50.7 42.9 %copy-start.1 = (f32[1,512]{1,0:T(1,128)S(1)}, f32[1,512]{1,0:T(1,128)}, u32[]{:S(2)}) copy-start(f32[1,512]{1,0:T(1,128)} %gain.2) | copy-start | bytes 6148
  98.2 9.0 %collective-permute-start = (bf16[512,1024]{1,0:T(8,128)(2,1)S(1)}, bf16[512,1024]{1,0:T(8,128)(2,1)S(1)}, u32[]{:S(2)}, u32[]{:S(2)}) collective-permute-start(bf16[512,1024]{1,0:T(8,128)(2,1)S(1)} %get-tuple-element.11.own), channel_id=1, source_target_pairs={{0,1},{1,0},{2,3},{3,2},{4,5},{5,4},{6,7},{7,6},{8,9},{9,8},{10,11... | collective-permute-start | bytes 3145736 | tf_op jit(solution)/shard_map/ppermute | solution.py:443
  104.9 2.3 %copy-start.3 = (bf16[1,512,512]{2,1,0:T(8,128)(2,1)S(1)}, bf16[1,512,512]{2,1,0:T(8,128)(2,1)}, u32[]{:S(2)}) copy-start(bf16[1,512,512]{2,1,0:T(8,128)(2,1)} %param.15) | copy-start | bytes 1572868
  104.9 2.3 %copy-start.4 = (f32[1,512]{1,0:T(1,128)S(1)}, f32[1,512]{1,0:T(1,128)}, u32[]{:S(2)}) copy-start(f32[1,512]{1,0:T(1,128)} %gain.3) | copy-start | bytes 6148

commit v7 on v6

--- a/solution.py
+++ b/solution.py
@@ -10,17 +10,17 @@
 LANES = 8
 FETCH_PARTS = 2
 SPARE = 16
+FINISH_PARTS = 2
 F32 = jnp.float32
 BF16 = jnp.bfloat16
 I32 = jnp.int32
 ASK_BYTES = 53248 * 1024
 VMEM_BYTES = 53248 * 1024
-WARM_BYTES = 54528 * 1024
 QUERY_BYTES = 52224 * 1024
 HBM = pl.BlockSpec(memory_space=pltpu.HBM)
 VMEM = pl.BlockSpec(memory_space=pltpu.VMEM)
 SMEM = pl.BlockSpec(memory_space=pltpu.SMEM)
-KEYS_BYTES = 52224 * 1024
+KEYS_BYTES = 51712 * 1024
 LAYER_BYTES = 51200 * 1024
 DMA = pltpu.SemaphoreType.DMA
 
@@ -182,15 +182,24 @@
     )(numbers, table)
 
 
-def picked_hist(replies, column, width):
+def picked(dense, column, hot):
+    at = column.astype(I32)
+    count = dense.shape[0]
+    cold = dot(one_hot(at, count), dense)
+    return cold + dot(one_hot(at - count, hot.shape[0]), hot[...])
+
+
+def picked_hist(replies, column, hot):
     owners = replies.shape[0]
+    width = hot.shape[1]
     count = owners * SLOTS
     dense = replies[:, :, :width].astype(F32).reshape(count, width).astype(BF16)
-    return dot(one_hot(column.astype(I32), count), dense)
-
-
-def picked_cand(replies, column, width):
+    return picked(dense, column, hot)
+
+
+def picked_cand(replies, column, hot):
     owners = replies.shape[0]
+    width = hot.shape[1]
     count = owners * SLOTS
     part = width // 4
     dense = replies[:, :, width:].astype(F32).reshape(count, width - part)
@@ -200,53 +209,23 @@
         other = moved_down(dense[:, s * part : (s + 1) * part], 8 - (SLOTS - 1 - s))
         end = jnp.where(place == s, other, end)
     dense = jnp.concatenate([dense, end], axis=1).astype(BF16)
-    return dot(one_hot(column.astype(I32), count), dense)
-
-
-def warm_kernel(picks, hot, out, rows, sems, *, count):
-    n = picks.shape[1]
-    for side in range(2):
-        at = to_column(picks[side : side + 1, :]).astype(I32) - count
-        rows[side * n : (side + 1) * n, :] = dot(one_hot(at, hot.shape[0]), hot[...]).astype(BF16)
-    (copy,) = started(((rows, out.at[pl.ds(0, 2 * n)]),), sems)
-    copy.wait()
-
-
-def warm_rows(picks, hot, count):
-    n = picks.shape[1]
-    width = hot.shape[1]
-    return pl.pallas_call(
-        lambda *refs: warm_kernel(*refs, count=count),
-        out_shape=jax.ShapeDtypeStruct((SPARE * n, width), BF16),
-        in_specs=[VMEM, VMEM],
-        out_specs=HBM,
-        scratch_shapes=[pltpu.VMEM((2 * n, width), BF16), DMA((1,))],
-        compiler_params=pltpu.CompilerParams(vmem_limit_bytes=WARM_BYTES),
-        cost_estimate=pl.CostEstimate(
-            flops=10**9, bytes_accessed=2 * 10**6, transcendentals=0
-        ),
-        name="warm",
-    )(picks, hot)
+    return picked(dense, column, hot)
 
 
 def keys_kernel(
-    picks, gain, replies, warm_in, w_in, rows_out, kv, warm, rows, ins, w_v, w_k, sems
+    picks, gain, hot, replies, w_in, rows_out, kv, rows, ins, w_v, w_k, sems
 ):
-    n, width = warm.shape[0] // 2, warm.shape[1]
+    n, width = rows.shape[0] // 2, rows.shape[1]
     hist, cand = pl.ds(0, n), pl.ds(n, n)
-    in_cand, in_hist, in_v, in_k = started(
+    in_v, in_k = started(
         (
-            (warm_in.at[cand], warm.at[cand]),
-            (warm_in.at[hist], warm.at[hist]),
             (w_in.at[:, pl.ds(width, width)], w_v),
             (w_in.at[:, pl.ds(3 * width, width)], w_k),
         ),
         sems,
     )
     column = to_column(picks[1:2, :])
-    y = picked_cand(replies, column, width)
-    in_cand.wait()
-    y = y + warm[cand, :].astype(F32)
+    y = picked_cand(replies, column, hot)
     rows[cand, :] = y.astype(BF16)
     ins[cand, :] = norm(y, gain[...]).astype(BF16)
     done = started(
@@ -257,9 +236,7 @@
         sems.at[pl.ds(4, 2)],
     )
     column = to_column(picks[0:1, :])
-    x = picked_hist(replies, column, width)
-    in_hist.wait()
-    x = x + warm[hist, :].astype(F32)
+    x = picked_hist(replies, column, hot)
     rows[hist, :] = x.astype(BF16)
     inner = norm(x, gain[...]).astype(BF16)
     ins[hist, :] = inner
@@ -278,19 +255,18 @@
         copy.wait()
 
 
-def keys(replies, warm, picks, w_in, gain):
+def keys(replies, hot, picks, w_in, gain):
     n = picks.shape[1]
-    width = warm.shape[1]
+    width = hot.shape[1]
     return pl.pallas_call(
         keys_kernel,
         out_shape=(
             jax.ShapeDtypeStruct((SPARE * n, width), BF16),
             jax.ShapeDtypeStruct((n, 2 * width), BF16),
         ),
-        in_specs=[VMEM] * 3 + [HBM] * 2,
+        in_specs=[VMEM] * 4 + [HBM],
         out_specs=(HBM, VMEM),
         scratch_shapes=[
-            pltpu.VMEM((2 * n, width), BF16),
             pltpu.VMEM((2 * n, width), BF16),
             pltpu.VMEM((2 * n, width), BF16),
             pltpu.VMEM((width, width), BF16),
@@ -302,7 +278,7 @@
             flops=3 * 10**9, bytes_accessed=6 * 10**6, transcendentals=10**6
         ),
         name="keys",
-    )(picks, gain, replies, warm, w_in)
+    )(picks, gain, hot, replies, w_in)
 
 
 def queries_kernel(rows_in, w_in, qs, ins, w_q, sems):
@@ -365,22 +341,32 @@
         ),
         sems,
     )
-    causal = iota((n, n), 1) <= iota((n, n), 0)
+    half = n // 2
+    causal = iota((half, half), 1) <= iota((half, half), 0)
+
+    def masked(w):
+        w = jnp.concatenate([jnp.where(causal, w[:half], 0.0), w[half:]], axis=0)
+        return w.astype(BF16)
 
     def heads(everyone):
         for h in range(HEADS):
             at = slice(h * head_dim, (h + 1) * head_dim)
             past = slice(width + h * head_dim, width + (h + 1) * head_dim)
-            near = weights(qs[:, at], own[:, at], head_dim)
-            near = jnp.concatenate([jnp.where(causal, near[:n], 0.0), near[n:]], axis=0)
-            total = dot(near.astype(BF16), own[:, past])
+            first = masked(weights(qs[:, at], own[:half, at], head_dim))
+            first = dot(first, own[:half, past])
+            second = masked(weights(qs[half:, at], own[half:, at], head_dim))
+            second = dot(second, own[half:, past])
             if everyone:
-                far = weights(qs[:, at], other[:, at], head_dim)
-                mix[:, at] = total + dot(far.astype(BF16), other[:, past])
+                far = weights(qs[:, at], other[:, at], head_dim).astype(BF16)
+                far = dot(far, other[:, past])
+                mix[:half, at] = first[:half] + far[:half]
+                mix[half:, at] = first[half:] + second + far[half:]
             else:
-                far = weights(qs[n:, at], other[:, at], head_dim)
-                mix[:n, at] = total[:n]
-                mix[n:, at] = total[n:] + dot(far.astype(BF16), other[:, past])
+                far = weights(qs[n:, at], other[:, at], head_dim).astype(BF16)
+                far = dot(far, other[:, past])
+                mix[:half, at] = first[:half]
+                mix[half:n, at] = first[half:n] + second[: n - half]
+                mix[n:, at] = first[n:] + second[n - half :] + far
 
     @pl.when(user[0] == 1)
     def _():
@@ -394,10 +380,14 @@
         arrival.wait()
     us[...] = silu(dot(ins[...], w_u[...]))
     done = []
-    for i, (rows, out) in enumerate(((hist, hist_out), (cand, cand_out))):
+    step = n // FINISH_PARTS
+    for i in range(2 * FINISH_PARTS):
+        rows = pl.ds(i * step, step)
+        out = hist_out if i < FINISH_PARTS else cand_out
         gated = (norm(mix[rows, :], gain[...]) * us[rows, :]).astype(BF16)
         outs[rows, :] = (xs[rows, :].astype(F32) + dot(gated, w_out[...])).astype(BF16)
-        done += started(((outs.at[rows], out),), sems.at[pl.ds(4 + i, 1)])
+        place = pl.ds(i % FINISH_PARTS * step, step)
+        done += started(((outs.at[rows], out.at[place]),), sems.at[pl.ds(4 + i, 1)])
     for copy in done:
         copy.wait()
 
@@ -418,7 +408,7 @@
             pltpu.VMEM((2 * n, width), F32),
             pltpu.VMEM((2 * n, width), F32),
             pltpu.VMEM((2 * n, width), BF16),
-            DMA((6,)),
+            DMA((4 + 2 * FINISH_PARTS,)),
         ],
         compiler_params=pltpu.CompilerParams(vmem_limit_bytes=LAYER_BYTES),
         cost_estimate=pl.CostEstimate(
@@ -438,8 +428,7 @@
     asked, picks = ask(hist_ids, cand_ids, hot_ids[None], owners, shift)
     numbers = exchange(asked[:, None, :])[:, 0, :]
     replies = exchange(fetch(numbers, table))
-    warm = warm_rows(picks, hot_table, owners * SLOTS)
-    rows, own = keys(replies, warm, picks, w_in[0], in_gain)
+    rows, own = keys(replies, hot_table, picks, w_in[0], in_gain)
     other = lax.ppermute(own, "user", [(0, 1), (1, 0)])
     qs = queries(rows, w_in[0])
     user = lax.axis_index("user")[None].astype(I32)

time: 116 us -> 114 us (0.983)
  blocking collectives: 35 us -> 87.9 us
  waiting for transfers between devices: 41.4 us -> 0.01 us
  starting transfers between devices: 16.2 us -> 6.72 us
  Pallas kernels: 21 us -> 17.8 us
    all_to_all x1 -> x2, blocking collectives: 35 us -> 87.9 us  [exchange(): return lax.all_to_all(array, ('req', 'cand'), 0, 0, tiled=True)]
    all_to_all x1 -> x0, waiting for transfers between devices: 41.4 us -> none  [exchange(): return lax.all_to_all(array, ('req', 'cand'), 0, 0, tiled=True)]
    all_to_all x1 -> x0, starting transfers between devices: 9.51 us -> none  [exchange(): return lax.all_to_all(array, ('req', 'cand'), 0, 0, tiled=True)]
    pallas_call x1 -> x0, Pallas kernels: 1.48 us -> none  [warm_rows(): pl.pallas_call(lambda *refs: warm_kernel(*refs, count=count), out_shape=j...]
    pallas_call x1, Pallas kernels: 4.53 us -> 3.11 us  [keys(): pl.pallas_call(keys_kernel, out_shape=(jax.ShapeDtypeStruct((SPARE * n, w...]
  transfers between devices with their start and end apart: 2 -> 1, of which waited for: 1 -> 0; matrix products, arithmetic and copies ran while one was open for 0% -> 0% of each run, Pallas kernels for 3% -> 2%
where the time goes in v7:
time: 114 us
  blocking collectives  87.9 us (77%)
  Pallas kernels  17.8 us (16%)
  starting transfers between devices  6.72 us (6%)
    all_to_all x2, blocking collectives, exchange(): return lax.all_to_all(array, ('req', 'cand'), 0, 0, tiled=True)  87.9 us
    pallas_call x1, Pallas kernels, layer(): pl.pallas_call(layer_kernel, out_shape=(shape, shape), in_specs=[SMEM] +...  7.7 us
    ppermute x1, starting transfers between devices, per_device(): other = lax.ppermute(own, 'user', [(0, 1), (1, 0)])  6.72 us
    pallas_call x1, Pallas kernels, fetch(): pl.pallas_call(fetch_kernel, out_shape=jax.ShapeDtypeStruct(shape, BF16),...  3.45 us
    pallas_call x1, Pallas kernels, keys(): pl.pallas_call(keys_kernel, out_shape=(jax.ShapeDtypeStruct((SPARE * n, w...  3.11 us
  transfers between devices with their start and end apart: 1, of which 0 were waited for; matrix products, arithmetic and copies ran while one was open for 0% of the time, Pallas kernels for 2%

profile of v7, /device:TPU:1, one launch (start us, length us, event | category | flops | bytes accessed | tf_op | source)
XLA Modules:
  0.0 114.2 jit_solution(6549364575145672090)
XLA Ops:
  0.6 0.0 copy-start
  0.6 0.8 pad_add_fusion.refs_0_
  1.4 1.3 %ask.1 = (s32[256,8]{1,0:T(8,128)S(1)}, f32[2,512]{1,0:T(2,128)S(1)}) custom-call(s32[1,1280]{1,0:T(1,128)S(1)} %pad_add_fusion.refs_0_), custom_call_target="tpu_custom_call" | custom-call | flops 1000000000 | bytes 100000 | tf_op jit(solution)/shard_map/ask/pallas_call | solution.py:97
  2.7 34.9 %all_to_all.10 = s32[256,1,8]{2,1,0:T(1,128)S(1)} all-to-all(s32[256,1,8]{2,1,0:T(1,128)S(1)} %bitcast.10), channel_id=1, replica_groups=mesh['req'=8,'cand'=32,'user'=2] {'req','cand'}, dimensions={0} | all-to-all | bytes 16384 | tf_op jit(solution)/shard_map/all_to_all | solution.py:422
  37.7 0.0 copy-done
  37.7 3.5 %fetch.1 = bf16[256,4,896]{2,1,0:T(4,128)(2,1)} custom-call(s32[256,8]{1,0:T(8,128)S(1)} %bitcast.11, bf16[1024,512]{1,0:T(8,128)(2,1)S(1)} %copy-done), custom_call_target="tpu_custom_call" | custom-call | flops 3000000000 | bytes 3000000 | tf_op jit(solution)/shard_map/fetch/pallas_call | solution.py:171
  41.1 0.0 copy-start.2
  41.1 0.0 copy-start.3
  41.1 53.0 %all_to_all.11.replies = bf16[256,4,896]{2,1,0:T(4,128)(2,1)S(1)} all-to-all(bf16[256,4,896]{2,1,0:T(4,128)(2,1)} %fetch.1), channel_id=1, replica_groups=mesh['req'=8,'cand'=32,'user'=2] {'req','cand'}, dimensions={0} | all-to-all | bytes 3670016 | tf_op jit(solution)/shard_map/all_to_all | solution.py:422
  94.1 0.0 copy-done.2
  94.1 0.0 copy-done.3
  94.1 3.1 %keys.1 = (bf16[8192,512]{1,0:T(8,128)(2,1)}, bf16[512,1024]{1,0:T(8,128)(2,1)S(1)}) custom-call(f32[2,512]{1,0:T(2,128)S(1)} %get-tuple-element.8.picks, f32[1,512]{1,0:T(1,128)S(1)} %copy-done.3, bf16[256,512]{1,0:T(8,128)(2,1)S(1)} %copy-done.2, bf16[256,4,896]{2,1,0:T(4,128)(2,1)S(1)} %all_to_all.11.replies, bf16[512,2048]{1,0:T(8,128)(2,1)} %bitcast.13), custom_call_target="tpu_custom_call" | custom-call | flops 3000000000 | bytes 6000000 | tf_op jit(solution)/shard_map/keys/pallas_call | solution.py:261
  97.3 6.7 %collective-permute-start = (bf16[512,1024]{1,0:T(8,128)(2,1)S(1)}, bf16[512,1024]{1,0:T(8,128)(2,1)S(1)}, u32[]{:S(2)}, u32[]{:S(2)}) collective-permute-start(bf16[512,1024]{1,0:T(8,128)(2,1)S(1)} %get-tuple-element.11.own), channel_id=1, source_target_pairs={{0,1},{1,0},{2,3},{3,2},{4,5},{5,4},{6,7},{7,6},{8,9},{9,8},{10,11... | collective-permute-start | bytes 3145736 | tf_op jit(solution)/shard_map/ppermute | solution.py:432
  104.0 0.0 copy-start.1
  104.0 0.0 copy-start.4
  104.0 2.2 %queries.1.qs = bf16[1024,512]{1,0:T(8,128)(2,1)S(1)} custom-call(bf16[8192,512]{1,0:T(8,128)(2,1)} %get-tuple-element.10.rows_in, bf16[512,2048]{1,0:T(8,128)(2,1)} %bitcast.14), custom_call_target="tpu_custom_call" | custom-call | flops 2000000000 | bytes 4000000 | tf_op jit(solution)/shard_map/queries/pallas_call | solution.py:304
  106.3 0.0 collective-permute-done.other
  106.3 0.0 copy-done.1
  106.3 0.0 copy-done.4
  106.3 7.7 %layer.1 = (bf16[512,512]{1,0:T(8,128)(2,1)}, bf16[512,512]{1,0:T(8,128)(2,1)}) custom-call(s32[1]{0:T(128)} %bitcast.user, f32[1,512]{1,0:T(1,128)S(1)} %copy-done.4, bf16[1024,512]{1,0:T(8,128)(2,1)S(1)} %queries.1.qs, bf16[512,1024]{1,0:T(8,128)(2,1)S(1)} %get-tuple-element.11.own, bf16[512,1024]{1,0:T(8,128)(2,1)S(1)} %collective-permute-done.other, ...), custom_call_target="tpu_custom_call" | custom-call | flops 6000000000 | bytes 9000000 | tf_op jit(solution)/shard_map/layer/pallas_call | solution.py:398
Async XLA Ops:
  0.6 37.0 %copy-start = (bf16[1024,512]{1,0:T(8,128)(2,1)S(1)}, bf16[1024,512]{1,0:T(8,128)(2,1)}, u32[]{:S(2)}) copy-start(bf16[1024,512]{1,0:T(8,128)(2,1)} %table.1) | copy-start | bytes 3145732
  41.1 53.0 %copy-start.2 = (bf16[256,512]{1,0:T(8,128)(2,1)S(1)}, bf16[256,512]{1,0:T(8,128)(2,1)}, u32[]{:S(2)}) copy-start(bf16[256,512]{1,0:T(8,128)(2,1)} %hot.1) | copy-start | bytes 786436
  41.1 53.0 %copy-start.3 = (f32[1,512]{1,0:T(1,128)S(1)}, f32[1,512]{1,0:T(1,128)}, u32[]{:S(2)}) copy-start(f32[1,512]{1,0:T(1,128)} %gain.2) | copy-start | bytes 6148
  97.3 9.0 %collective-permute-start = (bf16[512,1024]{1,0:T(8,128)(2,1)S(1)}, bf16[512,1024]{1,0:T(8,128)(2,1)S(1)}, u32[]{:S(2)}, u32[]{:S(2)}) collective-permute-start(bf16[512,1024]{1,0:T(8,128)(2,1)S(1)} %get-tuple-element.11.own), channel_id=1, source_target_pairs={{0,1},{1,0},{2,3},{3,2},{4,5},{5,4},{6,7},{7,6},{8,9},{9,8},{10,11... | collective-permute-start | bytes 3145736 | tf_op jit(solution)/shard_map/ppermute | solution.py:432
  104.0 2.3 %copy-start.1 = (bf16[1,512,512]{2,1,0:T(8,128)(2,1)S(1)}, bf16[1,512,512]{2,1,0:T(8,128)(2,1)}, u32[]{:S(2)}) copy-start(bf16[1,512,512]{2,1,0:T(8,128)(2,1)} %param.15) | copy-start | bytes 1572868
  104.0 2.3 %copy-start.4 = (f32[1,512]{1,0:T(1,128)S(1)}, f32[1,512]{1,0:T(1,128)}, u32[]{:S(2)}) copy-start(f32[1,512]{1,0:T(1,128)} %gain.3) | copy-start | bytes 6148

commit v8 on v7

--- a/solution.py
+++ b/solution.py
@@ -212,15 +212,36 @@
     return picked(dense, column, hot)
 
 
+def weights(q, k, head_dim):
+    half = dot_nt(q, k) * (0.5 / head_dim**0.5)
+    return half + half * jnp.tanh(half)
+
+
+def causal_parts(q, kv, half, at, past, head_dim):
+    causal = iota((half, half), 1) <= iota((half, half), 0)
+
+    def masked(w):
+        top = jnp.where(causal, w[:half], 0.0)
+        if w.shape[0] > half:
+            top = jnp.concatenate([top, w[half:]], axis=0)
+        return top.astype(BF16)
+
+    first = masked(weights(q[:, at], kv[:half, at], head_dim))
+    second = masked(weights(q[half:, at], kv[half:, at], head_dim))
+    return dot(first, kv[:half, past]), dot(second, kv[half:, past])
+
+
 def keys_kernel(
-    picks, gain, hot, replies, w_in, rows_out, kv, rows, ins, w_v, w_k, sems
+    user, picks, gain, hot, replies, w_in, rows_out, near_out, kv,
+    rows, ins, w_v, w_k, w_q, near, sems,
 ):
     n, width = rows.shape[0] // 2, rows.shape[1]
     hist, cand = pl.ds(0, n), pl.ds(n, n)
-    in_v, in_k = started(
+    in_v, in_k, in_q = started(
         (
             (w_in.at[:, pl.ds(width, width)], w_v),
             (w_in.at[:, pl.ds(3 * width, width)], w_k),
+            (w_in.at[:, pl.ds(2 * width, width)], w_q),
         ),
         sems,
     )
@@ -251,34 +272,53 @@
     kv[:, width:] = silu(dot(inner, w_v[...])).astype(BF16)
     in_k.wait()
     kv[:, :width] = silu(dot(inner, w_k[...])).astype(BF16)
+    in_q.wait()
+
+    @pl.when(user[0] == 1)
+    def _():
+        q = silu(dot(ins[hist, :], w_q[...])).astype(BF16)
+        half = n // 2
+        head_dim = width // HEADS
+        for h in range(HEADS):
+            at = slice(h * head_dim, (h + 1) * head_dim)
+            past = slice(width + h * head_dim, width + (h + 1) * head_dim)
+            first, second = causal_parts(q, kv, half, at, past, head_dim)
+            near[:half, at] = first[:half]
+            near[half:, at] = first[half:] + second
+        (copy,) = started(((near, near_out.at[hist]),), sems.at[pl.ds(8, 1)])
+        copy.wait()
+
     for copy in done:
         copy.wait()
 
 
-def keys(replies, hot, picks, w_in, gain):
+def keys(user, replies, hot, picks, w_in, gain):
     n = picks.shape[1]
     width = hot.shape[1]
     return pl.pallas_call(
         keys_kernel,
         out_shape=(
             jax.ShapeDtypeStruct((SPARE * n, width), BF16),
+            jax.ShapeDtypeStruct((SPARE // 2 * n, width), F32),
             jax.ShapeDtypeStruct((n, 2 * width), BF16),
         ),
-        in_specs=[VMEM] * 4 + [HBM],
-        out_specs=(HBM, VMEM),
+        in_specs=[SMEM] + [VMEM] * 4 + [HBM],
+        out_specs=(HBM, HBM, VMEM),
         scratch_shapes=[
             pltpu.VMEM((2 * n, width), BF16),
             pltpu.VMEM((2 * n, width), BF16),
             pltpu.VMEM((width, width), BF16),
             pltpu.VMEM((width, width), BF16),
-            DMA((8,)),
+            pltpu.VMEM((width, width), BF16),
+            pltpu.VMEM((n, width), F32),
+            DMA((9,)),
         ],
         compiler_params=pltpu.CompilerParams(vmem_limit_bytes=KEYS_BYTES),
         cost_estimate=pl.CostEstimate(
             flops=3 * 10**9, bytes_accessed=6 * 10**6, transcendentals=10**6
         ),
         name="keys",
-    )(picks, gain, hot, replies, w_in)
+    )(user, picks, gain, hot, replies, w_in)
 
 
 def queries_kernel(rows_in, w_in, qs, ins, w_q, sems):
@@ -319,14 +359,9 @@
     )(rows, w_in)
 
 
-def weights(q, k, head_dim):
-    half = dot_nt(q, k) * (0.5 / head_dim**0.5)
-    return half + half * jnp.tanh(half)
-
-
 def layer_kernel(
-    user, gain, qs, own, other, rows_in, w_in, w_last, hist_out, cand_out,
-    xs, ins, w_u, w_out, us, mix, outs, sems,
+    user, gain, qs, own, other, rows_in, near_in, w_in, w_last, hist_out, cand_out,
+    xs, ins, near, w_u, w_out, us, mix, outs, sems,
 ):
     n, width = own.shape[0], own.shape[1] // 2
     head_dim = width // HEADS
@@ -342,39 +377,34 @@
         sems,
     )
     half = n // 2
-    causal = iota((half, half), 1) <= iota((half, half), 0)
-
-    def masked(w):
-        w = jnp.concatenate([jnp.where(causal, w[:half], 0.0), w[half:]], axis=0)
-        return w.astype(BF16)
-
-    def heads(everyone):
+
+    @pl.when(user[0] == 1)
+    def _():
+        last = 4 + 2 * FINISH_PARTS
+        (copy,) = started(((near_in.at[hist], near),), sems.at[pl.ds(last, 1)])
         for h in range(HEADS):
             at = slice(h * head_dim, (h + 1) * head_dim)
             past = slice(width + h * head_dim, width + (h + 1) * head_dim)
-            first = masked(weights(qs[:, at], own[:half, at], head_dim))
-            first = dot(first, own[:half, past])
-            second = masked(weights(qs[half:, at], own[half:, at], head_dim))
-            second = dot(second, own[half:, past])
-            if everyone:
-                far = weights(qs[:, at], other[:, at], head_dim).astype(BF16)
-                far = dot(far, other[:, past])
-                mix[:half, at] = first[:half] + far[:half]
-                mix[half:, at] = first[half:] + second + far[half:]
-            else:
-                far = weights(qs[n:, at], other[:, at], head_dim).astype(BF16)
-                far = dot(far, other[:, past])
-                mix[:half, at] = first[:half]
-                mix[half:n, at] = first[half:n] + second[: n - half]
-                mix[n:, at] = first[n:] + second[n - half :] + far
-
-    @pl.when(user[0] == 1)
-    def _():
-        heads(True)
+            first = weights(qs[n:, at], own[:, at], head_dim).astype(BF16)
+            first = dot(first, own[:, past])
+            far = weights(qs[:, at], other[:, at], head_dim).astype(BF16)
+            far = dot(far, other[:, past])
+            mix[:n, at] = far[:n]
+            mix[n:, at] = first + far[n:]
+        copy.wait()
+        mix[:n, :] += near[...]
 
     @pl.when(user[0] == 0)
     def _():
-        heads(False)
+        for h in range(HEADS):
+            at = slice(h * head_dim, (h + 1) * head_dim)
+            past = slice(width + h * head_dim, width + (h + 1) * head_dim)
+            first, second = causal_parts(qs, own, half, at, past, head_dim)
+            far = weights(qs[n:, at], other[:, at], head_dim).astype(BF16)
+            far = dot(far, other[:, past])
+            mix[:half, at] = first[:half]
+            mix[half:n, at] = first[half:n] + second[: n - half]
+            mix[n:, at] = first[n:] + second[n - half :] + far
 
     for arrival in arrivals:
         arrival.wait()
@@ -392,30 +422,31 @@
         copy.wait()
 
 
-def layer(user, rows, qs, own, other, gain, w_in, w_out):
+def layer(user, rows, near, qs, own, other, gain, w_in, w_out):
     n, width = own.shape[0], own.shape[1] // 2
     shape = jax.ShapeDtypeStruct((n, width), BF16)
     return pl.pallas_call(
         layer_kernel,
         out_shape=(shape, shape),
-        in_specs=[SMEM] + [VMEM] * 4 + [HBM] * 3,
+        in_specs=[SMEM] + [VMEM] * 4 + [HBM] * 4,
         out_specs=(HBM, HBM),
         scratch_shapes=[
             pltpu.VMEM((2 * n, width), BF16),
             pltpu.VMEM((2 * n, width), BF16),
+            pltpu.VMEM((n, width), F32),
             pltpu.VMEM((width, width), BF16),
             pltpu.VMEM((width, width), BF16),
             pltpu.VMEM((2 * n, width), F32),
             pltpu.VMEM((2 * n, width), F32),
             pltpu.VMEM((2 * n, width), BF16),
-            DMA((4 + 2 * FINISH_PARTS,)),
+            DMA((5 + 2 * FINISH_PARTS,)),
         ],
         compiler_params=pltpu.CompilerParams(vmem_limit_bytes=LAYER_BYTES),
         cost_estimate=pl.CostEstimate(
             flops=6 * 10**9, bytes_accessed=9 * 10**6, transcendentals=6 * 10**6
         ),
         name="layer",
-    )(user, gain, qs, own, other, rows, w_in, w_out)
+    )(user, gain, qs, own, other, rows, near, w_in, w_out)
 
 
 def exchange(array):
@@ -428,11 +459,11 @@
     asked, picks = ask(hist_ids, cand_ids, hot_ids[None], owners, shift)
     numbers = exchange(asked[:, None, :])[:, 0, :]
     replies = exchange(fetch(numbers, table))
-    rows, own = keys(replies, hot_table, picks, w_in[0], in_gain)
+    user = lax.axis_index("user")[None].astype(I32)
+    rows, near, own = keys(user, replies, hot_table, picks, w_in[0], in_gain)
     other = lax.ppermute(own, "user", [(0, 1), (1, 0)])
     qs = queries(rows, w_in[0])
-    user = lax.axis_index("user")[None].astype(I32)
-    hist_out, cand_out = layer(user, rows, qs, own, other, attn_gain, w_in[0], w_out[0])
+    hist_out, cand_out = layer(user, rows, near, qs, own, other, attn_gain, w_in[0], w_out[0])
     return hist_out[None], cand_out[None]
 
 

time: 114 us -> 113 us (level)
  blocking collectives: 87.9 us -> 34.9 us
  waiting for transfers between devices: 0.01 us -> 42.9 us
  starting transfers between devices: 6.72 us -> 13.6 us
  Pallas kernels: 17.8 us -> 19.1 us
    all_to_all x2 -> x1, blocking collectives: 87.9 us -> 34.9 us  [exchange(): return lax.all_to_all(array, ('req', 'cand'), 0, 0, tiled=True)]
    all_to_all x0 -> x1, waiting for transfers between devices: none -> 42.9 us  [exchange(): return lax.all_to_all(array, ('req', 'cand'), 0, 0, tiled=True)]
    all_to_all x0 -> x1, starting transfers between devices: none -> 9.51 us  [exchange(): return lax.all_to_all(array, ('req', 'cand'), 0, 0, tiled=True)]
    pallas_call x1, Pallas kernels: 3.11 us -> 5.77 us  [keys(): pl.pallas_call(keys_kernel, out_shape=(jax.ShapeDtypeStruct((SPARE * n, w...]
    ppermute x1, starting transfers between devices: 6.72 us -> 4.08 us  [per_device(): other = lax.ppermute(own, 'user', [(0, 1), (1, 0)])]
    pallas_call x1, Pallas kernels: 7.7 us -> 6.37 us  [layer(): pl.pallas_call(layer_kernel, out_shape=(shape, shape), in_specs=[SMEM] +...]
  transfers between devices with their start and end apart: 1 -> 2, of which waited for: 0 -> 1; matrix products, arithmetic and copies ran while one was open for 0% -> 0% of each run, Pallas kernels for 2% -> 2%
where the time goes in v8:
time: 113 us; the launch traced here: 112 us
  waiting for transfers between devices  42.9 us (38%)
  blocking collectives  34.9 us (31%)
  Pallas kernels  19.1 us (17%)
  starting transfers between devices  13.6 us (12%)
    all_to_all x1, waiting for transfers between devices, exchange(): return lax.all_to_all(array, ('req', 'cand'), 0, 0, tiled=True)  42.9 us
    all_to_all x1, blocking collectives, exchange(): return lax.all_to_all(array, ('req', 'cand'), 0, 0, tiled=True)  34.9 us
    all_to_all x1, starting transfers between devices, exchange(): return lax.all_to_all(array, ('req', 'cand'), 0, 0, tiled=True)  9.51 us
    pallas_call x1, Pallas kernels, layer(): pl.pallas_call(layer_kernel, out_shape=(shape, shape), in_specs=[SMEM] +...  6.37 us
    pallas_call x1, Pallas kernels, keys(): pl.pallas_call(keys_kernel, out_shape=(jax.ShapeDtypeStruct((SPARE * n, w...  5.77 us
    ppermute x1, starting transfers between devices, per_device(): other = lax.ppermute(own, 'user', [(0, 1), (1, 0)])  4.08 us
    pallas_call x1, Pallas kernels, fetch(): pl.pallas_call(fetch_kernel, out_shape=jax.ShapeDtypeStruct(shape, BF16),...  3.48 us
  transfers between devices with their start and end apart: 2, of which 1 were waited for; matrix products, arithmetic and copies ran while one was open for 0% of the time, Pallas kernels for 2%

profile of v8, /device:TPU:1, one launch (start us, length us, event | category | flops | bytes accessed | tf_op | source)
XLA Modules:
  0.0 112.3 jit_solution(6851770245954913858)
XLA Ops:
  0.6 0.0 copy-start.2
  0.6 0.8 pad_add_fusion.refs_0_
  1.4 1.3 %ask.1 = (s32[256,8]{1,0:T(8,128)S(1)}, f32[2,512]{1,0:T(2,128)S(1)}) custom-call(s32[1,1280]{1,0:T(1,128)S(1)} %pad_add_fusion.refs_0_), custom_call_target="tpu_custom_call" | custom-call | flops 1000000000 | bytes 100000 | tf_op jit(solution)/shard_map/ask/pallas_call | solution.py:97
  2.7 34.9 %all_to_all.10 = s32[256,1,8]{2,1,0:T(1,128)S(1)} all-to-all(s32[256,1,8]{2,1,0:T(1,128)S(1)} %bitcast.11), channel_id=1, replica_groups=mesh['req'=8,'cand'=32,'user'=2] {'req','cand'}, dimensions={0} | all-to-all | bytes 16384 | tf_op jit(solution)/shard_map/all_to_all | solution.py:453
  37.7 0.0 copy-done.2
  37.7 3.5 %fetch.1 = bf16[256,4,896]{2,1,0:T(4,128)(2,1)} custom-call(s32[256,8]{1,0:T(8,128)S(1)} %bitcast.12, bf16[1024,512]{1,0:T(8,128)(2,1)S(1)} %copy-done.2), custom_call_target="tpu_custom_call" | custom-call | flops 3000000000 | bytes 3000000 | tf_op jit(solution)/shard_map/fetch/pallas_call | solution.py:171
  41.1 0.0 copy-start.3
  41.2 0.0 copy-start.4
  41.2 9.5 %all-to-all-start.1 = ((bf16[256,4,896]{2,1,0:T(4,128)(2,1)}), bf16[256,4,896]{2,1,0:T(4,128)(2,1)S(1)}, u32[]{:S(2)}, u32[]{:S(2)}) async-start(bf16[256,4,896]{2,1,0:T(4,128)(2,1)} %fetch.1), calls=%async_computation.1 | async-start | bytes 3670016 | tf_op jit(solution)/shard_map/all_to_all | solution.py:453
  50.7 42.9 %all-to-all-done.1.replies = bf16[256,4,896]{2,1,0:T(4,128)(2,1)S(1)} async-done(((bf16[256,4,896]{2,1,0:T(4,128)(2,1)}), bf16[256,4,896]{2,1,0:T(4,128)(2,1)S(1)}, u32[]{:S(2)}, u32[]{:S(2)}) %all-to-all-start.1) | async-done | bytes 1835040 | tf_op jit(solution)/shard_map/all_to_all | solution.py:453
  93.6 0.0 copy-done.3
  93.6 0.0 copy-done.4
  93.6 5.8 %keys.1 = (bf16[8192,512]{1,0:T(8,128)(2,1)}, f32[4096,512]{1,0:T(8,128)}, bf16[512,1024]{1,0:T(8,128)(2,1)S(1)}) custom-call(s32[1]{0:T(128)} %bitcast.user, f32[2,512]{1,0:T(2,128)S(1)} %get-tuple-element.9.picks, f32[1,512]{1,0:T(1,128)S(1)} %copy-done.4, bf16[256,512]{1,0:T(8,128)(2,1)S(1)} %copy-done.3, ...), custom_call_target="tpu_custom_call" | custom-call | flops 3000000000 | bytes 6000000 | tf_op jit(solution)/shard_map/keys/pallas_call | solution.py:298
  99.4 4.1 %collective-permute-start = (bf16[512,1024]{1,0:T(8,128)(2,1)S(1)}, bf16[512,1024]{1,0:T(8,128)(2,1)S(1)}, u32[]{:S(2)}, u32[]{:S(2)}) collective-permute-start(bf16[512,1024]{1,0:T(8,128)(2,1)S(1)} %get-tuple-element.12.own), channel_id=1, source_target_pairs={{0,1},{1,0},{2,3},{3,2},{4,5},{5,4},{6,7},{7,6},{8,9},{9,8},{10,11... | collective-permute-start | bytes 3145736 | tf_op jit(solution)/shard_map/ppermute | solution.py:464
  103.5 0.0 copy-start
  103.5 0.0 copy-start.1
  103.5 2.2 %queries.1.qs = bf16[1024,512]{1,0:T(8,128)(2,1)S(1)} custom-call(bf16[8192,512]{1,0:T(8,128)(2,1)} %get-tuple-element.11.rows_in, bf16[512,2048]{1,0:T(8,128)(2,1)} %bitcast.14), custom_call_target="tpu_custom_call" | custom-call | flops 2000000000 | bytes 4000000 | tf_op jit(solution)/shard_map/queries/pallas_call | solution.py:344
  105.8 0.0 collective-permute-done.other
  105.8 0.0 copy-done
  105.8 0.0 copy-done.1
  105.8 6.4 %layer.1 = (bf16[512,512]{1,0:T(8,128)(2,1)}, bf16[512,512]{1,0:T(8,128)(2,1)}) custom-call(s32[1]{0:T(128)} %bitcast.user, f32[1,512]{1,0:T(1,128)S(1)} %copy-done.1, bf16[1024,512]{1,0:T(8,128)(2,1)S(1)} %queries.1.qs, bf16[512,1024]{1,0:T(8,128)(2,1)S(1)} %get-tuple-element.12.own, bf16[512,1024]{1,0:T(8,128)(2,1)S(1)} %collective-permute-done.other, ...), custom_call_target="tpu_custom_call" | custom-call | flops 6000000000 | bytes 9000000 | tf_op jit(solution)/shard_map/layer/pallas_call | solution.py:428
Async XLA Ops:
  0.6 37.0 %copy-start.2 = (bf16[1024,512]{1,0:T(8,128)(2,1)S(1)}, bf16[1024,512]{1,0:T(8,128)(2,1)}, u32[]{:S(2)}) copy-start(bf16[1024,512]{1,0:T(8,128)(2,1)} %table.1) | copy-start | bytes 3145732
  41.1 52.5 %copy-start.3 = (bf16[256,512]{1,0:T(8,128)(2,1)S(1)}, bf16[256,512]{1,0:T(8,128)(2,1)}, u32[]{:S(2)}) copy-start(bf16[256,512]{1,0:T(8,128)(2,1)} %hot.1) | copy-start | bytes 786436
  41.2 52.5 %copy-start.4 = (f32[1,512]{1,0:T(1,128)S(1)}, f32[1,512]{1,0:T(1,128)}, u32[]{:S(2)}) copy-start(f32[1,512]{1,0:T(1,128)} %gain.2) | copy-start | bytes 6148
  41.2 52.4 %all-to-all-start.1 = ((bf16[256,4,896]{2,1,0:T(4,128)(2,1)}), bf16[256,4,896]{2,1,0:T(4,128)(2,1)S(1)}, u32[]{:S(2)}, u32[]{:S(2)}) async-start(bf16[256,4,896]{2,1,0:T(4,128)(2,1)} %fetch.1), calls=%async_computation.1 | async-start | bytes 3670016 | tf_op jit(solution)/shard_map/all_to_all | solution.py:453
  99.4 6.4 %collective-permute-start = (bf16[512,1024]{1,0:T(8,128)(2,1)S(1)}, bf16[512,1024]{1,0:T(8,128)(2,1)S(1)}, u32[]{:S(2)}, u32[]{:S(2)}) collective-permute-start(bf16[512,1024]{1,0:T(8,128)(2,1)S(1)} %get-tuple-element.12.own), channel_id=1, source_target_pairs={{0,1},{1,0},{2,3},{3,2},{4,5},{5,4},{6,7},{7,6},{8,9},{9,8},{10,11... | collective-permute-start | bytes 3145736 | tf_op jit(solution)/shard_map/ppermute | solution.py:464
  103.5 2.3 %copy-start = (bf16[1,512,512]{2,1,0:T(8,128)(2,1)S(1)}, bf16[1,512,512]{2,1,0:T(8,128)(2,1)}, u32[]{:S(2)}) copy-start(bf16[1,512,512]{2,1,0:T(8,128)(2,1)} %param.15) | copy-start | bytes 1572868
  103.5 2.3 %copy-start.1 = (f32[1,512]{1,0:T(1,128)S(1)}, f32[1,512]{1,0:T(1,128)}, u32[]{:S(2)}) copy-start(f32[1,512]{1,0:T(1,128)} %gain.3) | copy-start | bytes 6148

commit v9 on v8

--- a/solution.py
+++ b/solution.py
@@ -376,6 +376,11 @@
         ),
         sems,
     )
+    def gates():
+        for arrival in arrivals:
+            arrival.wait()
+        us[...] = silu(dot(ins[...], w_u[...]))
+
     half = n // 2
 
     @pl.when(user[0] == 1)
@@ -383,6 +388,8 @@
         last = 4 + 2 * FINISH_PARTS
         (copy,) = started(((near_in.at[hist], near),), sems.at[pl.ds(last, 1)])
         for h in range(HEADS):
+            if h == HEADS - 1:
+                gates()
             at = slice(h * head_dim, (h + 1) * head_dim)
             past = slice(width + h * head_dim, width + (h + 1) * head_dim)
             first = weights(qs[n:, at], own[:, at], head_dim).astype(BF16)
@@ -397,6 +404,8 @@
     @pl.when(user[0] == 0)
     def _():
         for h in range(HEADS):
+            if h == HEADS - 1:
+                gates()
             at = slice(h * head_dim, (h + 1) * head_dim)
             past = slice(width + h * head_dim, width + (h + 1) * head_dim)
             first, second = causal_parts(qs, own, half, at, past, head_dim)
@@ -406,9 +415,6 @@
             mix[half:n, at] = first[half:n] + second[: n - half]
             mix[n:, at] = first[n:] + second[n - half :] + far
 
-    for arrival in arrivals:
-        arrival.wait()
-    us[...] = silu(dot(ins[...], w_u[...]))
     done = []
     step = n // FINISH_PARTS
     for i in range(2 * FINISH_PARTS):

time: 113 us -> 114 us (level)
  Pallas kernels: 19.1 us -> 20.3 us
    pallas_call x1, Pallas kernels: 6.37 us -> 7.53 us  [layer(): pl.pallas_call(layer_kernel, out_shape=(shape, shape), in_specs=[SMEM] +...]
where the time goes in v9:
time: 114 us
  waiting for transfers between devices  42.9 us (38%)
  blocking collectives  34.9 us (31%)
  Pallas kernels  20.3 us (18%)
  starting transfers between devices  13.6 us (12%)
    all_to_all x1, waiting for transfers between devices, exchange(): return lax.all_to_all(array, ('req', 'cand'), 0, 0, tiled=True)  42.9 us
    all_to_all x1, blocking collectives, exchange(): return lax.all_to_all(array, ('req', 'cand'), 0, 0, tiled=True)  34.9 us
    all_to_all x1, starting transfers between devices, exchange(): return lax.all_to_all(array, ('req', 'cand'), 0, 0, tiled=True)  9.51 us
    pallas_call x1, Pallas kernels, layer(): pl.pallas_call(layer_kernel, out_shape=(shape, shape), in_specs=[SMEM] +...  7.53 us
    pallas_call x1, Pallas kernels, keys(): pl.pallas_call(keys_kernel, out_shape=(jax.ShapeDtypeStruct((SPARE * n, w...  5.77 us
    ppermute x1, starting transfers between devices, per_device(): other = lax.ppermute(own, 'user', [(0, 1), (1, 0)])  4.08 us
    pallas_call x1, Pallas kernels, fetch(): pl.pallas_call(fetch_kernel, out_shape=jax.ShapeDtypeStruct(shape, BF16),...  3.48 us
  transfers between devices with their start and end apart: 2, of which 1 were waited for; matrix products, arithmetic and copies ran while one was open for 0% of the time, Pallas kernels for 2%

profile of v9, /device:TPU:1, one launch (start us, length us, event | category | flops | bytes accessed | tf_op | source)
XLA Modules:
  0.0 113.5 jit_solution(1917588353106218522)
XLA Ops:
  0.6 0.0 copy-start.2
  0.6 0.8 pad_add_fusion.refs_0_
  1.4 1.3 %ask.1 = (s32[256,8]{1,0:T(8,128)S(1)}, f32[2,512]{1,0:T(2,128)S(1)}) custom-call(s32[1,1280]{1,0:T(1,128)S(1)} %pad_add_fusion.refs_0_), custom_call_target="tpu_custom_call" | custom-call | flops 1000000000 | bytes 100000 | tf_op jit(solution)/shard_map/ask/pallas_call | solution.py:97
  2.7 34.9 %all_to_all.10 = s32[256,1,8]{2,1,0:T(1,128)S(1)} all-to-all(s32[256,1,8]{2,1,0:T(1,128)S(1)} %bitcast.11), channel_id=1, replica_groups=mesh['req'=8,'cand'=32,'user'=2] {'req','cand'}, dimensions={0} | all-to-all | bytes 16384 | tf_op jit(solution)/shard_map/all_to_all | solution.py:459
  37.7 0.0 copy-done.2
  37.7 3.5 %fetch.1 = bf16[256,4,896]{2,1,0:T(4,128)(2,1)} custom-call(s32[256,8]{1,0:T(8,128)S(1)} %bitcast.12, bf16[1024,512]{1,0:T(8,128)(2,1)S(1)} %copy-done.2), custom_call_target="tpu_custom_call" | custom-call | flops 3000000000 | bytes 3000000 | tf_op jit(solution)/shard_map/fetch/pallas_call | solution.py:171
  41.1 0.0 copy-start.3
  41.2 0.0 copy-start.4
  41.2 9.5 %all-to-all-start.1 = ((bf16[256,4,896]{2,1,0:T(4,128)(2,1)}), bf16[256,4,896]{2,1,0:T(4,128)(2,1)S(1)}, u32[]{:S(2)}, u32[]{:S(2)}) async-start(bf16[256,4,896]{2,1,0:T(4,128)(2,1)} %fetch.1), calls=%async_computation.1 | async-start | bytes 3670016 | tf_op jit(solution)/shard_map/all_to_all | solution.py:459
  50.7 42.9 %all-to-all-done.1.replies = bf16[256,4,896]{2,1,0:T(4,128)(2,1)S(1)} async-done(((bf16[256,4,896]{2,1,0:T(4,128)(2,1)}), bf16[256,4,896]{2,1,0:T(4,128)(2,1)S(1)}, u32[]{:S(2)}, u32[]{:S(2)}) %all-to-all-start.1) | async-done | bytes 1835040 | tf_op jit(solution)/shard_map/all_to_all | solution.py:459
  93.6 0.0 copy-done.3
  93.6 0.0 copy-done.4
  93.6 5.8 %keys.1 = (bf16[8192,512]{1,0:T(8,128)(2,1)}, f32[4096,512]{1,0:T(8,128)}, bf16[512,1024]{1,0:T(8,128)(2,1)S(1)}) custom-call(s32[1]{0:T(128)} %bitcast.user, f32[2,512]{1,0:T(2,128)S(1)} %get-tuple-element.9.picks, f32[1,512]{1,0:T(1,128)S(1)} %copy-done.4, bf16[256,512]{1,0:T(8,128)(2,1)S(1)} %copy-done.3, ...), custom_call_target="tpu_custom_call" | custom-call | flops 3000000000 | bytes 6000000 | tf_op jit(solution)/shard_map/keys/pallas_call | solution.py:298
  99.4 4.1 %collective-permute-start = (bf16[512,1024]{1,0:T(8,128)(2,1)S(1)}, bf16[512,1024]{1,0:T(8,128)(2,1)S(1)}, u32[]{:S(2)}, u32[]{:S(2)}) collective-permute-start(bf16[512,1024]{1,0:T(8,128)(2,1)S(1)} %get-tuple-element.12.own), channel_id=1, source_target_pairs={{0,1},{1,0},{2,3},{3,2},{4,5},{5,4},{6,7},{7,6},{8,9},{9,8},{10,11... | collective-permute-start | bytes 3145736 | tf_op jit(solution)/shard_map/ppermute | solution.py:470
  103.5 0.0 copy-start
  103.5 0.0 copy-start.1
  103.5 2.2 %queries.1.qs = bf16[1024,512]{1,0:T(8,128)(2,1)S(1)} custom-call(bf16[8192,512]{1,0:T(8,128)(2,1)} %get-tuple-element.11.rows_in, bf16[512,2048]{1,0:T(8,128)(2,1)} %bitcast.14), custom_call_target="tpu_custom_call" | custom-call | flops 2000000000 | bytes 4000000 | tf_op jit(solution)/shard_map/queries/pallas_call | solution.py:344
  105.8 0.0 collective-permute-done.other
  105.8 0.0 copy-done
  105.8 0.0 copy-done.1
  105.8 7.5 %layer.1 = (bf16[512,512]{1,0:T(8,128)(2,1)}, bf16[512,512]{1,0:T(8,128)(2,1)}) custom-call(s32[1]{0:T(128)} %bitcast.user, f32[1,512]{1,0:T(1,128)S(1)} %copy-done.1, bf16[1024,512]{1,0:T(8,128)(2,1)S(1)} %queries.1.qs, bf16[512,1024]{1,0:T(8,128)(2,1)S(1)} %get-tuple-element.12.own, bf16[512,1024]{1,0:T(8,128)(2,1)S(1)} %collective-permute-done.other, ...), custom_call_target="tpu_custom_call" | custom-call | flops 6000000000 | bytes 9000000 | tf_op jit(solution)/shard_map/layer/pallas_call | solution.py:434
Async XLA Ops:
  0.6 37.0 %copy-start.2 = (bf16[1024,512]{1,0:T(8,128)(2,1)S(1)}, bf16[1024,512]{1,0:T(8,128)(2,1)}, u32[]{:S(2)}) copy-start(bf16[1024,512]{1,0:T(8,128)(2,1)} %table.1) | copy-start | bytes 3145732
  41.1 52.5 %copy-start.3 = (bf16[256,512]{1,0:T(8,128)(2,1)S(1)}, bf16[256,512]{1,0:T(8,128)(2,1)}, u32[]{:S(2)}) copy-start(bf16[256,512]{1,0:T(8,128)(2,1)} %hot.1) | copy-start | bytes 786436
  41.2 52.5 %copy-start.4 = (f32[1,512]{1,0:T(1,128)S(1)}, f32[1,512]{1,0:T(1,128)}, u32[]{:S(2)}) copy-start(f32[1,512]{1,0:T(1,128)} %gain.2) | copy-start | bytes 6148
  41.2 52.4 %all-to-all-start.1 = ((bf16[256,4,896]{2,1,0:T(4,128)(2,1)}), bf16[256,4,896]{2,1,0:T(4,128)(2,1)S(1)}, u32[]{:S(2)}, u32[]{:S(2)}) async-start(bf16[256,4,896]{2,1,0:T(4,128)(2,1)} %fetch.1), calls=%async_computation.1 | async-start | bytes 3670016 | tf_op jit(solution)/shard_map/all_to_all | solution.py:459
  99.4 6.4 %collective-permute-start = (bf16[512,1024]{1,0:T(8,128)(2,1)S(1)}, bf16[512,1024]{1,0:T(8,128)(2,1)S(1)}, u32[]{:S(2)}, u32[]{:S(2)}) collective-permute-start(bf16[512,1024]{1,0:T(8,128)(2,1)S(1)} %get-tuple-element.12.own), channel_id=1, source_target_pairs={{0,1},{1,0},{2,3},{3,2},{4,5},{5,4},{6,7},{7,6},{8,9},{9,8},{10,11... | collective-permute-start | bytes 3145736 | tf_op jit(solution)/shard_map/ppermute | solution.py:470
  103.5 2.3 %copy-start = (bf16[1,512,512]{2,1,0:T(8,128)(2,1)S(1)}, bf16[1,512,512]{2,1,0:T(8,128)(2,1)}, u32[]{:S(2)}) copy-start(bf16[1,512,512]{2,1,0:T(8,128)(2,1)} %param.15) | copy-start | bytes 1572868
  103.5 2.3 %copy-start.1 = (f32[1,512]{1,0:T(1,128)S(1)}, f32[1,512]{1,0:T(1,128)}, u32[]{:S(2)}) copy-start(f32[1,512]{1,0:T(1,128)} %gain.3) | copy-start | bytes 6148
